TPU v7x, 32 devices: a whole 2x2x4 slice. The times are simulated.
32 devices in a mesh: rep: 8 (over y, x, core), shard: 4 (over z).
Axes of the slice: x: 2, y: 2, z: 4, core: 2. Of those that a mesh axis runs over, the one named last changes fastest.
Arguments:
- x_in: bfloat16 [32, 1024, 1024], P(('rep', 'shard')), may hold values from -6 to 6
- segment_ids: int32 [32, 1024], P(('rep', 'shard')), may hold values from 0 to 3, never falling along the last dimension, each value on 1 to 512 neighbouring positions
- norm_in: bfloat16 [1024], P('shard'), may hold values from 0.5 to 1.5
- mix_in: bfloat16 [1024, 3352], P('shard'), may hold values from -0.1875 to 0.1875
- attn_in: bfloat16 [1024, 768], P('shard'), may hold values from -0.1875 to 0.1875
- attn_out: bfloat16 [1024, 512], P('shard'), may hold values from -0.75 to 0.75
- mix_out: bfloat16 [1024, 1536], P('shard'), may hold values from -0.15625 to 0.15625
- norm_ff: bfloat16 [1024], P('shard'), may hold values from 0.5 to 1.5
- ff_in: bfloat16 [1024, 4096], P('shard'), may hold values from -0.1875 to 0.1875
- ff_out: bfloat16 [1024, 2048], P('shard'), may hold values from -0.125 to 0.125
- conv_kernel: bfloat16 [4, 1792], replicated, may hold values from -3 to 3
- conv_bias: bfloat16 [1792], replicated, may hold values from -3 to 3
- log_rate: float32 [24], replicated, may hold values from 0 to 2.77
- dt_bias: float32 [24], replicated, may hold values from -4.6 to -2.3
- skip: float32 [24], replicated, may hold values from 0.5 to 1.5
- gate_norm: bfloat16 [1536], replicated, may hold values from 0.5 to 1.5
- cotangent: bfloat16 [32, 1024, 1024], P(('rep', 'shard')), may hold values from -6 to 6
Outputs:
- output: bfloat16 [32, 1024, 1024], P(('rep', 'shard'))
- input_grad: bfloat16 [32, 1024, 1024], P(('rep', 'shard'))
- norm_in_grad: float32 [1024], P('shard')
- mix_in_grad: float32 [1024, 3352], P('shard')
- attn_in_grad: float32 [1024, 768], P('shard')
- attn_out_grad: float32 [1024, 512], P('shard')
- mix_out_grad: float32 [1024, 1536], P('shard')
- norm_ff_grad: float32 [1024], P('shard')
- ff_in_grad: float32 [1024, 4096], P('shard')
- ff_out_grad: float32 [1024, 2048], P('shard')
- conv_kernel_grad: float32 [4, 1792], replicated
- conv_bias_grad: float32 [1792], replicated
- log_rate_grad: float32 [24], replicated
- dt_bias_grad: float32 [24], replicated
- skip_grad: float32 [24], replicated
- gate_norm_grad: float32 [1536], replicated
Inputs may be any that keep to these rules, and one draw needn't show every extreme that they name: `segment_ids`: within a sequence segment numbers never fall, so each document is one run of tokens; every number of 0 to 3 occurs in each sequence, in runs of at most 512 tokens.
All inputs are finite; a program needn't handle non-finite values.
Results may differ from a plain program's by a relative error of at most 0.019.
Values may be sent and summed in bfloat16 or wider, within the bound.
No kernel may reach another device: no remote copies, remote signals or barrier semaphores. Data moves between devices by JAX's collectives and lax.ppermute only.
A program may use at most 320 MiB of HBM per device.

v0:
```python
from functools import partial
import math

import jax
import jax.numpy as jnp
from jax import lax
from jax.sharding import PartitionSpec as P

AHEADS = 8
KVHEADS = 2
HDIM = 64
CONV = 4


EPS = 1e-05
THETA = 100000000000.0
HIGH = lax.Precision.HIGHEST


def matmul(left, right):
    return jnp.dot(left, right, preferred_element_type=jnp.float32)


def matmul_nt(left, right):
    return lax.dot_general(
        left, right, (((1,), (1,)), ((), ())), preferred_element_type=jnp.float32
    )


def matmul_tn(left, right):
    return lax.dot_general(
        left, right, (((0,), (0,)), ((), ())), preferred_element_type=jnp.float32
    )


def normed(values, gain):
    scale = lax.rsqrt(jnp.mean(values * values, axis=-1, keepdims=True) + EPS)
    return values * scale * gain


def swiglu(projection):
    width = projection.shape[-1] // 2
    return jax.nn.silu(projection[:, :width]) * projection[:, width:]


def rotary_tables(length, width):
    half = width // 2
    freq = jnp.exp(-(jnp.arange(half, dtype=jnp.float32) * (2.0 / width)) * math.log(THETA))
    angle = jnp.arange(length, dtype=jnp.float32)[:, None] * freq[None, :]
    return (jnp.cos(angle), jnp.sin(angle))


def rotate(values, cosine, sine):
    half = values.shape[-1] // 2
    first = values[..., :half]
    second = values[..., half:]
    cos_b = cosine[None, :, None, :]
    sin_b = sine[None, :, None, :]
    return jnp.concatenate(
        [first * cos_b - second * sin_b, second * cos_b + first * sin_b], axis=-1
    )


def attention_inputs(attn_proj, cosine, sine):
    sequences, length = (attn_proj.shape[0], attn_proj.shape[1])
    width = AHEADS * HDIM
    query = rotate(attn_proj[..., :width].reshape(sequences, length, AHEADS, HDIM), cosine, sine)
    keys = rotate(
        attn_proj[..., width : width + KVHEADS * HDIM].reshape(sequences, length, KVHEADS, HDIM),
        cosine,
        sine,
    )
    values = attn_proj[..., width + KVHEADS * HDIM :].reshape(sequences, length, KVHEADS, HDIM)
    return (query, keys, values)


def conv_mixed(conv_input, segment_ids, conv_kernel, conv_bias):
    length = conv_input.shape[1]
    total = conv_bias + conv_kernel[CONV - 1] * conv_input
    for offset in range(1, CONV):
        earlier = jnp.pad(conv_input, ((0, 0), (offset, 0), (0, 0)))[:, :length]
        earlier_ids = jnp.pad(segment_ids, ((0, 0), (offset, 0)), constant_values=-1)[:, :length]
        total = total + conv_kernel[CONV - 1 - offset] * jnp.where(
            (earlier_ids == segment_ids)[..., None], earlier, 0.0
        )
    return jax.nn.silu(total)


def scan_block(carry, item):
    state, last_id = carry
    inputs, step_sizes, log_decay, b_values, c_values, block_ids = item
    block = block_ids.shape[0]
    order = jnp.arange(block, dtype=jnp.int32)
    same = (block_ids[:, None] == block_ids[None, :]) & (order[:, None] >= order[None, :])
    totals = jnp.cumsum(log_decay, axis=0).T
    gaps = totals[:, :, None] - totals[:, None, :]
    decays = jnp.where(same[None], jnp.exp(jnp.where(same[None], gaps, 0.0)), 0.0)
    intersection = jnp.dot(c_values, b_values.T, precision=HIGH, preferred_element_type=jnp.float32)
    mixing = decays * intersection[None] * step_sizes.T[:, None, :]
    within = jnp.einsum("hts,shp->thp", mixing, inputs, precision=HIGH)
    entering = jnp.where((block_ids == last_id)[:, None], jnp.exp(totals.T), 0.0)
    carried = jnp.einsum("tn,hpn->thp", c_values, state, precision=HIGH) * entering[:, :, None]
    tail_id = block_ids[block - 1]
    leaving = jnp.where(
        (block_ids == tail_id)[:, None], jnp.exp(totals[:, block - 1 :] - totals).T, 0.0
    )
    kept_rate = jnp.where(tail_id == last_id, jnp.exp(totals[:, block - 1]), 0.0)
    fresh = jnp.einsum(
        "shp,sn->hpn", inputs * (leaving * step_sizes)[:, :, None], b_values, precision=HIGH
    )
    return ((fresh + state * kept_rate[:, None, None], tail_id), within + carried)


def ssd_sequence(inputs, step_sizes, rate, b_values, c_values, segment_ids):
    length, heads, width = inputs.shape
    block = min(128, length)
    blocks = length // block
    log_decay = step_sizes * rate[None, :]

    def cut(values):
        return values.reshape((blocks, block) + values.shape[1:])

    initial = (jnp.zeros((heads, width, b_values.shape[1]), jnp.float32), jnp.array(-1, jnp.int32))
    final, outputs = lax.scan(
        jax.checkpoint(scan_block),
        initial,
        (
            cut(inputs),
            cut(step_sizes),
            cut(log_decay),
            cut(b_values),
            cut(c_values),
            cut(segment_ids),
        ),
    )
    return outputs.reshape(length, heads, width)


def mixer_core(projected, segment_ids, conv_kernel, conv_bias, log_rate, dt_bias, skip, gate_norm):
    inner = gate_norm.shape[0]
    heads = log_rate.shape[0]
    width = inner // heads
    channels = conv_bias.shape[0]
    states = (channels - inner) // 2
    sequences, length = segment_ids.shape
    gate_part = projected[..., :inner]
    conv_input = projected[..., inner : inner + channels]
    step_raw = projected[..., inner + channels :]
    conv_out = conv_mixed(conv_input, segment_ids, conv_kernel, conv_bias)
    inputs = conv_out[..., :inner].reshape(sequences, length, heads, width)
    b_values = conv_out[..., inner : inner + states]
    c_values = conv_out[..., inner + states :]
    step_sizes = jax.nn.softplus(step_raw + dt_bias)
    rate = -jnp.exp(log_rate)
    scanned = jax.vmap(ssd_sequence, in_axes=(0, 0, None, 0, 0, 0))(
        inputs, step_sizes, rate, b_values, c_values, segment_ids
    )
    output = scanned + skip[:, None] * inputs
    gated = output.reshape(sequences, length, inner) * jax.nn.silu(gate_part)
    return normed(gated, gate_norm)


def masked_scores(query, keys, query_ids, key_ids, query_pos):
    scale = query.shape[-1] ** (-0.5)
    scores = jnp.einsum("qkgd,skd->kgqs", query, keys, preferred_element_type=jnp.float32) * scale
    key_pos = jnp.arange(keys.shape[0], dtype=jnp.int32)
    allowed = (query_ids[:, None] == key_ids[None, :]) & (query_pos[:, None] >= key_pos[None, :])
    return jnp.where(allowed[None, None], scores, -jnp.inf)


def attend_block(query, keys, values, query_ids, key_ids, query_pos):
    scores = masked_scores(query, keys, query_ids, key_ids, query_pos)
    top = jnp.max(scores, axis=-1, keepdims=True)
    expd = jnp.exp(scores - top)
    total = jnp.sum(expd, axis=-1, keepdims=True)
    probs_low = (expd / total).astype(jnp.bfloat16)
    result = jnp.einsum("kgqs,skd->qkgd", probs_low, values, preferred_element_type=jnp.float32)
    return (result, top + jnp.log(total))


def attend_back(query, keys, values, query_ids, key_ids, query_pos, log_sum, grad_out):
    scale = query.shape[-1] ** (-0.5)
    scores = masked_scores(query, keys, query_ids, key_ids, query_pos)
    probs = jnp.exp(scores - log_sum)
    grad_probs = jnp.einsum("qkgd,skd->kgqs", grad_out, values, preferred_element_type=jnp.float32)
    inner = jnp.sum(probs * grad_probs, axis=-1, keepdims=True)
    grad_scores = (probs * (grad_probs - inner)).astype(jnp.bfloat16)
    grad_query = (
        jnp.einsum("kgqs,skd->qkgd", grad_scores, keys, preferred_element_type=jnp.float32) * scale
    )
    grad_keys = (
        jnp.einsum("kgqs,qkgd->skd", grad_scores, query, preferred_element_type=jnp.float32) * scale
    )
    grad_values = jnp.einsum(
        "kgqs,qkgd->skd", probs.astype(jnp.bfloat16), grad_out, preferred_element_type=jnp.float32
    )
    return (grad_query, grad_keys, grad_values)


def attention_forward(query, keys, values, segment_ids):
    length = query.shape[0]
    block = min(512, length)
    blocks = length // block
    positions = jnp.arange(length, dtype=jnp.int32)

    def one_block(index):
        start = index * block
        part = lax.dynamic_slice_in_dim(query, start, block, 0)
        part_ids = lax.dynamic_slice_in_dim(segment_ids, start, block, 0)
        part_pos = lax.dynamic_slice_in_dim(positions, start, block, 0)
        return attend_block(part, keys, values, part_ids, segment_ids, part_pos)

    results, log_sums = lax.map(one_block, jnp.arange(blocks, dtype=jnp.int32))
    return (results.reshape(query.shape), log_sums)


def attention_backward(query, keys, values, segment_ids, log_sums, grad_attended):
    length = query.shape[0]
    block = min(512, length)
    blocks = length // block
    positions = jnp.arange(length, dtype=jnp.int32)

    def one_block(carry, index):
        keys_acc, values_acc = carry
        start = index * block
        part = lax.dynamic_slice_in_dim(query, start, block, 0)
        part_ids = lax.dynamic_slice_in_dim(segment_ids, start, block, 0)
        part_pos = lax.dynamic_slice_in_dim(positions, start, block, 0)
        part_grad = lax.dynamic_slice_in_dim(grad_attended, start, block, 0)
        grad_query, grad_keys, grad_values = attend_back(
            part, keys, values, part_ids, segment_ids, part_pos, log_sums[index], part_grad
        )
        return ((keys_acc + grad_keys, values_acc + grad_values), grad_query)

    zeros = jnp.zeros(keys.shape, jnp.float32)
    (keys_acc, values_acc), query_grads = lax.scan(
        one_block, (zeros, zeros), jnp.arange(blocks, dtype=jnp.int32)
    )
    return (query_grads.reshape(query.shape), keys_acc, values_acc)


def shards(
    x_in,
    segment_ids,
    norm_in,
    mix_in,
    attn_in,
    attn_out,
    mix_out,
    norm_ff,
    ff_in,
    ff_out,
    conv_kernel,
    conv_bias,
    log_rate,
    dt_bias,
    skip,
    gate_norm,
    cotangent,
):
    sequences, length, model = x_in.shape
    tokens = sequences * length
    groups = AHEADS // KVHEADS
    full = (
        lax.all_gather(norm_in, "shard", axis=0, tiled=True),
        lax.all_gather(mix_in, "shard", axis=0, tiled=True),
        lax.all_gather(attn_in, "shard", axis=0, tiled=True),
        lax.all_gather(attn_out, "shard", axis=0, tiled=True),
        lax.all_gather(mix_out, "shard", axis=0, tiled=True),
        lax.all_gather(norm_ff, "shard", axis=0, tiled=True),
        lax.all_gather(ff_in, "shard", axis=0, tiled=True),
        lax.all_gather(ff_out, "shard", axis=0, tiled=True),
    )
    (
        full_norm_in,
        full_mix_in,
        full_attn_in,
        full_attn_out,
        full_mix_out,
        full_norm_ff,
        full_ff_in,
        full_ff_out,
    ) = full
    resid = x_in.reshape(tokens, model).astype(jnp.float32)
    first_normed, first_back = jax.vjp(normed, resid, full_norm_in.astype(jnp.float32))
    first_low = first_normed.astype(jnp.bfloat16)
    projected = matmul(first_low, full_mix_in)
    attn_proj = matmul(first_low, full_attn_in)

    def mixer_local(projection, kernel, kernel_bias, rates, biases, skips, gains):
        return mixer_core(projection, segment_ids, kernel, kernel_bias, rates, biases, skips, gains)

    mixed_norm, mixer_back = jax.vjp(
        mixer_local,
        projected.reshape(sequences, length, -1),
        conv_kernel.astype(jnp.float32),
        conv_bias.astype(jnp.float32),
        log_rate,
        dt_bias,
        skip,
        gate_norm.astype(jnp.float32),
    )
    mixed_low = mixed_norm.reshape(tokens, -1).astype(jnp.bfloat16)
    mixer_branch = matmul_nt(mixed_low, full_mix_out)
    cosine, sine = rotary_tables(length, HDIM)
    (query, keys, values), rotary_back = jax.vjp(
        partial(attention_inputs, cosine=cosine, sine=sine),
        attn_proj.reshape(sequences, length, -1),
    )
    query_low = query.astype(jnp.bfloat16).reshape(sequences, length, KVHEADS, groups, HDIM)
    keys_low = keys.astype(jnp.bfloat16)
    values_low = values.astype(jnp.bfloat16)
    attended, log_sums = lax.map(
        lambda item: attention_forward(item[0], item[1], item[2], item[3]),
        (query_low, keys_low, values_low, segment_ids),
    )
    attended_low = attended.reshape(tokens, -1).astype(jnp.bfloat16)
    attn_branch = matmul_nt(attended_low, full_attn_out)
    hidden = resid + attn_branch + mixer_branch
    second_normed, second_back = jax.vjp(normed, hidden, full_norm_ff.astype(jnp.float32))
    second_low = second_normed.astype(jnp.bfloat16)
    ff_proj = matmul(second_low, full_ff_in)
    activated, swiglu_back = jax.vjp(swiglu, ff_proj)
    act_low = activated.astype(jnp.bfloat16)
    ff_branch = matmul_nt(act_low, full_ff_out)
    output = (hidden + ff_branch).astype(jnp.bfloat16).reshape(x_in.shape)
    grad_out = cotangent.reshape(tokens, model)
    grad_act = matmul(grad_out, full_ff_out)
    grad_ff = swiglu_back(grad_act)[0].astype(jnp.bfloat16)
    grad_second = matmul_nt(grad_ff, full_ff_in)
    grad_hidden, norm_ff_grad = second_back(grad_second)
    grad_hidden = grad_hidden + grad_out.astype(jnp.float32)
    branch_low = grad_hidden.astype(jnp.bfloat16)
    grad_attended = matmul(branch_low, full_attn_out).astype(jnp.bfloat16)
    grad_mixed = matmul(branch_low, full_mix_out)
    mixer_grads = mixer_back(grad_mixed.reshape(sequences, length, -1))
    grad_projected = mixer_grads[0].reshape(tokens, -1).astype(jnp.bfloat16)
    grad_attended = grad_attended.reshape(sequences, length, KVHEADS, groups, HDIM)
    query_grad, keys_grad, values_grad = lax.map(
        lambda item: attention_backward(item[0], item[1], item[2], item[3], item[4], item[5]),
        (query_low, keys_low, values_low, segment_ids, log_sums, grad_attended),
    )
    grad_attn_proj = rotary_back(
        (query_grad.reshape(sequences, length, AHEADS, HDIM), keys_grad, values_grad)
    )[0]
    grad_attn_proj = grad_attn_proj.reshape(tokens, -1).astype(jnp.bfloat16)
    grad_first = matmul_nt(grad_projected, full_mix_in) + matmul_nt(grad_attn_proj, full_attn_in)
    grad_resid, norm_in_grad = first_back(grad_first)
    input_grad = (grad_resid + grad_hidden).astype(jnp.bfloat16).reshape(x_in.shape)
    ff_out_grad = matmul_tn(grad_out, act_low)
    ff_in_grad = matmul_tn(second_low, grad_ff)
    attn_out_grad = matmul_tn(branch_low, attended_low)
    mix_out_grad = matmul_tn(branch_low, mixed_low)
    mix_in_grad = matmul_tn(first_low, grad_projected)
    attn_in_grad = matmul_tn(first_low, grad_attn_proj)
    slices = (
        lax.psum_scatter(
            norm_in_grad.astype(jnp.bfloat16), "shard", scatter_dimension=0, tiled=True
        ).astype(jnp.float32),
        lax.psum_scatter(
            mix_in_grad.astype(jnp.bfloat16), "shard", scatter_dimension=0, tiled=True
        ).astype(jnp.float32),
        lax.psum_scatter(
            attn_in_grad.astype(jnp.bfloat16), "shard", scatter_dimension=0, tiled=True
        ).astype(jnp.float32),
        lax.psum_scatter(
            attn_out_grad.astype(jnp.bfloat16), "shard", scatter_dimension=0, tiled=True
        ).astype(jnp.float32),
        lax.psum_scatter(
            mix_out_grad.astype(jnp.bfloat16), "shard", scatter_dimension=0, tiled=True
        ).astype(jnp.float32),
        lax.psum_scatter(
            norm_ff_grad.astype(jnp.bfloat16), "shard", scatter_dimension=0, tiled=True
        ).astype(jnp.float32),
        lax.psum_scatter(
            ff_in_grad.astype(jnp.bfloat16), "shard", scatter_dimension=0, tiled=True
        ).astype(jnp.float32),
        lax.psum_scatter(
            ff_out_grad.astype(jnp.bfloat16), "shard", scatter_dimension=0, tiled=True
        ).astype(jnp.float32),
    )
    owned = (
        lax.psum(slices[0].astype(jnp.bfloat16), "rep").astype(jnp.float32),
        lax.psum(slices[1].astype(jnp.bfloat16), "rep").astype(jnp.float32),
        lax.psum(slices[2].astype(jnp.bfloat16), "rep").astype(jnp.float32),
        lax.psum(slices[3].astype(jnp.bfloat16), "rep").astype(jnp.float32),
        lax.psum(slices[4].astype(jnp.bfloat16), "rep").astype(jnp.float32),
        lax.psum(slices[5].astype(jnp.bfloat16), "rep").astype(jnp.float32),
        lax.psum(slices[6].astype(jnp.bfloat16), "rep").astype(jnp.float32),
        lax.psum(slices[7].astype(jnp.bfloat16), "rep").astype(jnp.float32),
    )
    small = lax.psum(
        (
            mixer_grads[1],
            mixer_grads[2],
            mixer_grads[3],
            mixer_grads[4],
            mixer_grads[5],
            mixer_grads[6],
        ),
        ("rep", "shard"),
    )
    return (
        output,
        input_grad,
        owned[0],
        owned[1],
        owned[2],
        owned[3],
        owned[4],
        owned[5],
        owned[6],
        owned[7],
        small[0],
        small[1],
        small[2],
        small[3],
        small[4],
        small[5],
    )


def solution(mesh):
    in_specs = (
        P(("rep", "shard"), None, None),
        P(("rep", "shard"), None),
        P("shard"),
        P("shard", None),
        P("shard", None),
        P("shard", None),
        P("shard", None),
        P("shard"),
        P("shard", None),
        P("shard", None),
        P(),
        P(),
        P(),
        P(),
        P(),
        P(),
        P(("rep", "shard"), None, None),
    )
    out_specs = (
        P(("rep", "shard"), None, None),
        P(("rep", "shard"), None, None),
        P("shard"),
        P("shard", None),
        P("shard", None),
        P("shard", None),
        P("shard", None),
        P("shard"),
        P("shard", None),
        P("shard", None),
        P(),
        P(),
        P(),
        P(),
        P(),
        P(),
    )
    return jax.shard_map(shards, mesh=mesh, in_specs=in_specs, out_specs=out_specs, check_vma=False)
```

profile of v0, /device:TPU:0, one launch (start us, length us, event | category | flops | bytes accessed | tf_op | source)
XLA Modules:
  0.0 1941.3 jit_solution(18012318960666142452)
XLA Ops:
  14.3 12.8 all-gather
  32.7 7.7 all-gather.1
  54.5 28.3 %while.93 = (s32[]{:T(128)}, bf16[2,512,2,4,64]{1,4,3,2,0:T(8,128)(2,1)S(1)}, f32[2,2,4,512,1]{3,2,1,4,0:T(4,128)S(1)}, s32[2]{0:T(128)S(1)}, s32[1024]{0:T(1024...) while((s32[]{:T(128)}, ...), condition=%wide.region_4.5_spmd, body=%wide.region_1.4_spmd.sunk | while | flops 1125642240 | bytes 54673616 | solution.py:213
  85.1 89.1 %all-gather.13.cloned.1.call-done = bf16[1024,3352]{0,1:T(8,128)(2,1)} async-done(((bf16[256,3352]{0,1:T(8,128)(2,1)}), bf16[1024,3352]{0,1:T(8,128)(2,1)}) %all-gather.13.cloned.1.call-update) | async-done | bytes 6864912 | tf_op jit(solution)/shard_map/all_gather | solution.py:266
  174.2 14.0 convolution_bitcast_fusion.8
  192.4 9.4 fusion.172
  219.0 309.7 %while.94 = (s32[]{:T(128)}, f32[1,24,64,128]{3,2,1,0:T(8,128)S(1)}, s32[1]{0:T(128)}, f32[8,1,128,24,64]{2,0,4,3,1:T(8,128)}, f32[8,1,24,64,128]{4,3,2,1,0:T(8,...) while((s32[]{:T(128)}, ...), condition=%wide.region_7.8_spmd.clone, body=%wide.region_5.7_spmd.clone.sunk | while | flops 935126272 | bytes 10140466 | solution.py:124
  235.3 20.8 %dynamic_update_slice.120 = f32[8,1,128,24,64]{2,0,4,3,1:T(8,128)} dynamic-update-slice(f32[8,1,128,24,64]{2,0,4,3,1:T(8,128)} %get-tuple-element.1569, f32[1,1,128,24,64]{2,0,4,3,1:T(1,128)S(1)} %bitcast.799, s32[]{:T(128)S(6)} %copy.331, s32[]{:T(128)} %constant.236.clone.1..sunk.1, s32[]{:T(128)} %constant.236.clone.1..sunk.1, s32[]{:T(128)} %constant.236.clone.1..sunk.1, ...) | dynamic-update-slice | bytes 1572868 | tf_op jit(solution)/shard_map/jvp(vmap())/while/body/jit(dynamic_update_index_in_dim)/dynamic_update_slice | solution.py:124
  273.9 20.9 %dynamic_update_slice.120 = f32[8,1,128,24,64]{2,0,4,3,1:T(8,128)} dynamic-update-slice(f32[8,1,128,24,64]{2,0,4,3,1:T(8,128)} %get-tuple-element.1569, f32[1,1,128,24,64]{2,0,4,3,1:T(1,128)S(1)} %bitcast.799, s32[]{:T(128)S(6)} %copy.331, s32[]{:T(128)} %constant.236.clone.1..sunk.1, s32[]{:T(128)} %constant.236.clone.1..sunk.1, s32[]{:T(128)} %constant.236.clone.1..sunk.1, ...) | dynamic-update-slice | bytes 1572868 | tf_op jit(solution)/shard_map/jvp(vmap())/while/body/jit(dynamic_update_index_in_dim)/dynamic_update_slice | solution.py:124
  312.7 20.8 %dynamic_update_slice.120 = f32[8,1,128,24,64]{2,0,4,3,1:T(8,128)} dynamic-update-slice(f32[8,1,128,24,64]{2,0,4,3,1:T(8,128)} %get-tuple-element.1569, f32[1,1,128,24,64]{2,0,4,3,1:T(1,128)S(1)} %bitcast.799, s32[]{:T(128)S(6)} %copy.331, s32[]{:T(128)} %constant.236.clone.1..sunk.1, s32[]{:T(128)} %constant.236.clone.1..sunk.1, s32[]{:T(128)} %constant.236.clone.1..sunk.1, ...) | dynamic-update-slice | bytes 1572868 | tf_op jit(solution)/shard_map/jvp(vmap())/while/body/jit(dynamic_update_index_in_dim)/dynamic_update_slice | solution.py:124
  341.0 5.3 fusion.344
  351.4 20.8 %dynamic_update_slice.120 = f32[8,1,128,24,64]{2,0,4,3,1:T(8,128)} dynamic-update-slice(f32[8,1,128,24,64]{2,0,4,3,1:T(8,128)} %get-tuple-element.1569, f32[1,1,128,24,64]{2,0,4,3,1:T(1,128)S(1)} %bitcast.799, s32[]{:T(128)S(6)} %copy.331, s32[]{:T(128)} %constant.236.clone.1..sunk.1, s32[]{:T(128)} %constant.236.clone.1..sunk.1, s32[]{:T(128)} %constant.236.clone.1..sunk.1, ...) | dynamic-update-slice | bytes 1572868 | tf_op jit(solution)/shard_map/jvp(vmap())/while/body/jit(dynamic_update_index_in_dim)/dynamic_update_slice | solution.py:124
  390.0 20.7 %dynamic_update_slice.120 = f32[8,1,128,24,64]{2,0,4,3,1:T(8,128)} dynamic-update-slice(f32[8,1,128,24,64]{2,0,4,3,1:T(8,128)} %get-tuple-element.1569, f32[1,1,128,24,64]{2,0,4,3,1:T(1,128)S(1)} %bitcast.799, s32[]{:T(128)S(6)} %copy.331, s32[]{:T(128)} %constant.236.clone.1..sunk.1, s32[]{:T(128)} %constant.236.clone.1..sunk.1, s32[]{:T(128)} %constant.236.clone.1..sunk.1, ...) | dynamic-update-slice | bytes 1572868 | tf_op jit(solution)/shard_map/jvp(vmap())/while/body/jit(dynamic_update_index_in_dim)/dynamic_update_slice | solution.py:124
  428.7 20.8 %dynamic_update_slice.120 = f32[8,1,128,24,64]{2,0,4,3,1:T(8,128)} dynamic-update-slice(f32[8,1,128,24,64]{2,0,4,3,1:T(8,128)} %get-tuple-element.1569, f32[1,1,128,24,64]{2,0,4,3,1:T(1,128)S(1)} %bitcast.799, s32[]{:T(128)S(6)} %copy.331, s32[]{:T(128)} %constant.236.clone.1..sunk.1, s32[]{:T(128)} %constant.236.clone.1..sunk.1, s32[]{:T(128)} %constant.236.clone.1..sunk.1, ...) | dynamic-update-slice | bytes 1572868 | tf_op jit(solution)/shard_map/jvp(vmap())/while/body/jit(dynamic_update_index_in_dim)/dynamic_update_slice | solution.py:124
  467.4 20.8 %dynamic_update_slice.120 = f32[8,1,128,24,64]{2,0,4,3,1:T(8,128)} dynamic-update-slice(f32[8,1,128,24,64]{2,0,4,3,1:T(8,128)} %get-tuple-element.1569, f32[1,1,128,24,64]{2,0,4,3,1:T(1,128)S(1)} %bitcast.799, s32[]{:T(128)S(6)} %copy.331, s32[]{:T(128)} %constant.236.clone.1..sunk.1, s32[]{:T(128)} %constant.236.clone.1..sunk.1, s32[]{:T(128)} %constant.236.clone.1..sunk.1, ...) | dynamic-update-slice | bytes 1572868 | tf_op jit(solution)/shard_map/jvp(vmap())/while/body/jit(dynamic_update_index_in_dim)/dynamic_update_slice | solution.py:124
  506.1 20.7 %dynamic_update_slice.120 = f32[8,1,128,24,64]{2,0,4,3,1:T(8,128)} dynamic-update-slice(f32[8,1,128,24,64]{2,0,4,3,1:T(8,128)} %get-tuple-element.1569, f32[1,1,128,24,64]{2,0,4,3,1:T(1,128)S(1)} %bitcast.799, s32[]{:T(128)S(6)} %copy.331, s32[]{:T(128)} %constant.236.clone.1..sunk.1, s32[]{:T(128)} %constant.236.clone.1..sunk.1, s32[]{:T(128)} %constant.236.clone.1..sunk.1, ...) | dynamic-update-slice | bytes 1572868 | tf_op jit(solution)/shard_map/jvp(vmap())/while/body/jit(dynamic_update_index_in_dim)/dynamic_update_slice | solution.py:124
  528.7 7.1 transpose.256
  535.8 10.5 multiply_reduce_fusion.9
  546.4 9.3 fusion.231
  555.8 6.6 multiply_reduce_fusion.12
  562.4 16.3 fusion.226
  578.7 17.2 fusion.206
  595.9 18.0 multiply_reduce_fusion.10
  626.3 158.2 %while.96 = (s32[]{:T(128)}, f32[1024,2,64]{0,2,1:T(8,128)}, f32[1024,2,64]{0,2,1:T(8,128)}, f32[2,512,2,4,64]{1,0,4,3,2:T(2,128)}, s32[2]{0:T(128)S(1)}, /*inde...) while((s32[]{:T(128)}, f32[1024,2,64]{0,2,1:T(8,128)}, ...), condition=%wide.region_26.27_spmd.clone, body=%wide.region_24.26_spmd.clone.sunk | while | flops 2749755392 | bytes 230654768 | solution.py:236
  628.1 8.2 fusion.383
  640.3 15.3 fusion.385
  656.9 10.8 fusion.386
  667.7 6.1 fusion.387
  673.8 8.2 fusion.388
  685.8 19.6 %dynamic_update_slice.126 = f32[2,512,2,4,64]{1,0,4,3,2:T(2,128)} dynamic-update-slice(f32[2,512,2,4,64]{1,0,4,3,2:T(2,128)} %get-tuple-element.1715, f32[1,512,2,4,64]{1,0,4,3,2:T(1,128)S(1)} %copy.313, s32[]{:T(128)S(6)} %copy.377, s32[]{:T(128)} %constant.236.clone.1..sunk.3, s32[]{:T(128)} %constant.236.clone.1..sunk.3, s32[]{:T(128)} %constant.236.clone.1..sunk.3, s32[]{:T(128)} %constant.236.clone.1..sunk.3) | dynamic-update-slice | bytes 2097156 | tf_op jit(solution)/shard_map/while/body/eval_jaxpr/while/body/jit(dynamic_update_index_in_dim)/dynamic_update_slice | solution.py:213
  706.9 8.2 fusion.383
  719.1 15.3 fusion.385
  735.7 10.8 fusion.386
  746.5 6.1 fusion.387
  752.6 8.2 fusion.388
  764.6 19.6 %dynamic_update_slice.126 = f32[2,512,2,4,64]{1,0,4,3,2:T(2,128)} dynamic-update-slice(f32[2,512,2,4,64]{1,0,4,3,2:T(2,128)} %get-tuple-element.1715, f32[1,512,2,4,64]{1,0,4,3,2:T(1,128)S(1)} %copy.313, s32[]{:T(128)S(6)} %copy.377, s32[]{:T(128)} %constant.236.clone.1..sunk.3, s32[]{:T(128)} %constant.236.clone.1..sunk.3, s32[]{:T(128)} %constant.236.clone.1..sunk.3, s32[]{:T(128)} %constant.236.clone.1..sunk.3) | dynamic-update-slice | bytes 2097156 | tf_op jit(solution)/shard_map/while/body/eval_jaxpr/while/body/jit(dynamic_update_index_in_dim)/dynamic_update_slice | solution.py:213
  794.7 7.0 fusion.176
  804.8 16.1 multiply_reduce_fusion.8
  837.7 608.3 %while.95 = (s32[]{:T(128)}, f32[1,24,64,128]{3,2,1,0:T(8,128)}, f32[8,1,128,24,64]{2,0,4,3,1:T(8,128)}, f32[8,1,128,24]{3,2,1,0:T(8,128)}, f32[8,1,128,24]{3,2,...) while((s32[]{:T(128)}, f32[1,24,64,128]{3,2,1,0:T(8,128)}, ...), condition=%wide.region_23.24_spmd.clone, body=%wide.region_12.23_spmd.clone.sunk | while | flops 2200954112 | bytes 25661920 | solution.py:124
  866.4 20.8 %dynamic_update_slice.124 = f32[8,1,128,24,64]{2,0,4,3,1:T(8,128)} dynamic-update-slice(f32[8,1,128,24,64]{2,0,4,3,1:T(8,128)} %get-tuple-element.1657, f32[1,1,128,24,64]{2,0,4,3,1:T(1,128)} %bitcast.808, s32[]{:T(128)S(6)} %sub.404, s32[]{:T(128)} %constant.236.clone.1..sunk.2, s32[]{:T(128)} %constant.236.clone.1..sunk.2, s32[]{:T(128)} %constant.236.clone.1..sunk.2, s32[]{:T(128)} %constant.236.clone.1..sunk.2) | dynamic-update-slice | bytes 1572868 | tf_op jit(solution)/shard_map/transpose(jvp(vmap()))/while/body/jit(dynamic_update_index_in_dim)/dynamic_update_slice | solution.py:124
  942.6 20.8 %dynamic_update_slice.124 = f32[8,1,128,24,64]{2,0,4,3,1:T(8,128)} dynamic-update-slice(f32[8,1,128,24,64]{2,0,4,3,1:T(8,128)} %get-tuple-element.1657, f32[1,1,128,24,64]{2,0,4,3,1:T(1,128)} %bitcast.808, s32[]{:T(128)S(6)} %sub.404, s32[]{:T(128)} %constant.236.clone.1..sunk.2, s32[]{:T(128)} %constant.236.clone.1..sunk.2, s32[]{:T(128)} %constant.236.clone.1..sunk.2, s32[]{:T(128)} %constant.236.clone.1..sunk.2) | dynamic-update-slice | bytes 1572868 | tf_op jit(solution)/shard_map/transpose(jvp(vmap()))/while/body/jit(dynamic_update_index_in_dim)/dynamic_update_slice | solution.py:124
  1018.7 20.8 %dynamic_update_slice.124 = f32[8,1,128,24,64]{2,0,4,3,1:T(8,128)} dynamic-update-slice(f32[8,1,128,24,64]{2,0,4,3,1:T(8,128)} %get-tuple-element.1657, f32[1,1,128,24,64]{2,0,4,3,1:T(1,128)} %bitcast.808, s32[]{:T(128)S(6)} %sub.404, s32[]{:T(128)} %constant.236.clone.1..sunk.2, s32[]{:T(128)} %constant.236.clone.1..sunk.2, s32[]{:T(128)} %constant.236.clone.1..sunk.2, s32[]{:T(128)} %constant.236.clone.1..sunk.2) | dynamic-update-slice | bytes 1572868 | tf_op jit(solution)/shard_map/transpose(jvp(vmap()))/while/body/jit(dynamic_update_index_in_dim)/dynamic_update_slice | solution.py:124
  1094.8 20.8 %dynamic_update_slice.124 = f32[8,1,128,24,64]{2,0,4,3,1:T(8,128)} dynamic-update-slice(f32[8,1,128,24,64]{2,0,4,3,1:T(8,128)} %get-tuple-element.1657, f32[1,1,128,24,64]{2,0,4,3,1:T(1,128)} %bitcast.808, s32[]{:T(128)S(6)} %sub.404, s32[]{:T(128)} %constant.236.clone.1..sunk.2, s32[]{:T(128)} %constant.236.clone.1..sunk.2, s32[]{:T(128)} %constant.236.clone.1..sunk.2, s32[]{:T(128)} %constant.236.clone.1..sunk.2) | dynamic-update-slice | bytes 1572868 | tf_op jit(solution)/shard_map/transpose(jvp(vmap()))/while/body/jit(dynamic_update_index_in_dim)/dynamic_update_slice | solution.py:124
  1170.9 20.8 %dynamic_update_slice.124 = f32[8,1,128,24,64]{2,0,4,3,1:T(8,128)} dynamic-update-slice(f32[8,1,128,24,64]{2,0,4,3,1:T(8,128)} %get-tuple-element.1657, f32[1,1,128,24,64]{2,0,4,3,1:T(1,128)} %bitcast.808, s32[]{:T(128)S(6)} %sub.404, s32[]{:T(128)} %constant.236.clone.1..sunk.2, s32[]{:T(128)} %constant.236.clone.1..sunk.2, s32[]{:T(128)} %constant.236.clone.1..sunk.2, s32[]{:T(128)} %constant.236.clone.1..sunk.2) | dynamic-update-slice | bytes 1572868 | tf_op jit(solution)/shard_map/transpose(jvp(vmap()))/while/body/jit(dynamic_update_index_in_dim)/dynamic_update_slice | solution.py:124
  1247.0 20.8 %dynamic_update_slice.124 = f32[8,1,128,24,64]{2,0,4,3,1:T(8,128)} dynamic-update-slice(f32[8,1,128,24,64]{2,0,4,3,1:T(8,128)} %get-tuple-element.1657, f32[1,1,128,24,64]{2,0,4,3,1:T(1,128)} %bitcast.808, s32[]{:T(128)S(6)} %sub.404, s32[]{:T(128)} %constant.236.clone.1..sunk.2, s32[]{:T(128)} %constant.236.clone.1..sunk.2, s32[]{:T(128)} %constant.236.clone.1..sunk.2, s32[]{:T(128)} %constant.236.clone.1..sunk.2) | dynamic-update-slice | bytes 1572868 | tf_op jit(solution)/shard_map/transpose(jvp(vmap()))/while/body/jit(dynamic_update_index_in_dim)/dynamic_update_slice | solution.py:124
  1323.1 20.8 %dynamic_update_slice.124 = f32[8,1,128,24,64]{2,0,4,3,1:T(8,128)} dynamic-update-slice(f32[8,1,128,24,64]{2,0,4,3,1:T(8,128)} %get-tuple-element.1657, f32[1,1,128,24,64]{2,0,4,3,1:T(1,128)} %bitcast.808, s32[]{:T(128)S(6)} %sub.404, s32[]{:T(128)} %constant.236.clone.1..sunk.2, s32[]{:T(128)} %constant.236.clone.1..sunk.2, s32[]{:T(128)} %constant.236.clone.1..sunk.2, s32[]{:T(128)} %constant.236.clone.1..sunk.2) | dynamic-update-slice | bytes 1572868 | tf_op jit(solution)/shard_map/transpose(jvp(vmap()))/while/body/jit(dynamic_update_index_in_dim)/dynamic_update_slice | solution.py:124
  1399.2 20.8 %dynamic_update_slice.124 = f32[8,1,128,24,64]{2,0,4,3,1:T(8,128)} dynamic-update-slice(f32[8,1,128,24,64]{2,0,4,3,1:T(8,128)} %get-tuple-element.1657, f32[1,1,128,24,64]{2,0,4,3,1:T(1,128)} %bitcast.808, s32[]{:T(128)S(6)} %sub.404, s32[]{:T(128)} %constant.236.clone.1..sunk.2, s32[]{:T(128)} %constant.236.clone.1..sunk.2, s32[]{:T(128)} %constant.236.clone.1..sunk.2, s32[]{:T(128)} %constant.236.clone.1..sunk.2) | dynamic-update-slice | bytes 1572868 | tf_op jit(solution)/shard_map/transpose(jvp(vmap()))/while/body/jit(dynamic_update_index_in_dim)/dynamic_update_slice | solution.py:124
  1446.1 7.2 transpose.261
  1455.1 9.4 convert_bitcast_fusion.1
  1464.6 5.4 multiply_add_fusion.1
  1470.0 17.8 fusion.234
  1487.9 6.2 multiply_select_fusion.2
  1494.1 11.2 fusion.169
  1505.4 14.9 convolution_convert_fusion.1
  1520.9 17.8 convolution_convert_fusion
  1540.6 14.3 fusion.228
  1555.0 108.0 %reduce-scatter.7.cloned.1.call-done = bf16[256,3352]{0,1:T(8,128)(2,1)} async-done(((bf16[1024,3352]{0,1:T(8,128)(2,1)}), bf16[256,3352]{0,1:T(8,128)(2,1)}) %reduce-scatter.7.cloned.1.call-update) | async-done | bytes 1716240 | tf_op jit(solution)/shard_map/reduce_scatter | solution.py:360
  1663.0 147.4 %reduce-scatter.15.cloned.1.call-done = bf16[256,4096]{1,0:T(8,128)(2,1)} async-done(((bf16[1024,4096]{1,0:T(8,128)(2,1)}), bf16[256,4096]{1,0:T(8,128)(2,1)}) %reduce-scatter.15.cloned.1.call-update) | async-done | bytes 2097168 | tf_op jit(solution)/shard_map/reduce_scatter | solution.py:375
  1810.4 10.6 fusion.198
  1825.1 5.9 fusion.187
  1839.3 10.9 all-reduce.35
  1850.4 12.3 all-reduce.33
  1864.1 39.5 %all-reduce.32 = (f32[4,1792]{1,0:T(4,128)}, f32[1792]{0:T(1024)}, f32[24]{0:T(128)}, f32[24]{0:T(128)}, f32[24]{0:T(128)}, /*index=5*/f32[1536]{0:T(1024)}) all-reduce(f32[4,1792]{1,0:T(4,128)S(1)} %pad_add_fusion.2, f32[1792]{0:T(1024)S(1)} %get-tuple-element.1010, ...), channel_id=1, replica_groups=mesh['rep'=8,'shard'=4] {'rep','shard'}, use_global_device_ids=true, to_apply=%region_50.51 | all-reduce | flops 10568 | bytes 84544 | tf_op jit(solution)/shard_map/psum | solution.py:392
  1903.5 18.7 all-reduce.38.cloned.1.call-done
  (1002 shorter events, 721.5 us)
Async XLA Ops:
  7.2 21.0 %copy-start.32 = (s32[1,1024]{1,0:T(1,128)S(1)}, s32[1,1024]{1,0:T(1,128)}, u32[]{:S(2)}) copy-start(s32[1,1024]{1,0:T(1,128)} %param.26) | copy-start | bytes 12292
  7.2 21.7 %copy-start.88 = (bf16[4,1792]{1,0:T(4,128)(2,1)S(1)}, bf16[4,1792]{1,0:T(4,128)(2,1)}, u32[]{:S(2)}) copy-start(bf16[4,1792]{1,0:T(4,128)(2,1)} %param.35) | copy-start | bytes 43012
  7.2 22.4 %copy-start.90 = (bf16[1792]{0:T(1024)(128)(2,1)S(1)}, bf16[1792]{0:T(1024)(128)(2,1)}, u32[]{:S(2)}) copy-start(bf16[1792]{0:T(1024)(128)(2,1)} %param.36) | copy-start | bytes 10756
  7.2 22.9 %copy-start.101 = (f32[24]{0:T(128)S(1)}, f32[24]{0:T(128)}, u32[]{:S(2)}) copy-start(f32[24]{0:T(128)} %param.37) | copy-start | bytes 292
  7.2 23.5 %copy-start.97 = (f32[24]{0:T(128)S(1)}, f32[24]{0:T(128)}, u32[]{:S(2)}) copy-start(f32[24]{0:T(128)} %param.39) | copy-start | bytes 292
  7.2 42.3 %all-gather.9.cloned.1.call-start = ((), (), s32[]{:S(2)}) async-start(), calls=%async_computation.6 | async-start | bytes 1966080 | tf_op jit(solution)/shard_map/all_gather | solution.py:267
  8.0 23.5 %copy-start.91 = (bf16[1536]{0:T(1024)(128)(2,1)S(1)}, bf16[1536]{0:T(1024)(128)(2,1)}, u32[]{:S(2)}) copy-start(bf16[1536]{0:T(1024)(128)(2,1)} %param.40) | copy-start | bytes 9220
  8.0 24.7 %copy-start.100 = (bf16[256]{0:T(256)(128)(2,1)S(1)}, bf16[256]{0:T(256)(128)(2,1)}, u32[]{:S(2)}) copy-start(bf16[256]{0:T(256)(128)(2,1)} %param.32) | copy-start | bytes 1540
  8.0 166.2 %all-gather.13.cloned.1.call-start = ((), (), s32[]{:S(2)}) async-start(), calls=%async_computation.8 | async-start | bytes 8581120 | tf_op jit(solution)/shard_map/all_gather | solution.py:266
  8.7 537.6 %all-gather.15.cloned.1.call-start = ((), (), s32[]{:S(2)}) async-start(), calls=%async_computation.9 | async-start | bytes 3932160 | tf_op jit(solution)/shard_map/all_gather | solution.py:269
  9.5 546.2 %all-gather.11.cloned.1.call-start = ((), (), s32[]{:S(2)}) async-start(), calls=%async_computation.7 | async-start | bytes 1310720 | tf_op jit(solution)/shard_map/all_gather | solution.py:268
  10.1 552.3 %all-gather.17.cloned.1.call-start = ((), (), s32[]{:S(2)}) async-start(), calls=%async_computation.10 | async-start | bytes 10485760 | tf_op jit(solution)/shard_map/all_gather | solution.py:271
  10.6 568.0 %all-gather.19.cloned.1.call-start = ((), (), s32[]{:S(2)}) async-start(), calls=%async_computation.11 | async-start | bytes 5242880 | tf_op jit(solution)/shard_map/all_gather | solution.py:272
  11.2 1543.7 %reduce-scatter.11.cloned.1.call-start = ((), (), s32[]{:S(2)}) async-start(), calls=%async_computation.14 | async-start | bytes 1310720 | tf_op jit(solution)/shard_map/reduce_scatter | solution.py:366
  14.3 38.7 %copy-start.7 = (bf16[1,1024,1024]{1,2,0:T(8,128)(2,1)}, bf16[1,1024,1024]{1,2,0:T(8,128)(2,1)S(1)}, u32[]{:S(2)}) copy-start(bf16[1,1024,1024]{1,2,0:T(8,128)(2,1)S(1)} %copy.180) | copy-start | bytes 6291460
  27.1 25.9 %copy-start.78 = (f32[4,1,256]{2,1,0:T(1,128)}, f32[4,1,256]{2,1,0:T(1,128)S(1)}, u32[]{:S(2)}) copy-start(f32[4,1,256]{2,1,0:T(1,128)S(1)} %convert_element_type.227) | copy-start | bytes 12292
  27.6 25.4 %copy-start.82 = (f32[1024]{0:T(1024)}, f32[1024]{0:T(1024)S(1)}, u32[]{:S(2)}) copy-start(f32[1024]{0:T(1024)S(1)} %fusion.219) | copy-start | bytes 12292
  32.7 21.0 %copy-start.18 = (f32[1024,32]{0,1:T(8,128)}, f32[1024,32]{0,1:T(8,128)S(1)}, u32[]{:S(2)}) copy-start(f32[1024,32]{0,1:T(8,128)S(1)} %get-tuple-element.1184) | copy-start | bytes 393220
  32.7 21.0 %copy-start.20 = (f32[1024,32]{0,1:T(8,128)}, f32[1024,32]{0,1:T(8,128)S(1)}, u32[]{:S(2)}) copy-start(f32[1024,32]{0,1:T(8,128)S(1)} %get-tuple-element.1185) | copy-start | bytes 393220
  54.4 119.8 %copy-start.79 = (f32[4,1,256]{2,1,0:T(1,128)S(1)}, f32[4,1,256]{2,1,0:T(1,128)}, u32[]{:S(2)}) copy-start(f32[4,1,256]{2,1,0:T(1,128)} %copy-done.78) | copy-start | bytes 12292
  54.5 119.8 %copy-start.83 = (f32[1024]{0:T(1024)S(1)}, f32[1024]{0:T(1024)}, u32[]{:S(2)}) copy-start(f32[1024]{0:T(1024)} %copy-done.82) | copy-start | bytes 12292
  82.8 105.5 %copy-start.13 = (bf16[1024,2,64]{0,2,1:T(8,128)(2,1)}, bf16[1024,2,64]{0,2,1:T(8,128)(2,1)S(1)}, u32[]{:S(2)}) copy-start(bf16[1024,2,64]{0,2,1:T(8,128)(2,1)S(1)} %get-tuple-element.1773) | copy-start | bytes 786436
  82.8 105.5 %copy-start.42 = (f32[2,2,4,512,1]{3,2,1,4,0:T(4,128)}, f32[2,2,4,512,1]{3,2,1,4,0:T(4,128)S(1)}, u32[]{:S(2)}) copy-start(f32[2,2,4,512,1]{3,2,1,4,0:T(4,128)S(1)} %get-tuple-element.1704) | copy-start | bytes 98308
  562.4 51.5 %copy-start.62 = (f32[1024]{0:T(1024)}, f32[1024]{0:T(1024)S(1)}, u32[]{:S(2)}) copy-start(f32[1024]{0:T(1024)S(1)} %fusion.221) | copy-start | bytes 12292
  595.9 18.0 copy-start.10
  640.3 15.3 slice-start
  640.3 15.3 slice-start.1
  640.3 15.3 slice-start.2
  640.3 16.6 slice-start.3
  682.0 23.4 %copy-start.104 = (f32[1024,2,64]{0,2,1:T(8,128)}, f32[1024,2,64]{0,2,1:T(8,128)S(1)}, u32[]{:S(2)}) copy-start(f32[1024,2,64]{0,2,1:T(8,128)S(1)} %fusion.388) | copy-start | bytes 1572868 | tf_op jit(solution)/shard_map/while/body/eval_jaxpr/while
  682.0 23.4 %copy-start.3 = (bf16[1024,2,4,64]{0,3,2,1:T(8,128)(2,1)S(1)}, bf16[1024,2,4,64]{0,3,2,1:T(8,128)(2,1)}, u32[]{:S(2)}) copy-start(bf16[1024,2,4,64]{0,3,2,1:T(8,128)(2,1)} %copy-done.2) | copy-start | bytes 3145732 | tf_op jit(solution)/shard_map/while/body/eval_jaxpr/while
  682.1 23.4 %copy-start.57 = (s32[1024]{0:T(1024)S(1)}, s32[1024]{0:T(1024)}, u32[]{:S(2)}) copy-start(s32[1024]{0:T(1024)} %copy-done.56) | copy-start | bytes 12292 | tf_op jit(solution)/shard_map/while/body/eval_jaxpr/while
  682.1 23.4 %copy-start.109 = (s32[2]{0:T(128)S(1)}, s32[2]{0:T(128)}, u32[]{:S(2)}) copy-start(s32[2]{0:T(128)} %copy-done.108) | copy-start | bytes 28 | tf_op jit(solution)/shard_map/while/body/eval_jaxpr/while
  719.1 15.3 slice-start
  719.1 15.3 slice-start.1
  719.1 15.3 slice-start.2
  719.1 16.6 slice-start.3
  760.8 23.4 %copy-start.104 = (f32[1024,2,64]{0,2,1:T(8,128)}, f32[1024,2,64]{0,2,1:T(8,128)S(1)}, u32[]{:S(2)}) copy-start(f32[1024,2,64]{0,2,1:T(8,128)S(1)} %fusion.388) | copy-start | bytes 1572868 | tf_op jit(solution)/shard_map/while/body/eval_jaxpr/while
  760.9 23.4 %copy-start.3 = (bf16[1024,2,4,64]{0,3,2,1:T(8,128)(2,1)S(1)}, bf16[1024,2,4,64]{0,3,2,1:T(8,128)(2,1)}, u32[]{:S(2)}) copy-start(bf16[1024,2,4,64]{0,3,2,1:T(8,128)(2,1)} %copy-done.2) | copy-start | bytes 3145732 | tf_op jit(solution)/shard_map/while/body/eval_jaxpr/while
  760.9 23.4 %copy-start.57 = (s32[1024]{0:T(1024)S(1)}, s32[1024]{0:T(1024)}, u32[]{:S(2)}) copy-start(s32[1024]{0:T(1024)} %copy-done.56) | copy-start | bytes 12292 | tf_op jit(solution)/shard_map/while/body/eval_jaxpr/while
  760.9 23.4 %copy-start.109 = (s32[2]{0:T(128)S(1)}, s32[2]{0:T(128)}, u32[]{:S(2)}) copy-start(s32[2]{0:T(128)} %copy-done.108) | copy-start | bytes 28 | tf_op jit(solution)/shard_map/while/body/eval_jaxpr/while
  789.9 765.0 %reduce-scatter.9.cloned.1.call-start = ((), (), s32[]{:S(2)}) async-start(), calls=%async_computation.13 | async-start | bytes 1966080 | tf_op jit(solution)/shard_map/reduce_scatter | solution.py:363
  804.8 21.0 %slice-start.8 = ((s8[6291456]{0:T(1024)(128)(4,1)}), s8[2097152]{0:T(1024)(128)(4,1)S(1)}, s32[]{:S(2)}) async-start(s8[6291456]{0:T(1024)(128)(4,1)} %bitcast.805), calls=%async_computation.27 | async-start | bytes 4194304
  804.8 750.2 %reduce-scatter.13.cloned.1.call-start = ((), (), s32[]{:S(2)}) async-start(), calls=%async_computation.15 | async-start | bytes 3932160 | tf_op jit(solution)/shard_map/reduce_scatter | solution.py:369
  804.8 20.9 %slice-start.9 = ((s8[6291456]{0:T(1024)(128)(4,1)}), s8[4194304]{0:T(1024)(128)(4,1)S(1)}, s32[]{:S(2)}) async-start(s8[6291456]{0:T(1024)(128)(4,1)} %bitcast.805), calls=%async_computation.28 | async-start | bytes 8388608
  830.9 724.0 %reduce-scatter.17.cloned.1.call-start = ((), (), s32[]{:S(2)}) async-start(), calls=%async_computation.17 | async-start | bytes 5242880 | tf_op jit(solution)/shard_map/reduce_scatter | solution.py:378
  855.5 31.8 %copy-start.31 = (f32[128,128]{1,0:T(8,128)}, f32[128,128]{1,0:T(8,128)S(1)}, u32[]{:S(2)}) copy-start(f32[128,128]{1,0:T(8,128)S(1)} %fusion.364) | copy-start | bytes 196612 | tf_op jit(solution)/shard_map/transpose(jvp(vmap()))/while
  931.6 31.8 %copy-start.31 = (f32[128,128]{1,0:T(8,128)}, f32[128,128]{1,0:T(8,128)S(1)}, u32[]{:S(2)}) copy-start(f32[128,128]{1,0:T(8,128)S(1)} %fusion.364) | copy-start | bytes 196612 | tf_op jit(solution)/shard_map/transpose(jvp(vmap()))/while
  1007.7 31.8 %copy-start.31 = (f32[128,128]{1,0:T(8,128)}, f32[128,128]{1,0:T(8,128)S(1)}, u32[]{:S(2)}) copy-start(f32[128,128]{1,0:T(8,128)S(1)} %fusion.364) | copy-start | bytes 196612 | tf_op jit(solution)/shard_map/transpose(jvp(vmap()))/while
  1083.8 31.8 %copy-start.31 = (f32[128,128]{1,0:T(8,128)}, f32[128,128]{1,0:T(8,128)S(1)}, u32[]{:S(2)}) copy-start(f32[128,128]{1,0:T(8,128)S(1)} %fusion.364) | copy-start | bytes 196612 | tf_op jit(solution)/shard_map/transpose(jvp(vmap()))/while
  1159.9 31.8 %copy-start.31 = (f32[128,128]{1,0:T(8,128)}, f32[128,128]{1,0:T(8,128)S(1)}, u32[]{:S(2)}) copy-start(f32[128,128]{1,0:T(8,128)S(1)} %fusion.364) | copy-start | bytes 196612 | tf_op jit(solution)/shard_map/transpose(jvp(vmap()))/while
  1236.0 31.8 %copy-start.31 = (f32[128,128]{1,0:T(8,128)}, f32[128,128]{1,0:T(8,128)S(1)}, u32[]{:S(2)}) copy-start(f32[128,128]{1,0:T(8,128)S(1)} %fusion.364) | copy-start | bytes 196612 | tf_op jit(solution)/shard_map/transpose(jvp(vmap()))/while
  1312.1 31.8 %copy-start.31 = (f32[128,128]{1,0:T(8,128)}, f32[128,128]{1,0:T(8,128)S(1)}, u32[]{:S(2)}) copy-start(f32[128,128]{1,0:T(8,128)S(1)} %fusion.364) | copy-start | bytes 196612 | tf_op jit(solution)/shard_map/transpose(jvp(vmap()))/while
  1388.2 31.8 %copy-start.31 = (f32[128,128]{1,0:T(8,128)}, f32[128,128]{1,0:T(8,128)S(1)}, u32[]{:S(2)}) copy-start(f32[128,128]{1,0:T(8,128)S(1)} %fusion.364) | copy-start | bytes 196612 | tf_op jit(solution)/shard_map/transpose(jvp(vmap()))/while
  1464.5 198.5 %reduce-scatter.7.cloned.1.call-start = ((), (), s32[]{:S(2)}) async-start(), calls=%async_computation.12 | async-start | bytes 8581120 | tf_op jit(solution)/shard_map/reduce_scatter | solution.py:360
  1470.0 17.9 copy-start.51
  1470.0 17.9 copy-start.53
  1470.0 17.9 copy-start.55
  1520.3 290.1 %reduce-scatter.15.cloned.1.call-start = ((), (), s32[]{:S(2)}) async-start(), calls=%async_computation.16 | async-start | bytes 10485760 | tf_op jit(solution)/shard_map/reduce_scatter | solution.py:375
  1538.7 383.6 %all-reduce.38.cloned.1.call-start = ((), (), s32[]{:S(2)}) async-start(), calls=%async_computation.18 | async-start | bytes 12607488 | tf_op jit(solution)/shard_map/psum | solution.py:390
  1810.4 14.7 copy-start.39
  1831.8 32.1 %copy-start.70 = (f32[1536]{0:T(1024)S(1)}, f32[1536]{0:T(1024)}, u32[]{:S(2)}) copy-start(f32[1536]{0:T(1024)} %get-tuple-element.1142) | copy-start | bytes 18436
  1831.8 32.3 %copy-start.102 = (f32[24]{0:T(128)S(1)}, f32[24]{0:T(128)}, u32[]{:S(2)}) copy-start(f32[24]{0:T(128)} %param.37) | copy-start | bytes 292
  1831.8 32.3 %copy-start.89 = (f32[1536]{0:T(1024)S(1)}, f32[1536]{0:T(1024)}, u32[]{:S(2)}) copy-start(f32[1536]{0:T(1024)} %get-tuple-element.1006) | copy-start | bytes 18436
  (113 other events, 706.9 us)
Sparse Core Ops, SparseCore 0:
  9.6 39.8 all-gather.8
  51.1 123.0 all-gather.12
  175.8 61.6 all-gather.14
  239.0 26.5 all-gather.10
  267.0 149.1 all-gather.16
  417.6 78.9 all-gather.18
  790.0 25.3 reduce-scatter.10
  818.4 33.9 reduce-scatter.8
  855.4 59.1 reduce-scatter.12
  1464.6 75.2 reduce-scatter.16
  1542.2 120.7 reduce-scatter.6
  1665.3 144.9 reduce-scatter.14
  1815.0 107.2 all-reduce.37
where the time goes:
time: 1970 us; the launch traced here: 1940 us
  local copies, waits for them, and re-layouts  664 us (34%)
  matrix products  517 us (26%)
  waiting for transfers between devices  372 us (19%)
  other arithmetic  258 us (13%)
  blocking collectives  83.1 us (4%)
  loops' own time  30.8 us (2%)
    dynamic_update_slice x32, local copies, waits for them, and re-layouts, ssd_sequence(): lax.scan(jax.checkpoint(scan_block), initial, (cut(inputs), cut(step_size...  366 us
    reduce_scatter x1, waiting for transfers between devices, shards(): lax.psum_scatter(ff_in_grad.astype(jnp.bfloat16), 'shard', scatter_dimens...  147 us
    dot_general x24, matrix products, scan_block(): within = jnp.einsum('hts,shp->thp', mixing, inputs, precision=HIGH)  115 us
    reduce_scatter x1, waiting for transfers between devices, shards(): lax.psum_scatter(mix_in_grad.astype(jnp.bfloat16), 'shard', scatter_dimen...  108 us
    all_gather x1, waiting for transfers between devices, shards(): lax.all_gather(mix_in, 'shard', axis=0, tiled=True)  89.1 us
    dot_general x6, matrix products, matmul_nt(): lax.dot_general(left, right, (((1,), (1,)), ((), ())), preferred_element_...  64.8 us
    dot_general x6, matrix products, matmul(): return jnp.dot(left, right, preferred_element_type=jnp.float32)  61.9 us
    dot_general x24, matrix products, scan_block(): jnp.einsum('shp,sn->hpn', inputs * (leaving * step_sizes)[:, :, None], b_...  53.7 us
  transfers between devices with their start and end apart: 13, of which 5 were waited for; matrix products, arithmetic and copies ran while one was open for 62% of the time, Pallas kernels for 0%

commit v1 on v0

v1 whole, which is shorter than its diff:
```python
from functools import partial
import math

import jax
import jax.numpy as jnp
from jax import lax
from jax.experimental import pallas as pl
from jax.experimental.pallas import tpu as pltpu
from jax.sharding import PartitionSpec as P

AHEADS = 8
KVHEADS = 2
HDIM = 64
CONV = 4
EPS = 1e-05
THETA = 100000000000.0
HIGH = lax.Precision.HIGHEST
F32 = jnp.float32
BF16 = jnp.bfloat16
LANES = 128
CHUNK = 128
QBLOCK = 256
LONGEST = 512


def dot_nn(left, right, precision=None):
    return lax.dot_general(
        left, right, (((1,), (0,)), ((), ())), precision=precision, preferred_element_type=F32
    )


def dot_nt(left, right):
    return lax.dot_general(left, right, (((1,), (1,)), ((), ())), preferred_element_type=F32)


def dot_tn(left, right):
    return lax.dot_general(left, right, (((0,), (0,)), ((), ())), preferred_element_type=F32)


def sigmoid(values):
    return 0.5 * jnp.tanh(0.5 * values) + 0.5


def softplus(values):
    return jnp.maximum(values, 0.0) + jnp.log1p(jnp.exp(-jnp.abs(values)))


def iota(shape, axis):
    return lax.broadcasted_iota(jnp.int32, shape, axis)


def split_low(values):
    high = values.astype(BF16)
    return high, (values - high.astype(F32)).astype(BF16)


def turn(values, cosine, sine, sign):
    lane = iota(values.shape, 1)
    partner = jnp.where(
        (lane % HDIM) < HDIM // 2,
        -pltpu.roll(values, LANES - HDIM // 2, 1),
        pltpu.roll(values, HDIM // 2, 1),
    )
    return values * cosine + sign * partner * sine


def twice(values, head, low_half):
    swapped = pltpu.roll(values, HDIM, 1)
    return jnp.where(low_half == (head == 0), values, swapped)


def attention_fwd_kernel(proj_ref, cos_ref, sin_ref, idc_ref, idr_ref, q_ref, k_ref, v_ref, out_ref, lse_ref, k2_ref, v2_ref):
    length = proj_ref.shape[0]
    pairs = AHEADS // 2
    cosine = cos_ref[...]
    sine = sin_ref[...]
    for slab in range(pairs):
        cols = slice(slab * LANES, (slab + 1) * LANES)
        q_ref[:, cols] = turn(proj_ref[:, cols], cosine, sine, 1.0).astype(BF16)
    at = pairs * LANES
    keys = turn(proj_ref[:, at : at + LANES], cosine, sine, 1.0)
    values = proj_ref[:, at + LANES : at + 2 * LANES]
    k_ref[...] = keys.astype(BF16)
    v_ref[...] = values.astype(BF16)
    low_half = iota((length, LANES), 1) < HDIM
    for head in range(KVHEADS):
        k2_ref[head] = twice(keys, head, low_half).astype(BF16)
        v2_ref[head] = twice(values, head, low_half).astype(BF16)
    scale = HDIM ** (-0.5)
    low_q = iota((QBLOCK, LANES), 1) < HDIM
    zero = jnp.zeros((QBLOCK, LANES), BF16)
    for block in range(length // QBLOCK):
        start, stop = block * QBLOCK, (block + 1) * QBLOCK
        first = max(0, start - LONGEST)
        window = stop - first
        key_pos = iota((window, QBLOCK), 0) + first
        query_pos = iota((window, QBLOCK), 1) + start
        allowed = (idc_ref[first:stop, :] == idr_ref[:, start:stop]) & (query_pos >= key_pos)
        bias = jnp.where(allowed, 0.0, -1e30)
        for pair in range(pairs):
            group = pair * 2 // (AHEADS // KVHEADS)
            cols = slice(pair * LANES, (pair + 1) * LANES)
            query = q_ref[start:stop, cols]
            k2 = k2_ref[group, first:stop, :]
            v2 = v2_ref[group, first:stop, :]
            outs = []
            for side in range(2):
                part = jnp.where(low_q, query, zero) if side == 0 else jnp.where(low_q, zero, query)
                scores = dot_nt(k2, part) * scale + bias
                top = jnp.max(scores, axis=0, keepdims=True)
                expd = jnp.exp(scores - top)
                total = jnp.sum(expd, axis=0, keepdims=True)
                probs = (expd * (1.0 / total)).astype(BF16)
                outs.append(dot_tn(probs, v2))
                lse_ref[2 * pair + side : 2 * pair + side + 1, start:stop] = top + jnp.log(total)
            out_ref[start:stop, cols] = jnp.where(low_q, outs[0], outs[1]).astype(BF16)


def attention_fwd(proj, cosine, sine, id_col, id_row):
    length = proj.shape[0]
    shape = jax.ShapeDtypeStruct
    return pl.pallas_call(
        attention_fwd_kernel,
        out_shape=(
            shape((length, AHEADS * HDIM), BF16),
            shape((length, LANES), BF16),
            shape((length, LANES), BF16),
            shape((length, AHEADS * HDIM), BF16),
            shape((AHEADS, length), F32),
        ),
        scratch_shapes=[
            pltpu.VMEM((KVHEADS, length, LANES), BF16),
            pltpu.VMEM((KVHEADS, length, LANES), BF16),
        ],
        compiler_params=pltpu.CompilerParams(vmem_limit_bytes=48 << 20),
        cost_estimate=pl.CostEstimate(flops=30 * 10**9, bytes_accessed=8 << 20, transcendentals=5 * 10**6),
        name="attention_fwd",
    )(proj, cosine, sine, id_col, id_row)


def attention_bwd_kernel(q_ref, k_ref, v_ref, lse_ref, go_ref, cos_ref, sin_ref, idc_ref, idr_ref, grad_ref, k2_ref, v2_ref, dk_ref, dv_ref, dq_ref):
    length = q_ref.shape[0]
    pairs = AHEADS // 2
    keys = k_ref[...].astype(F32)
    values = v_ref[...].astype(F32)
    low_half = iota((length, LANES), 1) < HDIM
    for head in range(KVHEADS):
        k2_ref[head] = twice(keys, head, low_half).astype(BF16)
        v2_ref[head] = twice(values, head, low_half).astype(BF16)
    dk_ref[...] = jnp.zeros_like(dk_ref)
    dv_ref[...] = jnp.zeros_like(dv_ref)
    scale = HDIM ** (-0.5)
    low_q = iota((QBLOCK, LANES), 1) < HDIM
    zero = jnp.zeros((QBLOCK, LANES), BF16)
    for block in range(length // QBLOCK):
        start, stop = block * QBLOCK, (block + 1) * QBLOCK
        first = max(0, start - LONGEST)
        window = stop - first
        key_pos = iota((window, QBLOCK), 0) + first
        query_pos = iota((window, QBLOCK), 1) + start
        allowed = (idc_ref[first:stop, :] == idr_ref[:, start:stop]) & (query_pos >= key_pos)
        bias = jnp.where(allowed, 0.0, -1e30)
        for pair in range(pairs):
            group = pair * 2 // (AHEADS // KVHEADS)
            cols = slice(pair * LANES, (pair + 1) * LANES)
            query = q_ref[start:stop, cols]
            grad_out = go_ref[start:stop, cols]
            k2 = k2_ref[group, first:stop, :]
            v2 = v2_ref[group, first:stop, :]
            outs = []
            dk = dv = None
            for side in range(2):
                part = jnp.where(low_q, query, zero) if side == 0 else jnp.where(low_q, zero, query)
                grad = jnp.where(low_q, grad_out, zero) if side == 0 else jnp.where(low_q, zero, grad_out)
                head = 2 * pair + side
                scores = dot_nt(k2, part) * scale + bias
                probs = jnp.exp(scores - lse_ref[head : head + 1, start:stop])
                grad_probs = dot_nt(v2, grad)
                product = probs * grad_probs
                inner = jnp.sum(product, axis=0, keepdims=True)
                grad_scores = (product - probs * inner).astype(BF16)
                outs.append(dot_tn(grad_scores, k2))
                more_k = dot_nn(grad_scores, part)
                more_v = dot_nn(probs.astype(BF16), grad)
                dk = more_k if dk is None else dk + more_k
                dv = more_v if dv is None else dv + more_v
            dk_ref[group, first:stop, :] += dk
            dv_ref[group, first:stop, :] += dv
            dq_ref[start:stop, cols] = jnp.where(low_q, outs[0], outs[1]) * scale
    cosine = cos_ref[...]
    sine = sin_ref[...]
    for slab in range(pairs):
        cols = slice(slab * LANES, (slab + 1) * LANES)
        grad_ref[:, cols] = turn(dq_ref[:, cols], cosine, sine, -1.0).astype(BF16)

    def joined(ref):
        both = [ref[head] + pltpu.roll(ref[head], HDIM, 1) for head in range(KVHEADS)]
        return jnp.where(low_half, both[0], both[1])

    at = pairs * LANES
    grad_ref[:, at : at + LANES] = turn(joined(dk_ref) * scale, cosine, sine, -1.0).astype(BF16)
    grad_ref[:, at + LANES : at + 2 * LANES] = joined(dv_ref).astype(BF16)


def attention_bwd(query, keys, values, lse, grad_out, cosine, sine, id_col, id_row):
    length = query.shape[0]
    return pl.pallas_call(
        attention_bwd_kernel,
        out_shape=jax.ShapeDtypeStruct((length, (AHEADS + 2 * KVHEADS) * HDIM), BF16),
        scratch_shapes=[
            pltpu.VMEM((KVHEADS, length, LANES), BF16),
            pltpu.VMEM((KVHEADS, length, LANES), BF16),
            pltpu.VMEM((KVHEADS, length, LANES), F32),
            pltpu.VMEM((KVHEADS, length, LANES), F32),
            pltpu.VMEM((length, AHEADS * HDIM), F32),
        ],
        compiler_params=pltpu.CompilerParams(vmem_limit_bytes=48 << 20),
        cost_estimate=pl.CostEstimate(flops=50 * 10**9, bytes_accessed=8 << 20, transcendentals=5 * 10**6),
        name="attention_bwd",
    )(query, keys, values, lse, grad_out, cosine, sine, id_col, id_row)


def token_marks(ids):
    length = ids.shape[0]
    shape = jnp.arange(length, dtype=jnp.int32)
    columns = []
    for offset in range(1, CONV):
        earlier = jnp.pad(ids, (offset, 0), constant_values=-1)[:length]
        columns.append(earlier == ids)
    for offset in range(1, CONV):
        later = jnp.pad(ids, (0, offset), constant_values=-1)[offset:]
        columns.append(later == ids)
    by_chunk = ids.reshape(-1, CHUNK)
    before = jnp.concatenate([jnp.full((1,), -1, jnp.int32), by_chunk[:-1, -1]])
    columns.append((by_chunk == before[:, None]).reshape(-1))
    columns.append((by_chunk == by_chunk[:, -1:]).reshape(-1))
    columns = [column.astype(F32) for column in columns] + [ids.astype(F32)]
    return jnp.pad(jnp.stack(columns, axis=1), ((0, 0), (0, LANES - len(columns))))


def head_state(step_ref, dtb_ref, rate_ref, marks):
    shape = (CHUNK, CHUNK)
    lower = (iota(shape, 0) >= iota(shape, 1)).astype(F32)
    shifted = step_ref[...] + dtb_ref[0:1, :]
    sizes = softplus(shifted)
    rate = -jnp.exp(rate_ref[0:1, :])
    log_decay = sizes * rate
    totals = dot_nn(lower, log_decay, HIGH)
    entering = jnp.exp(totals) * marks[:, 6:7]
    leaving = jnp.exp(totals[CHUNK - 1 : CHUNK, :] - totals) * marks[:, 7:8]
    return shifted, sizes, rate, log_decay, totals, entering, leaving


def spread(columns, expand):
    stacked = jnp.concatenate(columns, axis=0)
    high, low = split_low(stacked)
    return dot_nn(jnp.concatenate([high, low], axis=1), expand)


def shifted_rows(full, offset, ahead):
    rows = full.shape[0]
    if ahead:
        return pltpu.roll(full, rows - offset, 0)[0:CHUNK]
    return pltpu.roll(full, offset, 0)[8 : 8 + CHUNK]


def halves(values, low_lane):
    return jnp.concatenate(
        [jnp.where(low_lane, values, 0.0), jnp.where(low_lane, 0.0, values)], axis=0
    ).astype(BF16)


def mixer_fwd_kernel(inner, pg_ref, pc_ref, step_ref, marks_ref, row_ref, kern_ref, bias_ref, rate_ref, dtb_ref, skip_ref, gain_ref, expand_ref,
                     scan_ref, start_ref, norm_ref, tail_ref, conv_ref, state_ref, wide_ref, gated_ref):
    channels = pc_ref.shape[1]
    slabs = inner // LANES

    @pl.when(pl.program_id(0) == 0)
    def _():
        tail_ref[...] = jnp.zeros_like(tail_ref)
        state_ref[...] = jnp.zeros_like(state_ref)

    marks = marks_ref[...]
    same = [jnp.broadcast_to(marks[:, j : j + 1], (CHUNK, LANES)) for j in range(CONV - 1)]
    for slab in range(channels // LANES):
        cols = slice(slab * LANES, (slab + 1) * LANES)
        here = pc_ref[:, cols].astype(F32)
        full = jnp.concatenate([tail_ref[:, cols], here], axis=0)
        tail_ref[:, cols] = here[CHUNK - 8 :]
        total = bias_ref[0:1, cols] + kern_ref[CONV - 1 : CONV, cols] * here
        for j in range(1, CONV):
            total = total + kern_ref[CONV - 1 - j : CONV - j, cols] * (same[j - 1] * shifted_rows(full, j, False))
        conv_ref[:, cols] = total * sigmoid(total)

    _, sizes, _, _, totals, entering, leaving = head_state(step_ref, dtb_ref, rate_ref, marks)
    wide_ref[...] = spread([sizes, leaving, entering], expand_ref[...])
    b_low = conv_ref[:, inner : inner + LANES].astype(BF16)
    c_low = conv_ref[:, inner + LANES : inner + 2 * LANES].astype(BF16)
    b_turned = conv_ref[:, inner : inner + LANES].T.astype(BF16)
    shape = (CHUNK, CHUNK)
    together = (marks[:, 8:9] == row_ref[0]) & (iota(shape, 0) >= iota(shape, 1))
    mixing = jnp.where(together, dot_nt(c_low, b_low), 0.0)
    totals_row = totals.T
    low_lane = iota((CHUNK, LANES), 1) < HDIM
    squares = jnp.zeros((CHUNK, LANES), F32)
    for slab in range(slabs):
        cols = slice(slab * LANES, (slab + 1) * LANES)
        parts = []
        for head in (2 * slab, 2 * slab + 1):
            gap = totals[:, head : head + 1] - totals_row[head : head + 1, :]
            parts.append(jnp.exp(jnp.minimum(gap, 0.0)) * mixing)
        both = jnp.concatenate(parts, axis=1).astype(BF16)
        values = conv_ref[:, cols]
        stepped = values * wide_ref[0:CHUNK, cols]
        state = state_ref[:, cols]
        state_low = state.astype(BF16)
        start_ref[0, :, cols] = state_low
        carry = wide_ref[2 * CHUNK : 3 * CHUNK, cols]
        scanned = (
            dot_nn(both, halves(stepped, low_lane))
            + dot_nn(c_low, state_low) * carry
            + skip_ref[0:1, cols] * values
        )
        scan_ref[:, cols] = scanned
        fresh = dot_nn(b_turned, (stepped * wide_ref[CHUNK : 2 * CHUNK, cols]).astype(BF16))
        state_ref[:, cols] = state * carry[CHUNK - 1 :, :] + fresh
        gate = pg_ref[:, cols].astype(F32)
        gated = scanned * (gate * sigmoid(gate))
        gated_ref[:, cols] = gated
        squares = squares + gated * gated
    scale = lax.rsqrt(jnp.sum(squares, axis=1, keepdims=True) / inner + EPS)
    for slab in range(slabs):
        cols = slice(slab * LANES, (slab + 1) * LANES)
        norm_ref[:, cols] = (gated_ref[:, cols] * scale * gain_ref[0:1, cols]).astype(BF16)


def mixer_fwd(gate_part, conv_input, step_raw, marks, rows, kern, bias, rate, dtb, skip, gain, expand):
    length, inner = gate_part.shape
    channels = conv_input.shape[1]
    chunks = length // CHUNK
    shape = jax.ShapeDtypeStruct

    def tokens(width):
        return pl.BlockSpec((CHUNK, width), lambda i: (i, 0))

    def whole(array):
        return pl.BlockSpec(array.shape, lambda i: (0,) * array.ndim)

    return pl.pallas_call(
        partial(mixer_fwd_kernel, inner),
        grid=(chunks,),
        in_specs=[tokens(inner), tokens(channels), tokens(LANES), tokens(LANES), pl.BlockSpec((1, 1, CHUNK), lambda i: (i, 0, 0))]
        + [whole(item) for item in (kern, bias, rate, dtb, skip, gain, expand)],
        out_specs=(tokens(inner), pl.BlockSpec((1, LANES, inner), lambda i: (i, 0, 0)), tokens(inner)),
        out_shape=(shape((length, inner), F32), shape((chunks, LANES, inner), BF16), shape((length, inner), BF16)),
        scratch_shapes=[
            pltpu.VMEM((8, channels), F32),
            pltpu.VMEM((CHUNK, channels), F32),
            pltpu.VMEM((LANES, inner), F32),
            pltpu.VMEM((3 * CHUNK, inner), F32),
            pltpu.VMEM((CHUNK, inner), F32),
        ],
        compiler_params=pltpu.CompilerParams(vmem_limit_bytes=48 << 20),
        cost_estimate=pl.CostEstimate(flops=30 * 10**9, bytes_accessed=20 << 20, transcendentals=8 * 10**6),
        name="mixer_fwd",
    )(gate_part, conv_input, step_raw, marks, rows, kern, bias, rate, dtb, skip, gain, expand)


def mixer_bwd_kernel(inner, chunks, e_ref, pg_ref, pc_ref, before_ref, step_ref, marks_ref, row_ref, scan_ref, start_ref, kern_ref, bias_ref, rate_ref, dtb_ref, skip_ref, gain_ref, expand_ref, gather_ref,
                     dgate_ref, dconv_ref, dstep_ref, dkern_ref, dgain_ref, dskip_ref, dhead_ref,
                     conv_ref, slope_ref, ds_ref, wide_ref, sums_ref, next_ref):
    channels = pc_ref.shape[1]
    slabs = inner // LANES
    step = pl.program_id(0)

    @pl.when(step == 0)
    def _():
        next_ref[...] = jnp.zeros_like(next_ref)
        ds_ref[...] = jnp.zeros_like(ds_ref)
        dkern_ref[...] = jnp.zeros_like(dkern_ref)
        dgain_ref[...] = jnp.zeros_like(dgain_ref)
        dskip_ref[...] = jnp.zeros_like(dskip_ref)
        dhead_ref[...] = jnp.zeros_like(dhead_ref)

    marks = marks_ref[...]
    same = [jnp.broadcast_to(marks[:, j : j + 1], (CHUNK, LANES)) for j in range(CONV - 1)]
    ahead = [jnp.broadcast_to(marks[:, 3 + j : 4 + j], (CHUNK, LANES)) for j in range(CONV - 1)]

    def window(cols):
        here = pc_ref[:, cols].astype(F32)
        return here, jnp.concatenate([before_ref[8:16, cols].astype(F32), here], axis=0)

    for slab in range(channels // LANES):
        cols = slice(slab * LANES, (slab + 1) * LANES)
        here, full = window(cols)
        total = bias_ref[0:1, cols] + kern_ref[CONV - 1 : CONV, cols] * here
        for j in range(1, CONV):
            total = total + kern_ref[CONV - 1 - j : CONV - j, cols] * (same[j - 1] * shifted_rows(full, j, False))
        gate = sigmoid(total)
        conv_ref[:, cols] = total * gate
        slope_ref[:, cols] = gate * (1.0 + total * (1.0 - gate))

    shifted, sizes, rate, log_decay, totals, entering, leaving = head_state(step_ref, dtb_ref, rate_ref, marks)
    wide_ref[...] = spread([sizes, leaving, entering], expand_ref[...])
    b_low = conv_ref[:, inner : inner + LANES].astype(BF16)
    c_low = conv_ref[:, inner + LANES : inner + 2 * LANES].astype(BF16)
    c_turned = conv_ref[:, inner + LANES : inner + 2 * LANES].T.astype(BF16)
    shape = (CHUNK, CHUNK)
    together = (marks[:, 8:9] == row_ref[0]) & (iota(shape, 0) <= iota(shape, 1))
    mixing = jnp.where(together, dot_nt(b_low, c_low), 0.0)
    totals_row = totals.T
    low_lane = iota((CHUNK, LANES), 1) < HDIM

    squares = jnp.zeros((CHUNK, LANES), F32)
    crossed = jnp.zeros((CHUNK, LANES), F32)
    for slab in range(slabs):
        cols = slice(slab * LANES, (slab + 1) * LANES)
        gate = pg_ref[:, cols].astype(F32)
        gated = scan_ref[:, cols] * (gate * sigmoid(gate))
        squares = squares + gated * gated
        crossed = crossed + gated * (gain_ref[0:1, cols] * e_ref[:, cols].astype(F32))
    scale = lax.rsqrt(jnp.sum(squares, axis=1, keepdims=True) / inner + EPS)
    pull = scale * scale * scale * (jnp.sum(crossed, axis=1, keepdims=True) / inner)

    def conv_back(cols, grad):
        pre = grad * slope_ref[:, cols]
        here, full = window(cols)
        behind = jnp.concatenate([pre, next_ref[:, cols]], axis=0)
        next_ref[:, cols] = pre[0:8]
        back = kern_ref[CONV - 1 : CONV, cols] * pre
        dkern_ref[CONV - 1 : CONV, cols] += jnp.sum(pre * here, axis=0, keepdims=True)
        for j in range(1, CONV):
            back = back + kern_ref[CONV - 1 - j : CONV - j, cols] * (ahead[j - 1] * shifted_rows(behind, j, True))
            dkern_ref[CONV - 1 - j : CONV - j, cols] += jnp.sum(
                pre * (same[j - 1] * shifted_rows(full, j, False)), axis=0, keepdims=True
            )
        dkern_ref[CONV : CONV + 1, cols] += jnp.sum(pre, axis=0, keepdims=True)
        dconv_ref[:, cols] = back.astype(BF16)

    d_mixing = jnp.zeros(shape, F32)
    d_b = jnp.zeros(shape, F32)
    d_c = jnp.zeros(shape, F32)
    last_row = iota((CHUNK, LANES), 0) == CHUNK - 1
    for slab in range(slabs):
        cols = slice(slab * LANES, (slab + 1) * LANES)
        gate = pg_ref[:, cols].astype(F32)
        opened = sigmoid(gate)
        silu = gate * opened
        scanned = scan_ref[:, cols]
        error = e_ref[:, cols].astype(F32)
        gated = scanned * silu
        dgain_ref[0:1, cols] += jnp.sum(error * gated * scale, axis=0, keepdims=True)
        d_gated = scale * (gain_ref[0:1, cols] * error) - gated * pull
        dgate_ref[:, cols] = (d_gated * scanned * (opened + silu * (1.0 - opened))).astype(BF16)
        grad = d_gated * silu
        grad_low = grad.astype(BF16)
        values = conv_ref[:, cols]
        size = wide_ref[0:CHUNK, cols]
        leave = wide_ref[CHUNK : 2 * CHUNK, cols]
        enter = wide_ref[2 * CHUNK : 3 * CHUNK, cols]
        stepped = values * size
        stepped_low = stepped.astype(BF16)
        grad_halves = halves(grad, low_lane)
        decays = []
        for head in (2 * slab, 2 * slab + 1):
            gap = totals_row[head : head + 1, :] - totals[:, head : head + 1]
            decays.append(jnp.exp(jnp.minimum(gap, 0.0)))
        both = jnp.concatenate([decay * mixing for decay in decays], axis=1).astype(BF16)
        ds_next = ds_ref[:, cols]
        ds_low = ds_next.astype(BF16)
        left = dot_nn(b_low, ds_low) * leave
        d_stepped = dot_nn(both, grad_halves) + left
        d_both = dot_nt(stepped_low, grad_halves)
        d_mixing = d_mixing + decays[0] * d_both[:, :CHUNK] + decays[1] * d_both[:, CHUNK:]
        entered = (grad * enter).astype(BF16)
        start = start_ref[0, :, cols]
        d_c = d_c + dot_nt(entered, start)
        d_b = d_b + dot_nt((stepped * leave).astype(BF16), ds_low)
        kept = enter[CHUNK - 1 :, :]
        ds_ref[:, cols] = ds_next * kept + dot_nn(c_turned, entered)
        skip = skip_ref[0:1, cols]
        grad_round = grad_low.astype(F32)
        step_round = stepped_low.astype(F32)
        tail = jnp.sum(step_round * left, axis=0, keepdims=True) + kept * jnp.sum(
            ds_next * start.astype(F32), axis=0, keepdims=True
        )
        turns = grad_round * (scanned - skip * values) - step_round * d_stepped
        turns = turns + jnp.where(last_row, tail, 0.0)
        sized = values * d_stepped
        for at, piece in ((0, turns), (1, sized)):
            high, low = split_low(piece)
            sums_ref[at * CHUNK : (at + 1) * CHUNK, cols] = high
            sums_ref[(at + 2) * CHUNK : (at + 3) * CHUNK, cols] = low
        dskip_ref[0:1, cols] += jnp.sum(grad * values, axis=0, keepdims=True)
        conv_back(cols, size * d_stepped + skip * grad)

    heads = dot_nn(sums_ref[...], gather_ref[...])
    heads = heads[0 : 2 * CHUNK] + heads[2 * CHUNK :]
    upper = (iota(shape, 0) <= iota(shape, 1)).astype(F32)
    d_decay = dot_nn(upper, heads[0:CHUNK], HIGH)
    d_sizes = heads[CHUNK:] + d_decay * rate
    d_step = d_sizes * sigmoid(shifted)
    dstep_ref[...] = d_step.astype(BF16)
    dhead_ref[0:1, :] += jnp.sum(d_decay * log_decay, axis=0, keepdims=True)
    dhead_ref[1:2, :] += jnp.sum(d_step, axis=0, keepdims=True)
    d_mixing = jnp.where(together, d_mixing, 0.0)
    d_b = d_b + dot_nn(d_mixing.astype(BF16), c_low)
    d_c = d_c + dot_nn(d_mixing.T.astype(BF16), b_low)
    conv_back(slice(inner, inner + LANES), d_b)
    conv_back(slice(inner + LANES, inner + 2 * LANES), d_c)


def mixer_bwd(error, gate_part, conv_input, step_raw, marks, rows, scanned, starts, kern, bias, rate, dtb, skip, gain, expand, gather):
    length, inner = gate_part.shape
    channels = conv_input.shape[1]
    chunks = length // CHUNK
    shape = jax.ShapeDtypeStruct

    def tokens(width):
        return pl.BlockSpec((CHUNK, width), lambda i: (chunks - 1 - i, 0))

    def whole(array):
        return pl.BlockSpec(array.shape, lambda i: (0,) * len(array.shape))

    per = CHUNK // 16
    sums = (
        shape((8, channels), F32),
        shape((8, inner), F32),
        shape((8, inner), F32),
        shape((8, LANES), F32),
    )
    return pl.pallas_call(
        partial(mixer_bwd_kernel, inner, chunks),
        grid=(chunks,),
        in_specs=[
            tokens(inner),
            tokens(inner),
            tokens(channels),
            pl.BlockSpec((16, channels), lambda i: (jnp.maximum((chunks - 1 - i) * per - 1, 0), 0)),
            tokens(LANES),
            tokens(LANES),
            pl.BlockSpec((1, 1, CHUNK), lambda i: (chunks - 1 - i, 0, 0)),
            tokens(inner),
            pl.BlockSpec((1, LANES, inner), lambda i: (chunks - 1 - i, 0, 0)),
        ]
        + [whole(item) for item in (kern, bias, rate, dtb, skip, gain, expand, gather)],
        out_specs=(tokens(inner), tokens(channels), tokens(LANES)) + tuple(whole(item) for item in sums),
        out_shape=(
            shape((length, inner), BF16),
            shape((length, channels), BF16),
            shape((length, LANES), BF16),
        )
        + sums,
        scratch_shapes=[
            pltpu.VMEM((CHUNK, channels), F32),
            pltpu.VMEM((CHUNK, channels), F32),
            pltpu.VMEM((LANES, inner), F32),
            pltpu.VMEM((3 * CHUNK, inner), F32),
            pltpu.VMEM((4 * CHUNK, inner), BF16),
            pltpu.VMEM((8, channels), F32),
        ],
        compiler_params=pltpu.CompilerParams(vmem_limit_bytes=48 << 20),
        cost_estimate=pl.CostEstimate(flops=70 * 10**9, bytes_accessed=30 << 20, transcendentals=10**7),
        name="mixer_bwd",
    )(error, gate_part, conv_input, conv_input, step_raw, marks, rows, scanned, starts, kern, bias, rate, dtb, skip, gain, expand, gather)


def norm_scale(values):
    return lax.rsqrt(jnp.mean(values * values, axis=-1, keepdims=True) + EPS)


def norm_back(values, scale, gain, error):
    pulled = gain * error
    pull = jnp.mean(values * pulled, axis=-1, keepdims=True)
    grad = scale * pulled - values * (scale * scale * scale * pull)
    return grad, jnp.sum(error * (values * scale), axis=0)


def rotary_tables(length, width):
    half = width // 2
    freq = jnp.exp(-(jnp.arange(half, dtype=F32) * (2.0 / width)) * math.log(THETA))
    angle = jnp.arange(length, dtype=F32)[:, None] * freq[None, :]
    repeats = (1, LANES // half)
    return jnp.tile(jnp.cos(angle), repeats), jnp.tile(jnp.sin(angle), repeats)


def gathered(weight):
    parts = lax.axis_size("rep")
    rows = weight.shape[0] // parts
    mine = lax.dynamic_slice_in_dim(weight, lax.axis_index("rep") * rows, rows, 0)
    return lax.all_gather(mine, ("shard", "rep"), axis=0, tiled=True)


def summed(grad):
    mine = lax.psum_scatter(grad.astype(BF16), ("shard", "rep"), scatter_dimension=0, tiled=True)
    return lax.all_gather(mine, "rep", axis=0, tiled=True).astype(F32)


def shards(
    x_in,
    segment_ids,
    norm_in,
    mix_in,
    attn_in,
    attn_out,
    mix_out,
    norm_ff,
    ff_in,
    ff_out,
    conv_kernel,
    conv_bias,
    log_rate,
    dt_bias,
    skip,
    gate_norm,
    cotangent,
):
    _, length, model = x_in.shape
    inner = gate_norm.shape[0]
    channels = conv_bias.shape[0]
    heads = log_rate.shape[0]
    qkv = attn_in.shape[1]
    lane_pad = LANES - heads

    step_in = jnp.pad(mix_in[:, inner + channels :], ((0, 0), (0, lane_pad)))
    small_in = gathered(jnp.concatenate([attn_in, step_in], axis=1))
    full_norms = lax.all_gather(jnp.stack([norm_in, norm_ff]), "shard", axis=1, tiled=True).astype(F32)
    conv_in = gathered(mix_in[:, inner : inner + channels])
    gate_in = gathered(mix_in[:, :inner])
    full_attn_out = gathered(attn_out)
    full_mix_out = gathered(mix_out)
    full_ff_in = gathered(ff_in)
    full_ff_out = gathered(ff_out)

    ids = segment_ids.reshape(length)
    marks = token_marks(ids)
    id_col = ids.reshape(length, 1)
    id_row = ids.reshape(1, length)
    chunk_rows = ids.astype(F32).reshape(length // CHUNK, 1, CHUNK)
    cosine, sine = rotary_tables(length, HDIM)

    def row(values, pad=0):
        return jnp.pad(values.astype(F32).reshape(1, -1), ((0, 7), (0, pad)))

    kern = jnp.pad(conv_kernel.astype(F32), ((0, 4), (0, 0)))
    bias = row(conv_bias)
    rate = row(log_rate, lane_pad)
    dtb = row(dt_bias, lane_pad)
    skips = row(jnp.repeat(skip, inner // heads))
    gain = row(gate_norm)
    owner = jnp.arange(inner, dtype=jnp.int32) // (inner // heads)
    expand = (owner[None, :] == jnp.arange(LANES, dtype=jnp.int32)[:, None]).astype(BF16)
    gather = expand.T
    expand = jnp.concatenate([expand, expand], axis=0)

    resid = x_in.reshape(length, model).astype(F32)
    first_scale = norm_scale(resid)
    first_low = (resid * first_scale * full_norms[0]).astype(BF16)
    small = dot_nn(first_low, small_in)
    query, keys, values, attended, lse = attention_fwd(small[:, :qkv], cosine, sine, id_col, id_row)
    step_raw = small[:, qkv:]
    conv_input = dot_nn(first_low, conv_in).astype(BF16)
    gate_part = dot_nn(first_low, gate_in).astype(BF16)
    scanned, starts, mixed = mixer_fwd(
        gate_part, conv_input, step_raw, marks, chunk_rows, kern, bias, rate, dtb, skips, gain, expand
    )
    hidden = resid + dot_nt(attended, full_attn_out) + dot_nt(mixed, full_mix_out)
    second_scale = norm_scale(hidden)
    second_low = (hidden * second_scale * full_norms[1]).astype(BF16)
    ff_proj = dot_nn(second_low, full_ff_in)
    width = ff_proj.shape[1] // 2
    opened = sigmoid(ff_proj[:, :width])
    silu = ff_proj[:, :width] * opened
    up = ff_proj[:, width:]
    act_low = (silu * up).astype(BF16)
    output = (hidden + dot_nt(act_low, full_ff_out)).astype(BF16).reshape(x_in.shape)

    grad_out = cotangent.reshape(length, model)
    ff_out_grad = summed(dot_tn(grad_out, act_low))
    grad_act = dot_nn(grad_out, full_ff_out)
    grad_ff = jnp.concatenate(
        [grad_act * up * (opened + silu * (1.0 - opened)), grad_act * silu], axis=1
    ).astype(BF16)
    ff_in_grad = summed(dot_tn(second_low, grad_ff))
    grad_second = dot_nt(grad_ff, full_ff_in)
    grad_hidden, norm_ff_grad = norm_back(hidden, second_scale, full_norms[1], grad_second)
    grad_hidden = grad_hidden + grad_out.astype(F32)
    branch_low = grad_hidden.astype(BF16)
    attn_out_grad = summed(dot_tn(branch_low, attended))
    mix_out_grad = summed(dot_tn(branch_low, mixed))
    grad_attended = dot_nn(branch_low, full_attn_out).astype(BF16)
    grad_mixed = dot_nn(branch_low, full_mix_out).astype(BF16)
    d_gate, d_conv, d_step, d_kern, d_gain, d_skip, d_head = mixer_bwd(
        grad_mixed, gate_part, conv_input, step_raw, marks, chunk_rows, scanned, starts,
        kern, bias, rate, dtb, skips, gain, expand, gather,
    )
    gate_in_grad = dot_tn(first_low, d_gate)
    conv_in_grad = dot_tn(first_low, d_conv)
    grad_attn_proj = attention_bwd(query, keys, values, lse, grad_attended, cosine, sine, id_col, id_row)
    d_small = jnp.concatenate([grad_attn_proj, d_step], axis=1)
    small_in_grad = dot_tn(first_low, d_small)
    gate_sum = summed(gate_in_grad)
    conv_sum = summed(conv_in_grad)
    small_sum = summed(small_in_grad)
    grad_first = dot_nt(d_gate, gate_in) + dot_nt(d_conv, conv_in) + dot_nt(d_small, small_in)
    grad_resid, norm_in_grad = norm_back(resid, first_scale, full_norms[0], grad_first)
    input_grad = (grad_resid + grad_hidden).astype(BF16).reshape(x_in.shape)
    mix_in_grad = jnp.concatenate([gate_sum, conv_sum, small_sum[:, qkv : qkv + heads]], axis=1)
    attn_in_grad = small_sum[:, :qkv]

    pieces = (
        d_kern[:CONV].reshape(-1),
        d_kern[CONV],
        d_gain[0],
        jnp.sum(d_skip[0].reshape(heads, -1), axis=1),
        d_head[0, :heads],
        d_head[1, :heads],
        norm_in_grad,
        norm_ff_grad,
    )
    packed = lax.psum(jnp.concatenate(pieces), ("rep", "shard"))
    split = []
    at = 0
    for piece in pieces:
        split.append(packed[at : at + piece.shape[0]])
        at += piece.shape[0]
    rows = norm_in.shape[0]
    mine = lax.axis_index("shard") * rows
    return (
        output,
        input_grad,
        lax.dynamic_slice_in_dim(split[6], mine, rows, 0),
        mix_in_grad,
        attn_in_grad,
        attn_out_grad,
        mix_out_grad,
        lax.dynamic_slice_in_dim(split[7], mine, rows, 0),
        ff_in_grad,
        ff_out_grad,
        split[0].reshape(conv_kernel.shape),
        split[1],
        split[4],
        split[5],
        split[3],
        split[2],
    )


def solution(mesh):
    in_specs = (
        P(("rep", "shard"), None, None),
        P(("rep", "shard"), None),
        P("shard"),
        P("shard", None),
        P("shard", None),
        P("shard", None),
        P("shard", None),
        P("shard"),
        P("shard", None),
        P("shard", None),
        P(),
        P(),
        P(),
        P(),
        P(),
        P(),
        P(("rep", "shard"), None, None),
    )
    out_specs = (
        P(("rep", "shard"), None, None),
        P(("rep", "shard"), None, None),
        P("shard"),
        P("shard", None),
        P("shard", None),
        P("shard", None),
        P("shard", None),
        P("shard"),
        P("shard", None),
        P("shard", None),
        P(),
        P(),
        P(),
        P(),
        P(),
        P(),
    )
    return jax.shard_map(shards, mesh=mesh, in_specs=in_specs, out_specs=out_specs, check_vma=False)
```

time: 1970 us -> 1450 us (0.74); the launches traced: 1940 us -> 1450 us
  local copies, waits for them, and re-layouts: 664 us -> 58.8 us
  waiting for transfers between devices: 372 us -> 968 us
  matrix products: 517 us -> 175 us
  other arithmetic: 258 us -> 24.7 us
  Pallas kernels: 0 us -> 102 us
  loops' own time: 30.8 us -> 0 us
  blocking collectives: 83.1 us -> 106 us
    dynamic_update_slice x36 -> x0, local copies, waits for them, and re-layouts: 407 us -> none  [the longest x32 366 us: ssd_sequence(): lax.scan(jax.checkpoint(scan_block), initial, (cut(inputs), cut(step_size...]
    reduce_scatter x6 -> x7, waiting for transfers between devices: 255 us -> 620 us  [summed(): lax.psum_scatter(grad.astype(BF16), ('shard', 'rep'), scatter_dimension=0...]
    dot_general x144 -> x21, matrix products: 517 us -> 175 us  [the longest x7 63 us: dot_nn(): lax.dot_general(left, right, (((1,), (0,)), ((), ())), precision=precisio...]
    all_gather x6 -> x9, waiting for transfers between devices: 93.8 us -> 348 us  [the longest x7 319 us: gathered(): return lax.all_gather(mine, ('shard', 'rep'), axis=0, tiled=True)]
    pallas_call x0 -> x4, Pallas kernels: none -> 102 us  [the longest x1 49.4 us: mixer_bwd(): pl.pallas_call(partial(mixer_bwd_kernel, inner, chunks), grid=(chunks,),...]
    reduce_sum x24 -> x2, other arithmetic: 62.9 us -> 0.59 us  [the longest x1 0.48 us: norm_scale(): return lax.rsqrt(jnp.mean(values * values, axis=-1, keepdims=True) + EPS)]
    squeeze x72 -> x1, local copies, waits for them, and re-layouts: 52.8 us -> 0.01 us  [shards(): d_head[1, :heads]]
    reduce_sum x41 -> x0, local copies, waits for them, and re-layouts: 46.5 us -> none  [the longest x16 22.8 us: scan_block(): gaps = totals[:, :, None] - totals[:, None, :]]
  transfers between devices with their start and end apart: 13 -> 16, of which waited for: 5 -> 15; matrix products, arithmetic and copies ran while one was open for 62% -> 15% of each run, Pallas kernels for 0% -> 7%
where the time goes in v1:
time: 1450 us
  waiting for transfers between devices  968 us (67%)
  matrix products  175 us (12%)
  blocking collectives  106 us (7%)
  Pallas kernels  102 us (7%)
  local copies, waits for them, and re-layouts  58.8 us (4%)
  other arithmetic  24.7 us (2%)
  between operations  15.1 us (1%)
    reduce_scatter x7, waiting for transfers between devices, summed(): lax.psum_scatter(grad.astype(BF16), ('shard', 'rep'), scatter_dimension=0...  620 us
    all_gather x7, waiting for transfers between devices, gathered(): return lax.all_gather(mine, ('shard', 'rep'), axis=0, tiled=True)  319 us
    dot_general x7, matrix products, dot_nn(): lax.dot_general(left, right, (((1,), (0,)), ((), ())), precision=precisio...  63 us
    dot_general x7, matrix products, dot_nt(): lax.dot_general(left, right, (((1,), (1,)), ((), ())), preferred_element_...  60.2 us
    dot_general x7, matrix products, dot_tn(): lax.dot_general(left, right, (((0,), (0,)), ((), ())), preferred_element_...  51.5 us
    all_gather x5, blocking collectives, summed(): return lax.all_gather(mine, 'rep', axis=0, tiled=True).astype(F32)  51.1 us
    pallas_call x1, Pallas kernels, mixer_bwd(): pl.pallas_call(partial(mixer_bwd_kernel, inner, chunks), grid=(chunks,),...  49.4 us
    psum x1, blocking collectives, shards(): packed = lax.psum(jnp.concatenate(pieces), ('rep', 'shard'))  41.8 us
  transfers between devices with their start and end apart: 16, of which 15 were waited for; matrix products, arithmetic and copies ran while one was open for 15% of the time, Pallas kernels for 7%

profile of v1, /device:TPU:0, one launch (start us, length us, event | category | flops | bytes accessed | tf_op | source)
XLA Modules:
  0.0 1450.6 jit_solution(16983734399867795549)
XLA Ops:
  8.3 1.4 fusion.24
  13.0 1.9 copy.119
  14.9 1.6 constant_dynamic-slice_fusion.2
  16.6 1.4 constant_dynamic-slice_fusion.5
  18.8 1.6 constant_dynamic-slice_fusion
  20.7 2.9 copy.82
  24.2 12.9 all_gather.45
  43.0 27.1 %all-gather.10.cloned.1.call-done = bf16[1024,896]{1,0:T(8,128)(2,1)} async-done(((bf16[32,896]{1,0:T(8,128)(2,1)}), bf16[1024,896]{1,0:T(8,128)(2,1)}) %all-gather.10.cloned.1.call-update) | async-done | bytes 1835024 | tf_op jit(solution)/shard_map/all_gather | solution.py:591
  70.1 4.7 fusion.53
  74.8 1.9 slice.136.proj_ref
  76.7 12.2 attention_fwd.1
  92.7 38.2 %all-gather.14.cloned.1.call-done = bf16[1024,1536]{1,0:T(8,128)(2,1)} async-done(((bf16[32,1536]{1,0:T(8,128)(2,1)}), bf16[1024,1536]{1,0:T(8,128)(2,1)}) %all-gather.14.cloned.1.call-update) | async-done | bytes 3145744 | tf_op jit(solution)/shard_map/all_gather | solution.py:591
  130.9 7.9 convolution_convert_fusion.4.pg_ref
  138.7 54.8 %all-gather.16.cloned.1.call-done = bf16[1024,1792]{1,0:T(8,128)(2,1)} async-done(((bf16[32,1792]{1,0:T(8,128)(2,1)}), bf16[1024,1792]{1,0:T(8,128)(2,1)}) %all-gather.16.cloned.1.call-update) | async-done | bytes 3670032 | tf_op jit(solution)/shard_map/all_gather | solution.py:591
  193.5 8.7 convolution_convert_fusion.6.pc_ref.before_ref
  202.3 19.6 %mixer_fwd.1 = (f32[1024,1536]{1,0:T(8,128)}, bf16[8,128,1536]{2,1,0:T(8,128)(2,1)S(1)}, bf16[1024,1536]{1,0:T(8,128)(2,1)}) custom-call(bf16[1024,1536]{1,0:T(8,128)(2,1)} %convolution_convert_fusion.4.pg_ref, bf16[1024,1792]{1,0:T(8,128)(2,1)} %convolution_convert_fusion.6.pc_ref.before_ref, f32[1024,128]{1,0:T(8,128)S(1)} %copy-done.2, ...), custom_call_target="tpu_custom_call" | custom-call | flops 30000001024 | bytes 20971520 | tf_op jit(solution)/shard_map/mixer_fwd/pallas_call | solution.py:349
  221.9 1.6 copy-done.19
  223.5 30.5 %all-gather.18.cloned.1.call-done = bf16[1024,1536]{1,0:T(8,128)(2,1)} async-done(((bf16[32,1536]{1,0:T(8,128)(2,1)}), bf16[1024,1536]{1,0:T(8,128)(2,1)}) %all-gather.18.cloned.1.call-update) | async-done | bytes 3145744 | tf_op jit(solution)/shard_map/all_gather | solution.py:591
  254.1 8.3 fusion.58
  262.4 46.9 %all-gather.12.cloned.1.call-done = bf16[1024,512]{1,0:T(8,128)(2,1)} async-done(((bf16[32,512]{1,0:T(8,128)(2,1)}), bf16[1024,512]{1,0:T(8,128)(2,1)}) %all-gather.12.cloned.1.call-update) | async-done | bytes 1048592 | tf_op jit(solution)/shard_map/all_gather | solution.py:591
  309.3 6.6 multiply_reduce_fusion.2
  315.9 73.2 %all-gather.20.cloned.1.call-done = bf16[1024,4096]{1,0:T(8,128)(2,1)} async-done(((bf16[32,4096]{1,0:T(8,128)(2,1)}), bf16[1024,4096]{1,0:T(8,128)(2,1)}) %all-gather.20.cloned.1.call-update) | async-done | bytes 8388624 | tf_op jit(solution)/shard_map/all_gather | solution.py:591
  389.0 16.1 %fusion.46 = f32[1024,4096]{1,0:T(8,128)} fusion(bf16[1024,4096]{1,0:T(8,128)(2,1)} %all-gather.20.cloned.1.call-done, f32[1024,1024]{0,1:T(8,128)} %get-tuple-element.123, f32[1024]{0:T(1024)S(1)} %bitcast.106, f32[1024]{0:T(1024)S(1)} %add_rsqrt_fusion), kind=kOutput, calls=%fused_computation.118 | convolution fusion | flops 8593080320 | bytes 29368320 | tf_op jit(solution)/shard_map/dot_general | solution.py:27
  405.2 48.0 %all-gather.22.cloned.1.call-done = bf16[1024,2048]{1,0:T(8,128)(2,1)} async-done(((bf16[32,2048]{1,0:T(8,128)(2,1)}), bf16[1024,2048]{1,0:T(8,128)(2,1)}) %all-gather.22.cloned.1.call-update) | async-done | bytes 4194320 | tf_op jit(solution)/shard_map/all_gather | solution.py:591
  453.1 16.6 %fusion.1 = (bf16[1024,2048]{1,0:T(8,128)(2,1)}, bf16[1024,2048]{1,0:T(8,128)(2,1)}, bf16[1024,2048]{1,0:T(8,128)(2,1)S(1)}) fusion(f32[1024,4096]{1,0:T(8,128)} %fusion.46, bf16[1024,2048]{1,0:T(8,128)(2,1)} %all-gather.22.cloned.1.call-done, bf16[1,1024,1024]{2,1,0:T(8,128)(2,1)} %param.33), kind=kOutput, calls=%fused_computation.4 | convolution fusion | flops 4324327424 | bytes 35651584 | tf_op jit(solution)/shard_map/dot_general | solution.py:27
  469.8 2.1 copy-done.65
  471.9 6.2 convert_bitcast_fusion
  478.1 6.5 copy.113
  484.6 15.4 %convolution_convert_fusion = bf16[1024,4096]{1,0:T(8,128)(2,1)} fusion(bf16[1024,2048]{1,0:T(8,128)(2,1)} %get-tuple-element.99, bf16[1024,2048]{1,0:T(8,128)(2,1)} %get-tuple-element.98, f32[1024,1024]{0,1:T(8,128)} %get-tuple-element.123, f32[1024]{0:T(1024)S(1)} %bitcast.107, f32[1024]{0:T(1024)S(1)} %add_rsqrt_fusion), kind=kOutput, calls=%fused_computation.14 | convolution fusion | flops 8614051840 | bytes 20979712 | tf_op jit(solution)/shard_map/dot_general | solution.py:37
  500.1 4.4 copy.93
  505.5 15.7 %multiply_reduce_fusion = (f32[1024]{0:T(1024)}, f32[1024]{0:T(1024)S(1)}, f32[1024,1024]{0,1:T(8,128)S(1)}) fusion(f32[1024,1024]{0,1:T(8,128)} %get-tuple-element.123, f32[1024]{0:T(1024)S(1)} %add_rsqrt_fusion, f32[1024]{0:T(1024)S(1)} %bitcast.108, bf16[1024,4096]{1,0:T(8,128)(2,1)} %all-gather.20.cloned.1.call-done, ...), kind=kOutput, calls=%fused_computation.27 | convolution fusion | flops 8613001216 | bytes 25182208 | tf_op jit(solution)/shard_map/dot_general | solution.py:33
  524.5 2.2 convolution_convert_fusion.8
  526.8 7.7 convolution_convert_fusion.3.e_ref
  534.6 49.4 %mixer_bwd.1 = (bf16[1024,1536]{1,0:T(8,128)(2,1)S(1)}, bf16[1024,1792]{1,0:T(8,128)(2,1)}, bf16[1024,128]{1,0:T(8,128)(2,1)S(1)}, f32[8,1792]{1,0:T(8,128)S(1)}...) custom-call(bf16[1024,1536]{1,0:T(8,128)(2,1)} %convolution_convert_fusion.3.e_ref, ...), custom_call_target="tpu_custom_call" | custom-call | flops 70000001024 | bytes 31457280 | tf_op jit(solution)/shard_map/mixer_bwd/pallas_call | solution.py:532
  586.6 20.6 %attention_bwd.1 = bf16[1024,768]{1,0:T(8,128)(2,1)S(1)} custom-call(bf16[1024,512]{1,0:T(8,128)(2,1)S(1)} %copy-done.21, bf16[1024,128]{1,0:T(8,128)(2,1)S(1)} %copy-done.23, bf16[1024,128]{1,0:T(8,128)(2,1)S(1)} %copy-done.25, f32[8,1024]{1,0:T(8,128)S(1)} %copy-done.27, bf16[1024,512]{1,0:T(8,128)(2,1)S(1)} %convolution_convert_fusion.9.go_ref, ...), custom_call_target="tpu_custom_call" | custom-call | flops 49999998976 | bytes 8388608 | tf_op jit(solution)/shard_map/attention_bwd/pallas_call | solution.py:207
  607.3 3.7 convolution_convert_fusion.7
  611.0 7.6 convolution_convert_fusion.2
  619.1 7.7 convolution_convert_fusion.1
  626.9 8.8 convolution_convert_fusion.5
  637.7 9.2 fusion.60
  647.0 6.5 fusion.59
  653.5 4.9 fusion.8
  658.5 41.8 %psum.7 = f32[12616]{0:T(1024)S(1)} all-reduce(f32[12616]{0:T(1024)S(1)} %concatenate.30), channel_id=1, replica_groups=mesh['rep'=8,'shard'=4] {'rep','shard'}, use_global_device_ids=true, to_apply=%region_7.8 | all-reduce | flops 12616 | bytes 100928 | tf_op jit(solution)/shard_map/psum | solution.py:721
  700.4 70.8 %reduce-scatter.20.cloned.1.call-done = bf16[32,4096]{1,0:T(8,128)(2,1)} async-done(((bf16[1024,4096]{1,0:T(8,128)(2,1)}), bf16[32,4096]{1,0:T(8,128)(2,1)}) %reduce-scatter.20.cloned.1.call-update) | async-done | bytes 262160 | tf_op jit(solution)/shard_map/reduce_scatter | solution.py:595
  774.4 7.1 fusion.16
  781.5 2.6 copy.105
  784.0 9.2 fusion.15
  793.2 2.6 copy.104
  796.4 107.7 %reduce-scatter.16.cloned.1.call-done = bf16[32,512]{1,0:T(8,128)(2,1)} async-done(((bf16[1024,512]{1,0:T(8,128)(2,1)}), bf16[32,512]{1,0:T(8,128)(2,1)}) %reduce-scatter.16.cloned.1.call-update) | async-done | bytes 32784 | tf_op jit(solution)/shard_map/reduce_scatter | solution.py:595
  904.1 8.5 all_gather.56
  913.5 125.5 %reduce-scatter.14.cloned.1.call-done = bf16[32,896]{1,0:T(8,128)(2,1)} async-done(((bf16[1024,896]{1,0:T(8,128)(2,1)}), bf16[32,896]{1,0:T(8,128)(2,1)}) %reduce-scatter.14.cloned.1.call-update) | async-done | bytes 57360 | tf_op jit(solution)/shard_map/reduce_scatter | solution.py:595
  1039.0 9.0 all_gather.55
  1048.9 92.8 %reduce-scatter.10.cloned.1.call-done = bf16[32,1536]{1,0:T(8,128)(2,1)} async-done(((bf16[1024,1536]{1,0:T(8,128)(2,1)}), bf16[32,1536]{1,0:T(8,128)(2,1)}) %reduce-scatter.10.cloned.1.call-update) | async-done | bytes 98320 | tf_op jit(solution)/shard_map/reduce_scatter | solution.py:595
  1141.7 10.5 all_gather.53
  1152.4 95.2 %reduce-scatter.18.cloned.1.call-done = bf16[32,1536]{1,0:T(8,128)(2,1)} async-done(((bf16[1024,1536]{1,0:T(8,128)(2,1)}), bf16[32,1536]{1,0:T(8,128)(2,1)}) %reduce-scatter.18.cloned.1.call-update) | async-done | bytes 98320 | tf_op jit(solution)/shard_map/reduce_scatter | solution.py:595
  1247.6 11.7 all_gather.57
  1260.6 128.1 %reduce-scatter.12.cloned.1.call-done = bf16[32,1792]{1,0:T(8,128)(2,1)} async-done(((bf16[1024,1792]{1,0:T(8,128)(2,1)}), bf16[32,1792]{1,0:T(8,128)(2,1)}) %reduce-scatter.12.cloned.1.call-update) | async-done | bytes 114704 | tf_op jit(solution)/shard_map/reduce_scatter | solution.py:595
  1388.7 11.4 all_gather.54
  1400.2 2.0 pad_maximum_fusion.3
  1402.3 5.3 copy.106
  1407.6 2.4 all-gather.26.cloned.1.call-done
  1410.0 2.8 convert_element_type.192
  1412.8 27.0 %all-gather.24.cloned.1.call-done = bf16[256,4096]{1,0:T(8,128)(2,1)} async-done(((bf16[32,4096]{1,0:T(8,128)(2,1)}), bf16[256,4096]{1,0:T(8,128)(2,1)}) %all-gather.24.cloned.1.call-update) | async-done | bytes 2097168 | tf_op jit(solution)/shard_map/all_gather | solution.py:596
  1439.8 4.1 convert_element_type.189
  (240 shorter events, 32.5 us)
Async XLA Ops:
  7.2 10.8 copy-start
  7.2 62.9 %all-gather.10.cloned.1.call-start = ((), (), s32[]{:S(2)}) async-start(), calls=%async_computation.7 | async-start | bytes 1892352 | tf_op jit(solution)/shard_map/all_gather | solution.py:591
  8.2 12.3 copy-start.7
  9.7 121.2 %all-gather.14.cloned.1.call-start = ((), (), s32[]{:S(2)}) async-start(), calls=%async_computation.9 | async-start | bytes 3244032 | tf_op jit(solution)/shard_map/all_gather | solution.py:591
  12.0 181.6 %all-gather.16.cloned.1.call-start = ((), (), s32[]{:S(2)}) async-start(), calls=%async_computation.10 | async-start | bytes 3784704 | tf_op jit(solution)/shard_map/all_gather | solution.py:591
  13.0 11.1 copy-start.62
  13.0 11.2 copy-start.63
  14.9 239.2 %all-gather.18.cloned.1.call-start = ((), (), s32[]{:S(2)}) async-start(), calls=%async_computation.11 | async-start | bytes 3244032 | tf_op jit(solution)/shard_map/all_gather | solution.py:591
  16.5 292.8 %all-gather.12.cloned.1.call-start = ((), (), s32[]{:S(2)}) async-start(), calls=%async_computation.8 | async-start | bytes 1081344 | tf_op jit(solution)/shard_map/all_gather | solution.py:591
  18.0 371.1 %all-gather.20.cloned.1.call-start = ((), (), s32[]{:S(2)}) async-start(), calls=%async_computation.12 | async-start | bytes 8650752 | tf_op jit(solution)/shard_map/all_gather | solution.py:591
  18.8 434.4 %all-gather.22.cloned.1.call-start = ((), (), s32[]{:S(2)}) async-start(), calls=%async_computation.13 | async-start | bytes 4325376 | tf_op jit(solution)/shard_map/all_gather | solution.py:591
  20.4 18.3 %copy-start.56 = (bf16[1792]{0:T(1024)(128)(2,1)S(1)}, bf16[1792]{0:T(1024)(128)(2,1)}, u32[]{:S(2)}) copy-start(bf16[1792]{0:T(1024)(128)(2,1)} %param.28) | copy-start | bytes 10756
  20.4 18.3 %copy-start.58 = (f32[24]{0:T(128)S(1)}, f32[24]{0:T(128)}, u32[]{:S(2)}) copy-start(f32[24]{0:T(128)} %param.31) | copy-start | bytes 292
  20.4 626.4 %reduce-scatter.22.cloned.1.call-start = ((), (), s32[]{:S(2)}) async-start(), calls=%async_computation.22 | async-start | bytes 4325376 | tf_op jit(solution)/shard_map/reduce_scatter | solution.py:595
  20.7 19.1 %copy-start.38 = (s32[1536]{0:T(1024)}, s32[1536]{0:T(1024)S(1)}, u32[]{:S(2)}) copy-start(s32[1536]{0:T(1024)S(1)} %add_select_fusion) | copy-start | bytes 18436
  20.7 19.7 %copy-start.55 = (bf16[1536]{0:T(1024)(128)(2,1)S(1)}, bf16[1536]{0:T(1024)(128)(2,1)}, u32[]{:S(2)}) copy-start(bf16[1536]{0:T(1024)(128)(2,1)} %param.32) | copy-start | bytes 9220
  20.7 20.3 %copy-start.59 = (f32[24]{0:T(128)S(1)}, f32[24]{0:T(128)}, u32[]{:S(2)}) copy-start(f32[24]{0:T(128)} %param.29) | copy-start | bytes 292
  20.7 20.3 %copy-start.60 = (f32[24]{0:T(128)S(1)}, f32[24]{0:T(128)}, u32[]{:S(2)}) copy-start(f32[24]{0:T(128)} %param.30) | copy-start | bytes 292
  23.6 14.9 %copy-start.29 = (bf16[1,1024,1024]{1,2,0:T(8,128)(2,1)}, bf16[1,1024,1024]{1,2,0:T(8,128)(2,1)S(1)}, u32[]{:S(2)}) copy-start(bf16[1,1024,1024]{1,2,0:T(8,128)(2,1)S(1)} %copy.82) | copy-start | bytes 6291460
  24.1 14.6 %copy-start.46 = (f32[1024]{0:T(1024)}, f32[1024]{0:T(1024)S(1)}, u32[]{:S(2)}) copy-start(f32[1024]{0:T(1024)S(1)} %fusion.9) | copy-start | bytes 12292
  24.1 169.4 %copy-start.50 = (f32[1024]{0:T(1024)}, f32[1024]{0:T(1024)S(1)}, u32[]{:S(2)}) copy-start(f32[1024]{0:T(1024)S(1)} %add_rsqrt_fusion.1) | copy-start | bytes 12292
  37.7 483.5 %copy-start.44 = (f32[1,1024]{1,0:T(1,128)}, f32[1,1024]{1,0:T(1,128)S(1)}, u32[]{:S(2)}) copy-start(f32[1,1024]{1,0:T(1,128)S(1)} %get-tuple-element.108) | copy-start | bytes 12292
  38.6 31.5 %copy-start.52 = (f32[1,1024]{1,0:T(1,128)S(1)}, f32[1,1024]{1,0:T(1,128)}, u32[]{:S(2)}) copy-start(f32[1,1024]{1,0:T(1,128)} %get-tuple-element.109) | copy-start | bytes 12292
  76.7 54.2 %copy-start.53 = (f32[1,1024]{1,0:T(1,128)S(1)}, f32[1,1024]{1,0:T(1,128)}, u32[]{:S(2)}) copy-start(f32[1,1024]{1,0:T(1,128)} %get-tuple-element.109) | copy-start | bytes 12292
  193.5 8.8 copy-start.2
  193.5 8.8 copy-start.4
  193.5 8.8 copy-start.8
  193.5 8.8 copy-start.10
  315.9 89.3 %copy-start.48 = (f32[1024]{0:T(1024)}, f32[1024]{0:T(1024)S(1)}, u32[]{:S(2)}) copy-start(f32[1024]{0:T(1024)S(1)} %get-tuple-element.122) | copy-start | bytes 12292
  315.9 205.4 %copy-start.42 = (f32[1024]{0:T(1024)}, f32[1024]{0:T(1024)S(1)}, u32[]{:S(2)}) copy-start(f32[1024]{0:T(1024)S(1)} %add_rsqrt_fusion) | copy-start | bytes 12292
  453.1 18.7 %copy-start.36 = (bf16[1,1024,1024]{2,1,0:T(8,128)(2,1)S(1)}, bf16[1,1024,1024]{2,1,0:T(8,128)(2,1)}, u32[]{:S(2)}) copy-start(bf16[1,1024,1024]{2,1,0:T(8,128)(2,1)} %param.33) | copy-start | bytes 6291460
  484.6 286.6 %reduce-scatter.20.cloned.1.call-start = ((), (), s32[]{:S(2)}) async-start(), calls=%async_computation.19 | async-start | bytes 8650752 | tf_op jit(solution)/shard_map/reduce_scatter | solution.py:595
  500.1 404.0 %reduce-scatter.16.cloned.1.call-start = ((), (), s32[]{:S(2)}) async-start(), calls=%async_computation.17 | async-start | bytes 1081344 | tf_op jit(solution)/shard_map/reduce_scatter | solution.py:595
  505.5 15.7 %copy-start.49 = (f32[1024]{0:T(1024)S(1)}, f32[1024]{0:T(1024)}, u32[]{:S(2)}) copy-start(f32[1024]{0:T(1024)} %copy-done.48) | copy-start | bytes 12292
  505.5 15.7 %copy-start.28 = (f32[1024,1024]{0,1:T(8,128)S(1)}, f32[1024,1024]{0,1:T(8,128)}, u32[]{:S(2)}) copy-start(f32[1024,1024]{0,1:T(8,128)} %get-tuple-element.123) | copy-start | bytes 12582916
  505.5 15.7 %copy-start.32 = (bf16[1,1024,1024]{1,2,0:T(8,128)(2,1)S(1)}, bf16[1,1024,1024]{1,2,0:T(8,128)(2,1)}, u32[]{:S(2)}) copy-start(bf16[1,1024,1024]{1,2,0:T(8,128)(2,1)} %copy.93) | copy-start | bytes 6291460
  526.7 7.8 copy-start.3
  526.8 7.8 copy-start.5
  526.8 512.2 %reduce-scatter.14.cloned.1.call-start = ((), (), s32[]{:S(2)}) async-start(), calls=%async_computation.16 | async-start | bytes 1892352 | tf_op jit(solution)/shard_map/reduce_scatter | solution.py:595
  526.8 7.8 copy-start.6
  526.8 7.8 copy-start.9
  526.8 7.8 copy-start.11
  534.6 49.4 %copy-start.35 = (bf16[1024,1024]{0,1:T(8,128)(2,1)S(1)}, bf16[1024,1024]{0,1:T(8,128)(2,1)}, u32[]{:S(2)}) copy-start(bf16[1024,1024]{0,1:T(8,128)(2,1)} %copy-done.34) | copy-start | bytes 6291460
  534.6 49.4 %copy-start.37 = (bf16[1024,512]{1,0:T(8,128)(2,1)S(1)}, bf16[1024,512]{1,0:T(8,128)(2,1)}, u32[]{:S(2)}) copy-start(bf16[1024,512]{1,0:T(8,128)(2,1)} %all-gather.12.cloned.1.call-done) | copy-start | bytes 3145732
  584.1 23.2 %copy-start.16 = (bf16[1024,128]{1,0:T(8,128)(2,1)}, bf16[1024,128]{1,0:T(8,128)(2,1)S(1)}, u32[]{:S(2)}) copy-start(bf16[1024,128]{1,0:T(8,128)(2,1)S(1)} %get-tuple-element.41) | copy-start | bytes 786436
  586.6 20.6 %copy-start.30 = (bf16[1,1024,1024]{1,2,0:T(8,128)(2,1)S(1)}, bf16[1,1024,1024]{1,2,0:T(8,128)(2,1)}, u32[]{:S(2)}) copy-start(bf16[1,1024,1024]{1,2,0:T(8,128)(2,1)} %copy-done.29) | copy-start | bytes 6291460
  586.6 20.7 %copy-start.51 = (f32[1024]{0:T(1024)S(1)}, f32[1024]{0:T(1024)}, u32[]{:S(2)}) copy-start(f32[1024]{0:T(1024)} %copy-done.50) | copy-start | bytes 12292
  586.6 20.7 %copy-start.54 = (f32[1,1024]{1,0:T(1,128)S(1)}, f32[1,1024]{1,0:T(1,128)}, u32[]{:S(2)}) copy-start(f32[1,1024]{1,0:T(1,128)} %get-tuple-element.109) | copy-start | bytes 12292
  611.0 530.7 %reduce-scatter.10.cloned.1.call-start = ((), (), s32[]{:S(2)}) async-start(), calls=%async_computation.14 | async-start | bytes 3244032 | tf_op jit(solution)/shard_map/reduce_scatter | solution.py:595
  618.7 628.9 %reduce-scatter.18.cloned.1.call-start = ((), (), s32[]{:S(2)}) async-start(), calls=%async_computation.18 | async-start | bytes 3244032 | tf_op jit(solution)/shard_map/reduce_scatter | solution.py:595
  626.8 761.9 %reduce-scatter.12.cloned.1.call-start = ((), (), s32[]{:S(2)}) async-start(), calls=%async_computation.15 | async-start | bytes 3784704 | tf_op jit(solution)/shard_map/reduce_scatter | solution.py:595
  626.9 8.8 copy-start.13
  635.7 774.3 %all-gather.26.cloned.1.call-start = ((), (), s32[]{:S(2)}) async-start(), calls=%async_computation.21 | async-start | bytes 1179648 | tf_op jit(solution)/shard_map/all_gather | solution.py:596
  646.9 6.6 copy-start.17
  646.9 792.9 %all-gather.24.cloned.1.call-start = ((), (), s32[]{:S(2)}) async-start(), calls=%async_computation.20 | async-start | bytes 2359296 | tf_op jit(solution)/shard_map/all_gather | solution.py:596
  646.9 6.5 copy-start.31
  646.9 6.5 copy-start.61
  647.0 6.5 copy-start.64
  653.5 4.9 copy-start.57
  653.5 117.8 %copy-start.47 = (f32[1024]{0:T(1024)S(1)}, f32[1024]{0:T(1024)}, u32[]{:S(2)}) copy-start(f32[1024]{0:T(1024)} %copy-done.46) | copy-start | bytes 12292
  653.5 120.9 %copy-start.41 = (f32[1024]{0:T(1024)S(1)}, f32[1024]{0:T(1024)}, u32[]{:S(2)}) copy-start(f32[1024]{0:T(1024)} %copy-done.40) | copy-start | bytes 12292
  653.5 120.9 %copy-start.43 = (f32[1024]{0:T(1024)S(1)}, f32[1024]{0:T(1024)}, u32[]{:S(2)}) copy-start(f32[1024]{0:T(1024)} %copy-done.42) | copy-start | bytes 12292
  653.5 120.9 %copy-start.45 = (f32[1,1024]{1,0:T(1,128)S(1)}, f32[1,1024]{1,0:T(1,128)}, u32[]{:S(2)}) copy-start(f32[1,1024]{1,0:T(1,128)} %copy-done.44) | copy-start | bytes 12292
  1402.3 41.7 %copy-start.1 = (bf16[256,4096]{1,0:T(8,128)(2,1)S(1)}, bf16[256,4096]{1,0:T(8,128)(2,1)}, u32[]{:S(2)}) copy-start(bf16[256,4096]{1,0:T(8,128)(2,1)} %param.25) | copy-start | bytes 6291460
  (19 other events, 36.3 us)
Sparse Core Ops, SparseCore 0:
  11.5 58.6 all-gather.9
  73.0 57.8 all-gather.13
  134.3 59.1 all-gather.15
  196.2 57.7 all-gather.17
  256.8 52.4 all-gather.11
  312.6 76.4 all-gather.19
  392.5 60.6 all-gather.21
  484.7 139.4 reduce-scatter.21
  626.5 144.6 reduce-scatter.19
  773.3 130.7 reduce-scatter.15
  906.4 132.4 reduce-scatter.13
  1044.2 97.3 reduce-scatter.9
  1147.1 100.4 reduce-scatter.17
  1249.7 138.9 reduce-scatter.11
  1390.6 19.3 all-gather.25
  1411.9 27.8 all-gather.23

commit v2 on v1

--- a/solution.py
+++ b/solution.py
@@ -95,7 +95,7 @@
         window = stop - first
         key_pos = iota((window, QBLOCK), 0) + first
         query_pos = iota((window, QBLOCK), 1) + start
-        allowed = (idc_ref[first:stop, :] == idr_ref[:, start:stop]) & (query_pos >= key_pos)
+        allowed = (idc_ref[first:stop, 8:9] == idr_ref[:, start:stop]) & (query_pos >= key_pos)
         bias = jnp.where(allowed, 0.0, -1e30)
         for pair in range(pairs):
             group = pair * 2 // (AHEADS // KVHEADS)
@@ -138,7 +138,9 @@
     )(proj, cosine, sine, id_col, id_row)
 
 
-def attention_bwd_kernel(q_ref, k_ref, v_ref, lse_ref, go_ref, cos_ref, sin_ref, idc_ref, idr_ref, grad_ref, k2_ref, v2_ref, dk_ref, dv_ref, dq_ref):
+def attention_bwd_kernel(n_deps, *refs):
+    q_ref, k_ref, v_ref, lse_ref, go_ref, cos_ref, sin_ref, idc_ref, idr_ref = refs[n_deps : n_deps + 9]
+    grad_ref, k2_ref, v2_ref, dk_ref, dv_ref, dq_ref = refs[n_deps + 9 :]
     length = q_ref.shape[0]
     pairs = AHEADS // 2
     keys = k_ref[...].astype(F32)
@@ -158,7 +160,7 @@
         window = stop - first
         key_pos = iota((window, QBLOCK), 0) + first
         query_pos = iota((window, QBLOCK), 1) + start
-        allowed = (idc_ref[first:stop, :] == idr_ref[:, start:stop]) & (query_pos >= key_pos)
+        allowed = (idc_ref[first:stop, 8:9] == idr_ref[:, start:stop]) & (query_pos >= key_pos)
         bias = jnp.where(allowed, 0.0, -1e30)
         for pair in range(pairs):
             group = pair * 2 // (AHEADS // KVHEADS)
@@ -202,10 +204,11 @@
     grad_ref[:, at + LANES : at + 2 * LANES] = joined(dv_ref).astype(BF16)
 
 
-def attention_bwd(query, keys, values, lse, grad_out, cosine, sine, id_col, id_row):
+def attention_bwd(deps, query, keys, values, lse, grad_out, cosine, sine, id_col, id_row):
     length = query.shape[0]
     return pl.pallas_call(
-        attention_bwd_kernel,
+        partial(attention_bwd_kernel, len(deps)),
+        in_specs=[pl.BlockSpec(memory_space=pl.ANY) for _ in deps] + [pl.BlockSpec(memory_space=pltpu.VMEM)] * 9,
         out_shape=jax.ShapeDtypeStruct((length, (AHEADS + 2 * KVHEADS) * HDIM), BF16),
         scratch_shapes=[
             pltpu.VMEM((KVHEADS, length, LANES), BF16),
@@ -217,7 +220,19 @@
         compiler_params=pltpu.CompilerParams(vmem_limit_bytes=48 << 20),
         cost_estimate=pl.CostEstimate(flops=50 * 10**9, bytes_accessed=8 << 20, transcendentals=5 * 10**6),
         name="attention_bwd",
-    )(query, keys, values, lse, grad_out, cosine, sine, id_col, id_row)
+    )(*deps, query, keys, values, lse, grad_out, cosine, sine, id_col, id_row)
+
+
+def gate_cols(slabs, slab):
+    half = slabs // 2
+    at = slab if slab < half else slab + half
+    return slice(at * LANES, (at + 1) * LANES)
+
+
+def conv_cols(slabs, slab):
+    half = slabs // 2
+    at = half + slab if slab < half else slabs + slab
+    return slice(at * LANES, (at + 1) * LANES)
 
 
 def token_marks(ids):
@@ -270,9 +285,9 @@
     ).astype(BF16)
 
 
-def mixer_fwd_kernel(inner, pg_ref, pc_ref, step_ref, marks_ref, row_ref, kern_ref, bias_ref, rate_ref, dtb_ref, skip_ref, gain_ref, expand_ref,
+def mixer_fwd_kernel(inner, proj_ref, step_ref, marks_ref, row_ref, kern_ref, bias_ref, rate_ref, dtb_ref, skip_ref, gain_ref, expand_ref,
                      scan_ref, start_ref, norm_ref, tail_ref, conv_ref, state_ref, wide_ref, gated_ref):
-    channels = pc_ref.shape[1]
+    channels = proj_ref.shape[1] - inner
     slabs = inner // LANES
 
     @pl.when(pl.program_id(0) == 0)
@@ -284,7 +299,7 @@
     same = [jnp.broadcast_to(marks[:, j : j + 1], (CHUNK, LANES)) for j in range(CONV - 1)]
     for slab in range(channels // LANES):
         cols = slice(slab * LANES, (slab + 1) * LANES)
-        here = pc_ref[:, cols].astype(F32)
+        here = proj_ref[:, conv_cols(slabs, slab)].astype(F32)
         full = jnp.concatenate([tail_ref[:, cols], here], axis=0)
         tail_ref[:, cols] = here[CHUNK - 8 :]
         total = bias_ref[0:1, cols] + kern_ref[CONV - 1 : CONV, cols] * here
@@ -324,7 +339,7 @@
         scan_ref[:, cols] = scanned
         fresh = dot_nn(b_turned, (stepped * wide_ref[CHUNK : 2 * CHUNK, cols]).astype(BF16))
         state_ref[:, cols] = state * carry[CHUNK - 1 :, :] + fresh
-        gate = pg_ref[:, cols].astype(F32)
+        gate = proj_ref[:, gate_cols(slabs, slab)].astype(F32)
         gated = scanned * (gate * sigmoid(gate))
         gated_ref[:, cols] = gated
         squares = squares + gated * gated
@@ -334,9 +349,10 @@
         norm_ref[:, cols] = (gated_ref[:, cols] * scale * gain_ref[0:1, cols]).astype(BF16)
 
 
-def mixer_fwd(gate_part, conv_input, step_raw, marks, rows, kern, bias, rate, dtb, skip, gain, expand):
-    length, inner = gate_part.shape
-    channels = conv_input.shape[1]
+def mixer_fwd(projected, step_raw, marks, rows, kern, bias, rate, dtb, skip, gain, expand):
+    length, wide = projected.shape
+    inner = gain.shape[1]
+    channels = wide - inner
     chunks = length // CHUNK
     shape = jax.ShapeDtypeStruct
 
@@ -349,7 +365,7 @@
     return pl.pallas_call(
         partial(mixer_fwd_kernel, inner),
         grid=(chunks,),
-        in_specs=[tokens(inner), tokens(channels), tokens(LANES), tokens(LANES), pl.BlockSpec((1, 1, CHUNK), lambda i: (i, 0, 0))]
+        in_specs=[tokens(wide), tokens(LANES), tokens(LANES), pl.BlockSpec((1, 1, CHUNK), lambda i: (i, 0, 0))]
         + [whole(item) for item in (kern, bias, rate, dtb, skip, gain, expand)],
         out_specs=(tokens(inner), pl.BlockSpec((1, LANES, inner), lambda i: (i, 0, 0)), tokens(inner)),
         out_shape=(shape((length, inner), F32), shape((chunks, LANES, inner), BF16), shape((length, inner), BF16)),
@@ -363,17 +379,30 @@
         compiler_params=pltpu.CompilerParams(vmem_limit_bytes=48 << 20),
         cost_estimate=pl.CostEstimate(flops=30 * 10**9, bytes_accessed=20 << 20, transcendentals=8 * 10**6),
         name="mixer_fwd",
-    )(gate_part, conv_input, step_raw, marks, rows, kern, bias, rate, dtb, skip, gain, expand)
-
-
-def mixer_bwd_kernel(inner, chunks, e_ref, pg_ref, pc_ref, before_ref, step_ref, marks_ref, row_ref, scan_ref, start_ref, kern_ref, bias_ref, rate_ref, dtb_ref, skip_ref, gain_ref, expand_ref, gather_ref,
-                     dgate_ref, dconv_ref, dstep_ref, dkern_ref, dgain_ref, dskip_ref, dhead_ref,
-                     conv_ref, slope_ref, ds_ref, wide_ref, sums_ref, next_ref):
-    channels = pc_ref.shape[1]
+    )(projected, step_raw, marks, rows, kern, bias, rate, dtb, skip, gain, expand)
+
+
+def mixer_bwd_kernel(inner, second, n_deps, *refs):
+    refs = refs[n_deps:]
+    e_ref, proj_ref, before_ref, step_ref, marks_ref, row_ref, scan_ref, start_ref = refs[:8]
+    kern_ref, bias_ref, rate_ref, dtb_ref, skip_ref, gain_ref, expand_ref, gather_ref = refs[8:16]
+    refs = refs[16:]
+    if second:
+        part_ref, first_ref, refs = refs[0], refs[1], refs[2:]
+        dproj_ref = refs[0].at[:, inner:]
+        refs[0][:, :inner] = first_ref[...]
+        dkern_ref, dgain_ref, dskip_ref, dhead_ref = refs[1:5]
+        refs = refs[5:]
+    else:
+        dproj_ref, dkern_ref, dgain_ref, dskip_ref, dhead_ref, part_ref = refs[:6]
+        refs = refs[6:]
+    conv_ref, slope_ref, ds_ref, wide_ref, sums_ref, next_ref = refs
+    channels = proj_ref.shape[1] - inner
     slabs = inner // LANES
-    step = pl.program_id(0)
-
-    @pl.when(step == 0)
+    half = slabs // 2
+    base = half if second else 0
+
+    @pl.when(pl.program_id(0) == 0)
     def _():
         next_ref[...] = jnp.zeros_like(next_ref)
         ds_ref[...] = jnp.zeros_like(ds_ref)
@@ -386,78 +415,98 @@
     same = [jnp.broadcast_to(marks[:, j : j + 1], (CHUNK, LANES)) for j in range(CONV - 1)]
     ahead = [jnp.broadcast_to(marks[:, 3 + j : 4 + j], (CHUNK, LANES)) for j in range(CONV - 1)]
 
-    def window(cols):
-        here = pc_ref[:, cols].astype(F32)
+    def lanes(slab):
+        return slice(slab * LANES, (slab + 1) * LANES)
+
+    def window(slab):
+        cols = conv_cols(slabs, slab)
+        here = proj_ref[:, cols].astype(F32)
         return here, jnp.concatenate([before_ref[8:16, cols].astype(F32), here], axis=0)
 
-    for slab in range(channels // LANES):
-        cols = slice(slab * LANES, (slab + 1) * LANES)
-        here, full = window(cols)
+    def own(slab):
+        return lanes(slab - base if slab < slabs else slab - slabs + half)
+
+    for slab in [base + j for j in range(half)] + [slabs, slabs + 1]:
+        cols = lanes(slab)
+        here, full = window(slab)
         total = bias_ref[0:1, cols] + kern_ref[CONV - 1 : CONV, cols] * here
         for j in range(1, CONV):
             total = total + kern_ref[CONV - 1 - j : CONV - j, cols] * (same[j - 1] * shifted_rows(full, j, False))
         gate = sigmoid(total)
-        conv_ref[:, cols] = total * gate
-        slope_ref[:, cols] = gate * (1.0 + total * (1.0 - gate))
+        conv_ref[:, own(slab)] = total * gate
+        if second or slab < slabs:
+            slope_ref[:, own(slab)] = gate * (1.0 + total * (1.0 - gate))
 
     shifted, sizes, rate, log_decay, totals, entering, leaving = head_state(step_ref, dtb_ref, rate_ref, marks)
-    wide_ref[...] = spread([sizes, leaving, entering], expand_ref[...])
-    b_low = conv_ref[:, inner : inner + LANES].astype(BF16)
-    c_low = conv_ref[:, inner + LANES : inner + 2 * LANES].astype(BF16)
-    c_turned = conv_ref[:, inner + LANES : inner + 2 * LANES].T.astype(BF16)
+    wide_ref[...] = spread([sizes, leaving, entering], expand_ref[:, base * LANES : (base + half) * LANES])
+    b_values = conv_ref[:, own(slabs)]
+    c_values = conv_ref[:, own(slabs + 1)]
+    b_low = b_values.astype(BF16)
+    c_low = c_values.astype(BF16)
+    c_turned = c_values.T.astype(BF16)
     shape = (CHUNK, CHUNK)
     together = (marks[:, 8:9] == row_ref[0]) & (iota(shape, 0) <= iota(shape, 1))
     mixing = jnp.where(together, dot_nt(b_low, c_low), 0.0)
     totals_row = totals.T
     low_lane = iota((CHUNK, LANES), 1) < HDIM
 
-    squares = jnp.zeros((CHUNK, LANES), F32)
-    crossed = jnp.zeros((CHUNK, LANES), F32)
-    for slab in range(slabs):
-        cols = slice(slab * LANES, (slab + 1) * LANES)
-        gate = pg_ref[:, cols].astype(F32)
-        gated = scan_ref[:, cols] * (gate * sigmoid(gate))
-        squares = squares + gated * gated
-        crossed = crossed + gated * (gain_ref[0:1, cols] * e_ref[:, cols].astype(F32))
-    scale = lax.rsqrt(jnp.sum(squares, axis=1, keepdims=True) / inner + EPS)
-    pull = scale * scale * scale * (jnp.sum(crossed, axis=1, keepdims=True) / inner)
-
-    def conv_back(cols, grad):
-        pre = grad * slope_ref[:, cols]
-        here, full = window(cols)
-        behind = jnp.concatenate([pre, next_ref[:, cols]], axis=0)
-        next_ref[:, cols] = pre[0:8]
+    if second:
+        scale = part_ref[:, 3 * LANES : 3 * LANES + 1]
+        pull = part_ref[:, 3 * LANES + 1 : 3 * LANES + 2]
+        d_mixing = part_ref[:, 0:LANES]
+        d_b = part_ref[:, LANES : 2 * LANES]
+        d_c = part_ref[:, 2 * LANES : 3 * LANES]
+    else:
+        squares = jnp.zeros((CHUNK, LANES), F32)
+        crossed = jnp.zeros((CHUNK, LANES), F32)
+        for slab in range(slabs):
+            cols = lanes(slab)
+            gate = proj_ref[:, gate_cols(slabs, slab)].astype(F32)
+            gated = scan_ref[:, cols] * (gate * sigmoid(gate))
+            squares = squares + gated * gated
+            crossed = crossed + gated * (gain_ref[0:1, cols] * e_ref[:, cols].astype(F32))
+        scale = lax.rsqrt(jnp.sum(squares, axis=1, keepdims=True) / inner + EPS)
+        pull = scale * scale * scale * (jnp.sum(crossed, axis=1, keepdims=True) / inner)
+        d_mixing = jnp.zeros(shape, F32)
+        d_b = jnp.zeros(shape, F32)
+        d_c = jnp.zeros(shape, F32)
+
+    def conv_back(slab, grad):
+        cols = lanes(slab)
+        mine = own(slab)
+        pre = grad * slope_ref[:, mine]
+        here, full = window(slab)
+        behind = jnp.concatenate([pre, next_ref[:, mine]], axis=0)
+        next_ref[:, mine] = pre[0:8]
         back = kern_ref[CONV - 1 : CONV, cols] * pre
-        dkern_ref[CONV - 1 : CONV, cols] += jnp.sum(pre * here, axis=0, keepdims=True)
+        dkern_ref[CONV - 1 : CONV, mine] += jnp.sum(pre * here, axis=0, keepdims=True)
         for j in range(1, CONV):
             back = back + kern_ref[CONV - 1 - j : CONV - j, cols] * (ahead[j - 1] * shifted_rows(behind, j, True))
-            dkern_ref[CONV - 1 - j : CONV - j, cols] += jnp.sum(
+            dkern_ref[CONV - 1 - j : CONV - j, mine] += jnp.sum(
                 pre * (same[j - 1] * shifted_rows(full, j, False)), axis=0, keepdims=True
             )
-        dkern_ref[CONV : CONV + 1, cols] += jnp.sum(pre, axis=0, keepdims=True)
-        dconv_ref[:, cols] = back.astype(BF16)
-
-    d_mixing = jnp.zeros(shape, F32)
-    d_b = jnp.zeros(shape, F32)
-    d_c = jnp.zeros(shape, F32)
+        dkern_ref[CONV : CONV + 1, mine] += jnp.sum(pre, axis=0, keepdims=True)
+        dproj_ref[:, half * LANES + mine.start : half * LANES + mine.stop] = back.astype(BF16)
+
     last_row = iota((CHUNK, LANES), 0) == CHUNK - 1
-    for slab in range(slabs):
-        cols = slice(slab * LANES, (slab + 1) * LANES)
-        gate = pg_ref[:, cols].astype(F32)
+    for slab in range(base, base + half):
+        cols = lanes(slab)
+        mine = own(slab)
+        gate = proj_ref[:, gate_cols(slabs, slab)].astype(F32)
         opened = sigmoid(gate)
         silu = gate * opened
         scanned = scan_ref[:, cols]
         error = e_ref[:, cols].astype(F32)
         gated = scanned * silu
-        dgain_ref[0:1, cols] += jnp.sum(error * gated * scale, axis=0, keepdims=True)
+        dgain_ref[0:1, mine] += jnp.sum(error * gated * scale, axis=0, keepdims=True)
         d_gated = scale * (gain_ref[0:1, cols] * error) - gated * pull
-        dgate_ref[:, cols] = (d_gated * scanned * (opened + silu * (1.0 - opened))).astype(BF16)
+        dproj_ref[:, mine] = (d_gated * scanned * (opened + silu * (1.0 - opened))).astype(BF16)
         grad = d_gated * silu
         grad_low = grad.astype(BF16)
-        values = conv_ref[:, cols]
-        size = wide_ref[0:CHUNK, cols]
-        leave = wide_ref[CHUNK : 2 * CHUNK, cols]
-        enter = wide_ref[2 * CHUNK : 3 * CHUNK, cols]
+        values = conv_ref[:, mine]
+        size = wide_ref[0:CHUNK, mine]
+        leave = wide_ref[CHUNK : 2 * CHUNK, mine]
+        enter = wide_ref[2 * CHUNK : 3 * CHUNK, mine]
         stepped = values * size
         stepped_low = stepped.astype(BF16)
         grad_halves = halves(grad, low_lane)
@@ -466,7 +515,7 @@
             gap = totals_row[head : head + 1, :] - totals[:, head : head + 1]
             decays.append(jnp.exp(jnp.minimum(gap, 0.0)))
         both = jnp.concatenate([decay * mixing for decay in decays], axis=1).astype(BF16)
-        ds_next = ds_ref[:, cols]
+        ds_next = ds_ref[:, mine]
         ds_low = ds_next.astype(BF16)
         left = dot_nn(b_low, ds_low) * leave
         d_stepped = dot_nn(both, grad_halves) + left
@@ -477,42 +526,50 @@
         d_c = d_c + dot_nt(entered, start)
         d_b = d_b + dot_nt((stepped * leave).astype(BF16), ds_low)
         kept = enter[CHUNK - 1 :, :]
-        ds_ref[:, cols] = ds_next * kept + dot_nn(c_turned, entered)
+        ds_ref[:, mine] = ds_next * kept + dot_nn(c_turned, entered)
         skip = skip_ref[0:1, cols]
         grad_round = grad_low.astype(F32)
         step_round = stepped_low.astype(F32)
         tail = jnp.sum(step_round * left, axis=0, keepdims=True) + kept * jnp.sum(
             ds_next * start.astype(F32), axis=0, keepdims=True
         )
-        turns = grad_round * (scanned - skip * values) - step_round * d_stepped
-        turns = turns + jnp.where(last_row, tail, 0.0)
+        steered = grad_round * (scanned - skip * values) - step_round * d_stepped
+        steered = steered + jnp.where(last_row, tail, 0.0)
         sized = values * d_stepped
-        for at, piece in ((0, turns), (1, sized)):
+        for at, piece in ((0, steered), (1, sized)):
             high, low = split_low(piece)
-            sums_ref[at * CHUNK : (at + 1) * CHUNK, cols] = high
-            sums_ref[(at + 2) * CHUNK : (at + 3) * CHUNK, cols] = low
-        dskip_ref[0:1, cols] += jnp.sum(grad * values, axis=0, keepdims=True)
-        conv_back(cols, size * d_stepped + skip * grad)
-
-    heads = dot_nn(sums_ref[...], gather_ref[...])
+            sums_ref[at * CHUNK : (at + 1) * CHUNK, mine] = high
+            sums_ref[(at + 2) * CHUNK : (at + 3) * CHUNK, mine] = low
+        dskip_ref[0:1, mine] += jnp.sum(grad * values, axis=0, keepdims=True)
+        conv_back(slab, size * d_stepped + skip * grad)
+
+    heads = dot_nn(sums_ref[...], gather_ref[base * LANES : (base + half) * LANES, :])
     heads = heads[0 : 2 * CHUNK] + heads[2 * CHUNK :]
     upper = (iota(shape, 0) <= iota(shape, 1)).astype(F32)
     d_decay = dot_nn(upper, heads[0:CHUNK], HIGH)
     d_sizes = heads[CHUNK:] + d_decay * rate
     d_step = d_sizes * sigmoid(shifted)
-    dstep_ref[...] = d_step.astype(BF16)
     dhead_ref[0:1, :] += jnp.sum(d_decay * log_decay, axis=0, keepdims=True)
     dhead_ref[1:2, :] += jnp.sum(d_step, axis=0, keepdims=True)
-    d_mixing = jnp.where(together, d_mixing, 0.0)
-    d_b = d_b + dot_nn(d_mixing.astype(BF16), c_low)
-    d_c = d_c + dot_nn(d_mixing.T.astype(BF16), b_low)
-    conv_back(slice(inner, inner + LANES), d_b)
-    conv_back(slice(inner + LANES, inner + 2 * LANES), d_c)
-
-
-def mixer_bwd(error, gate_part, conv_input, step_raw, marks, rows, scanned, starts, kern, bias, rate, dtb, skip, gain, expand, gather):
-    length, inner = gate_part.shape
-    channels = conv_input.shape[1]
+    if second:
+        d_mixing = jnp.where(together, d_mixing, 0.0)
+        d_b = d_b + dot_nn(d_mixing.astype(BF16), c_low)
+        d_c = d_c + dot_nn(d_mixing.T.astype(BF16), b_low)
+        dproj_ref[:, inner + 2 * LANES :] = (d_step + part_ref[:, 4 * LANES :]).astype(BF16)
+        conv_back(slabs, d_b)
+        conv_back(slabs + 1, d_c)
+    else:
+        part_ref[:, 0:LANES] = d_mixing
+        part_ref[:, LANES : 2 * LANES] = d_b
+        part_ref[:, 2 * LANES : 3 * LANES] = d_c
+        part_ref[:, 4 * LANES :] = d_step
+        part_ref[:, 3 * LANES : 3 * LANES + 1] = scale
+        part_ref[:, 3 * LANES + 1 : 3 * LANES + 2] = pull
+
+
+def mixer_bwd(second, deps, error, projected, step_raw, marks, rows, scanned, starts, kern, bias, rate, dtb, skip, gain, expand, gather, part=None):
+    length, wide = projected.shape
+    inner = gain.shape[1]
     chunks = length // CHUNK
     shape = jax.ShapeDtypeStruct
 
@@ -523,46 +580,49 @@
         return pl.BlockSpec(array.shape, lambda i: (0,) * len(array.shape))
 
     per = CHUNK // 16
+    conv = inner // 2 + (2 * LANES if second else 0)
+    made = inner + (inner // 2 + conv + LANES if second else 0)
+    kept = inner // 2 + 2 * LANES
     sums = (
-        shape((8, channels), F32),
-        shape((8, inner), F32),
-        shape((8, inner), F32),
+        shape((8, conv), F32),
+        shape((8, inner // 2), F32),
+        shape((8, inner // 2), F32),
         shape((8, LANES), F32),
     )
+    part_shape = () if second else (shape((length, 5 * LANES), F32),)
     return pl.pallas_call(
-        partial(mixer_bwd_kernel, inner, chunks),
+        partial(mixer_bwd_kernel, inner, second, len(deps)),
         grid=(chunks,),
-        in_specs=[
+        in_specs=[pl.BlockSpec(memory_space=pl.ANY) for _ in deps]
+        + [
             tokens(inner),
-            tokens(inner),
-            tokens(channels),
-            pl.BlockSpec((16, channels), lambda i: (jnp.maximum((chunks - 1 - i) * per - 1, 0), 0)),
+            tokens(wide),
+            pl.BlockSpec((16, wide), lambda i: (jnp.maximum((chunks - 1 - i) * per - 1, 0), 0)),
             tokens(LANES),
             tokens(LANES),
             pl.BlockSpec((1, 1, CHUNK), lambda i: (chunks - 1 - i, 0, 0)),
             tokens(inner),
             pl.BlockSpec((1, LANES, inner), lambda i: (chunks - 1 - i, 0, 0)),
         ]
-        + [whole(item) for item in (kern, bias, rate, dtb, skip, gain, expand, gather)],
-        out_specs=(tokens(inner), tokens(channels), tokens(LANES)) + tuple(whole(item) for item in sums),
-        out_shape=(
-            shape((length, inner), BF16),
-            shape((length, channels), BF16),
-            shape((length, LANES), BF16),
-        )
-        + sums,
+        + [whole(item) for item in (kern, bias, rate, dtb, skip, gain, expand, gather)]
+        + ([tokens(5 * LANES), tokens(inner)] if second else []),
+        out_specs=(tokens(made),)
+        + tuple(whole(item) for item in sums)
+        + (() if second else (tokens(5 * LANES),)),
+        out_shape=(shape((length, made), BF16),) + sums + part_shape,
         scratch_shapes=[
-            pltpu.VMEM((CHUNK, channels), F32),
-            pltpu.VMEM((CHUNK, channels), F32),
-            pltpu.VMEM((LANES, inner), F32),
-            pltpu.VMEM((3 * CHUNK, inner), F32),
-            pltpu.VMEM((4 * CHUNK, inner), BF16),
-            pltpu.VMEM((8, channels), F32),
+            pltpu.VMEM((CHUNK, kept), F32),
+            pltpu.VMEM((CHUNK, kept), F32),
+            pltpu.VMEM((LANES, inner // 2), F32),
+            pltpu.VMEM((3 * CHUNK, inner // 2), F32),
+            pltpu.VMEM((4 * CHUNK, inner // 2), BF16),
+            pltpu.VMEM((8, kept), F32),
         ],
         compiler_params=pltpu.CompilerParams(vmem_limit_bytes=48 << 20),
-        cost_estimate=pl.CostEstimate(flops=70 * 10**9, bytes_accessed=30 << 20, transcendentals=10**7),
-        name="mixer_bwd",
-    )(error, gate_part, conv_input, conv_input, step_raw, marks, rows, scanned, starts, kern, bias, rate, dtb, skip, gain, expand, gather)
+        cost_estimate=pl.CostEstimate(flops=30 * 10**9, bytes_accessed=20 << 20, transcendentals=5 * 10**6),
+        name="mixer_bwd_second" if second else "mixer_bwd_first",
+    )(*deps, error, projected, projected, step_raw, marks, rows, scanned, starts, kern, bias, rate, dtb, skip, gain, expand, gather,
+      *(part or ()))
 
 
 def norm_scale(values):
@@ -578,10 +638,207 @@
 
 def rotary_tables(length, width):
     half = width // 2
-    freq = jnp.exp(-(jnp.arange(half, dtype=F32) * (2.0 / width)) * math.log(THETA))
-    angle = jnp.arange(length, dtype=F32)[:, None] * freq[None, :]
-    repeats = (1, LANES // half)
-    return jnp.tile(jnp.cos(angle), repeats), jnp.tile(jnp.sin(angle), repeats)
+    place = (iota((length, LANES), 1) % half).astype(F32)
+    freq = jnp.exp(-(place * (2.0 / width)) * math.log(THETA))
+    angle = iota((length, LANES), 0).astype(F32) * freq
+    return jnp.cos(angle), jnp.sin(angle)
+
+
+def places(axis, bit):
+    return [(i, i ^ bit) for i in range(lax.axis_size(axis))]
+
+
+def turns(axis, by):
+    size = lax.axis_size(axis)
+    return [(i, (i + by) % size) for i in range(size)]
+
+
+def rep_bits():
+    count = lax.axis_size("rep").bit_length() - 1
+    return [1 << i for i in range(count)]
+
+
+def bit_orders(bits):
+    rest = bits[1:]
+    return rest + bits[:1], rest[::-1] + bits[:1]
+
+
+def have(bit):
+    return (lax.axis_index("rep") & bit) != 0
+
+
+def my_place(bits):
+    place = jnp.int32(0)
+    for bit in bits:
+        place = place * 2 + have(bit).astype(jnp.int32)
+    return place
+
+
+def nothing(*refs):
+    pass
+
+
+def after(value, *deps):
+    if not deps:
+        return value
+    return pl.pallas_call(
+        nothing,
+        in_specs=[pl.BlockSpec(memory_space=pl.ANY)] * (1 + len(deps)),
+        out_specs=pl.BlockSpec(memory_space=pl.ANY),
+        out_shape=jax.ShapeDtypeStruct(value.shape, value.dtype),
+        input_output_aliases={0: 0},
+        name="after",
+    )(value, *deps)
+
+
+class Moves:
+    def start(self, stages):
+        self.stages = list(stages)
+        self.under_way = None
+        self.flying = []
+
+    def advance(self, *deps):
+        if self.under_way is not None:
+            self.under_way([after(item, *deps) for item in self.flying])
+            self.under_way = None
+        if self.stages:
+            self.flying, self.under_way = self.stages.pop(0)()
+        return self
+
+    def finish(self):
+        while self.stages or self.under_way is not None:
+            self.advance()
+
+    def swap(self, bit, place):
+        def send():
+            return [
+                lax.ppermute(part, "rep", places("rep", own)) for part, own in zip(self.parts, bit)
+            ], take
+
+        def take(others):
+            parts = []
+            for part, other, own in zip(self.parts, others, bit):
+                mine = have(own)
+                low, high = jnp.where(mine, other, part), jnp.where(mine, part, other)
+                parts.append(jnp.concatenate([low, high], axis=place + self.bits.index(own)))
+            self.parts = parts
+
+        return send
+
+    def fold(self, bit, place):
+        def send():
+            return [
+                lax.ppermute(side(part, place + self.bits.index(own), own, False), "rep", places("rep", own))
+                for part, own in zip(self.parts, bit)
+            ], take
+
+        def take(others):
+            self.parts = [
+                folded(part, other, place + self.bits.index(own), own)
+                for part, other, own in zip(self.parts, others, bit)
+            ]
+
+        return send
+
+
+def side(part, axis, bit, mine):
+    at = have(bit).astype(jnp.int32)
+    return lax.dynamic_slice_in_dim(part, at if mine else 1 - at, 1, axis=axis)
+
+
+def folded(part, other, axis, bit):
+    return (side(part, axis, bit, True).astype(F32) + other.astype(F32)).astype(BF16)
+
+
+class Gather(Moves):
+    def __init__(self, weight):
+        self.bits = rep_bits()
+        self.groups = lax.axis_size("shard")
+        self.shape = (self.groups * weight.shape[0], weight.shape[1])
+        self.weight = weight
+        self.start([self.over_shard] + [self.swap(bit, 1) for bit in zip(*bit_orders(self.bits))])
+
+    def send_after(self, *deps):
+        self.deps = deps
+        return self.advance()
+
+    def over_shard(self):
+        rows, columns = self.weight.shape[0] >> len(self.bits), self.weight.shape[1]
+        mine = lax.dynamic_slice_in_dim(self.weight, my_place(self.bits) * rows, rows, 0)
+        mine = after(mine, *self.deps)
+        here = lax.axis_index("shard")
+
+        def take(others):
+            parts = jnp.zeros((self.groups, rows, columns), self.weight.dtype)
+            parts = lax.dynamic_update_slice(parts, mine[None], (here, 0, 0))
+            for by, other in enumerate(others, 1):
+                parts = lax.dynamic_update_slice(parts, other[None], ((here - by) % self.groups, 0, 0))
+            parts = parts.reshape((self.groups,) + (1,) * len(self.bits) + (rows, columns))
+            half = self.groups // 2
+            self.parts = [parts[:half], parts[half:]] if half else [parts]
+
+        return [lax.ppermute(mine, "shard", turns("shard", by)) for by in range(1, self.groups)], take
+
+    def result(self):
+        self.finish()
+        return jnp.concatenate(self.parts, axis=0).reshape(self.shape)
+
+
+class Sum(Moves):
+    def __init__(self, *grads):
+        self.bits = rep_bits()
+        self.groups = lax.axis_size("shard")
+        self.rows = grads[0].shape[0] // self.groups >> len(self.bits)
+        self.widths = [grad.shape[1] for grad in grads]
+        self.columns = sum(self.widths)
+        inside = (self.groups,) + (2,) * len(self.bits) + (self.rows,)
+        self.grads = [grad.reshape(inside + (grad.shape[1],)) for grad in grads]
+        orders = list(zip(*bit_orders(self.bits)))
+        self.start(
+            [self.over_bit_0]
+            + [self.fold(bit, 1) for bit in orders[:-1]]
+            + [self.over_shard]
+            + [self.swap(bit, 0) for bit in orders]
+        )
+        self.advance()
+
+    def over_bit_0(self):
+        def take(others):
+            parts = self.grads
+            if self.bits:
+                parts = [folded(part, other, 1, self.bits[0]) for part, other in zip(parts, others)]
+            part = jnp.concatenate(parts, axis=-1)
+            half = self.groups // 2
+            self.parts = [part[:half], part[half:]] if half else [part]
+
+        if not self.bits:
+            return [], take
+        bit = self.bits[0]
+        return [lax.ppermute(side(part, 1, bit, False), "rep", places("rep", bit)) for part in self.grads], take
+
+    def over_shard(self):
+        part = jnp.concatenate(self.parts, axis=0).reshape(self.groups, self.rows, self.columns)
+        here = lax.axis_index("shard")
+
+        def of(by):
+            return lax.dynamic_index_in_dim(part, (here + by) % self.groups, 0, keepdims=False)
+
+        def take(others):
+            total = of(0).astype(F32)
+            for other in others:
+                total = total + other.astype(F32)
+            mine = total.astype(BF16).reshape((1,) * len(self.bits) + (self.rows, self.columns))
+            half = self.rows // 2
+            self.parts = [mine[..., :half, :], mine[..., half:, :]]
+
+        return [lax.ppermute(of(by), "shard", turns("shard", by)) for by in range(1, self.groups)], take
+
+    def result(self):
+        self.finish()
+        whole = jnp.concatenate(self.parts, axis=-2)
+        whole = whole.reshape(-1, self.columns).astype(F32)
+        ends = [sum(self.widths[: at + 1]) for at in range(len(self.widths))]
+        return [whole[:, end - width : end] for end, width in zip(ends, self.widths)]
 
 
 def gathered(weight):
@@ -591,9 +848,13 @@
     return lax.all_gather(mine, ("shard", "rep"), axis=0, tiled=True)
 
 
-def summed(grad):
-    mine = lax.psum_scatter(grad.astype(BF16), ("shard", "rep"), scatter_dimension=0, tiled=True)
-    return lax.all_gather(mine, "rep", axis=0, tiled=True).astype(F32)
+def summed_small(values):
+    for axis in ("rep", "shard"):
+        bit = 1
+        while bit < lax.axis_size(axis):
+            values = values + lax.ppermute(values, axis, places(axis, bit))
+            bit *= 2
+    return values
 
 
 def shards(
@@ -622,20 +883,34 @@
     qkv = attn_in.shape[1]
     lane_pad = LANES - heads
 
-    step_in = jnp.pad(mix_in[:, inner + channels :], ((0, 0), (0, lane_pad)))
-    small_in = gathered(jnp.concatenate([attn_in, step_in], axis=1))
-    full_norms = lax.all_gather(jnp.stack([norm_in, norm_ff]), "shard", axis=1, tiled=True).astype(F32)
-    conv_in = gathered(mix_in[:, inner : inner + channels])
-    gate_in = gathered(mix_in[:, :inner])
-    full_attn_out = gathered(attn_out)
-    full_mix_out = gathered(mix_out)
-    full_ff_in = gathered(ff_in)
-    full_ff_out = gathered(ff_out)
+    main = inner + channels
+    half = inner // 2
+    extra = jnp.concatenate([attn_in, jnp.stack([norm_in, norm_ff], axis=1)], axis=1)
+    from_small = Gather(jnp.pad(extra, ((0, 0), (0, LANES - 2)))).send_after()
+    from_main = Gather(
+        jnp.concatenate(
+            [
+                mix_in[:, :half],
+                mix_in[:, inner : inner + half],
+                mix_in[:, half:inner],
+                mix_in[:, inner + half :],
+                jnp.zeros((mix_in.shape[0], lane_pad), BF16),
+            ],
+            axis=1,
+        )
+    ).send_after(*from_small.flying)
+    small_in = from_small.result()
+    main_in = from_main.result()
+    outs_wide = attn_out.shape[1] + mix_out.shape[1]
+    ff_wide = outs_wide + ff_in.shape[1]
+    late = gathered(jnp.concatenate([attn_out, mix_out, ff_in, ff_out], axis=1))
+    full_outs = late[:, :outs_wide]
+    full_ff_in = late[:, outs_wide:ff_wide]
+    full_ff_out = late[:, ff_wide:]
 
     ids = segment_ids.reshape(length)
     marks = token_marks(ids)
-    id_col = ids.reshape(length, 1)
-    id_row = ids.reshape(1, length)
+    id_row = ids.astype(F32).reshape(1, length)
     chunk_rows = ids.astype(F32).reshape(length // CHUNK, 1, CHUNK)
     cosine, sine = rotary_tables(length, HDIM)
 
@@ -654,17 +929,19 @@
     expand = jnp.concatenate([expand, expand], axis=0)
 
     resid = x_in.reshape(length, model).astype(F32)
+    full_norms = small_in[:, qkv : qkv + 2].astype(F32).T
     first_scale = norm_scale(resid)
     first_low = (resid * first_scale * full_norms[0]).astype(BF16)
-    small = dot_nn(first_low, small_in)
-    query, keys, values, attended, lse = attention_fwd(small[:, :qkv], cosine, sine, id_col, id_row)
-    step_raw = small[:, qkv:]
-    conv_input = dot_nn(first_low, conv_in).astype(BF16)
-    gate_part = dot_nn(first_low, gate_in).astype(BF16)
+    attn_proj = dot_nn(first_low, small_in[:, :qkv])
+    query, keys, values, attended, lse = attention_fwd(attn_proj, cosine, sine, marks, id_row)
+    step_raw = dot_nn(first_low, main_in[:, main:])
+    projected = dot_nn(first_low, main_in[:, :main]).astype(BF16)
     scanned, starts, mixed = mixer_fwd(
-        gate_part, conv_input, step_raw, marks, chunk_rows, kern, bias, rate, dtb, skips, gain, expand
-    )
-    hidden = resid + dot_nt(attended, full_attn_out) + dot_nt(mixed, full_mix_out)
+        projected, step_raw, marks, chunk_rows, kern, bias, rate, dtb, skips, gain, expand
+    )
+    attw = attended.shape[1]
+    branches = jnp.concatenate([attended, mixed], axis=1)
+    hidden = resid + dot_nt(branches, full_outs)
     second_scale = norm_scale(hidden)
     second_low = (hidden * second_scale * full_norms[1]).astype(BF16)
     ff_proj = dot_nn(second_low, full_ff_in)
@@ -676,37 +953,59 @@
     output = (hidden + dot_nt(act_low, full_ff_out)).astype(BF16).reshape(x_in.shape)
 
     grad_out = cotangent.reshape(length, model)
-    ff_out_grad = summed(dot_tn(grad_out, act_low))
+    ff_out_part = dot_tn(grad_out, act_low).astype(BF16)
     grad_act = dot_nn(grad_out, full_ff_out)
     grad_ff = jnp.concatenate(
         [grad_act * up * (opened + silu * (1.0 - opened)), grad_act * silu], axis=1
     ).astype(BF16)
-    ff_in_grad = summed(dot_tn(second_low, grad_ff))
+    sum_ff = Sum(ff_out_part, dot_tn(second_low, grad_ff).astype(BF16))
     grad_second = dot_nt(grad_ff, full_ff_in)
     grad_hidden, norm_ff_grad = norm_back(hidden, second_scale, full_norms[1], grad_second)
     grad_hidden = grad_hidden + grad_out.astype(F32)
     branch_low = grad_hidden.astype(BF16)
-    attn_out_grad = summed(dot_tn(branch_low, attended))
-    mix_out_grad = summed(dot_tn(branch_low, mixed))
-    grad_attended = dot_nn(branch_low, full_attn_out).astype(BF16)
-    grad_mixed = dot_nn(branch_low, full_mix_out).astype(BF16)
-    d_gate, d_conv, d_step, d_kern, d_gain, d_skip, d_head = mixer_bwd(
-        grad_mixed, gate_part, conv_input, step_raw, marks, chunk_rows, scanned, starts,
-        kern, bias, rate, dtb, skips, gain, expand, gather,
-    )
-    gate_in_grad = dot_tn(first_low, d_gate)
-    conv_in_grad = dot_tn(first_low, d_conv)
-    grad_attn_proj = attention_bwd(query, keys, values, lse, grad_attended, cosine, sine, id_col, id_row)
-    d_small = jnp.concatenate([grad_attn_proj, d_step], axis=1)
-    small_in_grad = dot_tn(first_low, d_small)
-    gate_sum = summed(gate_in_grad)
-    conv_sum = summed(conv_in_grad)
-    small_sum = summed(small_in_grad)
-    grad_first = dot_nt(d_gate, gate_in) + dot_nt(d_conv, conv_in) + dot_nt(d_small, small_in)
+    sum_ff.advance(branch_low)
+    outs_part = dot_tn(branch_low, branches).astype(BF16)
+    grad_branches = dot_nn(branch_low, full_outs).astype(BF16)
+    d_attn = attention_bwd(
+        sum_ff.parts, query, keys, values, lse, grad_branches[:, :attw], cosine, sine, marks, id_row
+    )
+    sum_ff.advance(d_attn)
+    sum_mid = Sum(outs_part, dot_tn(first_low, d_attn).astype(BF16))
+    common = (step_raw, marks, chunk_rows, scanned, starts, kern, bias, rate, dtb, skips, gain, expand, gather)
+    d_first, d_kern_a, d_gain_a, d_skip_a, d_head_a, handed = mixer_bwd(
+        False, sum_ff.parts, grad_branches[:, attw:], projected, *common
+    )
+    sum_ff.advance(d_first)
+    sum_mid.advance(d_first)
+    d_main, d_kern_b, d_gain_b, d_skip_b, d_head_b = mixer_bwd(
+        True, sum_ff.parts + sum_mid.parts, grad_branches[:, attw:], projected, *common, part=(handed, d_first)
+    )
+    sum_ff.advance(d_main)
+    sum_mid.advance(d_main)
+    sum_main = Sum(dot_tn(first_low, d_main).astype(BF16))
+    grad_first = dot_nt(d_main, main_in) + dot_nt(d_attn, small_in[:, :qkv])
     grad_resid, norm_in_grad = norm_back(resid, first_scale, full_norms[0], grad_first)
     input_grad = (grad_resid + grad_hidden).astype(BF16).reshape(x_in.shape)
-    mix_in_grad = jnp.concatenate([gate_sum, conv_sum, small_sum[:, qkv : qkv + heads]], axis=1)
-    attn_in_grad = small_sum[:, :qkv]
+    sums = (sum_ff, sum_mid, sum_main)
+    while any(item.stages for item in sums):
+        for item in sums:
+            item.advance()
+    ff_out_grad, ff_in_grad = sum_ff.result()
+    outs_sum, attn_in_grad = sum_mid.result()
+    main_sum = sum_main.result()[0]
+    mix_in_grad = jnp.concatenate(
+        [
+            main_sum[:, :half],
+            main_sum[:, inner : inner + half],
+            main_sum[:, half:inner],
+            main_sum[:, inner + half : main + heads],
+        ],
+        axis=1,
+    )
+    d_kern = jnp.concatenate([d_kern_a, d_kern_b], axis=1)
+    d_gain = jnp.concatenate([d_gain_a, d_gain_b], axis=1)
+    d_skip = jnp.concatenate([d_skip_a, d_skip_b], axis=1)
+    d_head = d_head_a + d_head_b
 
     pieces = (
         d_kern[:CONV].reshape(-1),
@@ -718,7 +1017,7 @@
         norm_in_grad,
         norm_ff_grad,
     )
-    packed = lax.psum(jnp.concatenate(pieces), ("rep", "shard"))
+    packed = summed_small(jnp.concatenate(pieces))
     split = []
     at = 0
     for piece in pieces:
@@ -732,8 +1031,8 @@
         lax.dynamic_slice_in_dim(split[6], mine, rows, 0),
         mix_in_grad,
         attn_in_grad,
-        attn_out_grad,
-        mix_out_grad,
+        outs_sum[:, :attw],
+        outs_sum[:, attw:],
         lax.dynamic_slice_in_dim(split[7], mine, rows, 0),
         ff_in_grad,
         ff_out_grad,

time: 1450 us -> 642 us (0.44)
  waiting for transfers between devices: 968 us -> 140 us
  blocking collectives: 106 us -> 0 us
  starting transfers between devices: 1.07 us -> 77.1 us
  other arithmetic: 24.7 us -> 70.3 us
  matrix products: 175 us -> 142 us
  local copies, waits for them, and re-layouts: 58.8 us -> 78.8 us
    reduce_scatter x7 -> x0, waiting for transfers between devices: 620 us -> none  [summed(): lax.psum_scatter(grad.astype(BF16), ('shard', 'rep'), scatter_dimension=0...]
    all_gather x7 -> x1, waiting for transfers between devices: 319 us -> 0.01 us  [gathered(): return lax.all_gather(mine, ('shard', 'rep'), axis=0, tiled=True)]
    ppermute x0 -> x67, waiting for transfers between devices: none -> 140 us  [the longest x30 50.5 us: send(): lax.ppermute(part, 'rep', places('rep', own))]
    ppermute x0 -> x67, starting transfers between devices: none -> 77.1 us  [the longest x30 29.8 us: send(): lax.ppermute(part, 'rep', places('rep', own))]
    all_gather x6 -> x0, blocking collectives: 64 us -> none  [the longest x5 51.1 us: summed(): return lax.all_gather(mine, 'rep', axis=0, tiled=True).astype(F32)]
    psum x1 -> x0, blocking collectives: 41.8 us -> none  [shards(): packed = lax.psum(jnp.concatenate(pieces), ('rep', 'shard'))]
    all_gather x2 -> x0, waiting for transfers between devices: 29.5 us -> none  [summed(): return lax.all_gather(mine, 'rep', axis=0, tiled=True).astype(F32)]
    convert_element_type x6 -> x21, other arithmetic: 9.36 us -> 32.8 us  [the longest x17 31.2 us: folded(): (side(part, axis, bit, True).astype(F32) + other.astype(F32)).astype(BF16)]
  transfers between devices with their start and end apart: 16 -> 68, of which waited for: 15 -> 24; matrix products, arithmetic and copies ran while one was open for 15% -> 27% of each run, Pallas kernels for 7% -> 17%
where the time goes in v2:
time: 642 us; the launch traced here: 635 us
  matrix products  142 us (22%)
  waiting for transfers between devices  140 us (22%)
  Pallas kernels  110 us (17%)
  local copies, waits for them, and re-layouts  78.8 us (12%)
  starting transfers between devices  77.1 us (12%)
  other arithmetic  70.3 us (11%)
  between operations  16.8 us (3%)
    pallas_call x2, Pallas kernels, mixer_bwd(): pl.pallas_call(partial(mixer_bwd_kernel, inner, second, len(deps)), grid=...  57.8 us
    dot_general x6, matrix products, dot_nn(): lax.dot_general(left, right, (((1,), (0,)), ((), ())), precision=precisio...  51.4 us
    ppermute x30, waiting for transfers between devices, send(): lax.ppermute(part, 'rep', places('rep', own))  50.5 us
    dot_general x5, matrix products, dot_nt(): lax.dot_general(left, right, (((1,), (1,)), ((), ())), preferred_element_...  49.2 us
    dot_general x5, matrix products, dot_tn(): lax.dot_general(left, right, (((0,), (0,)), ((), ())), preferred_element_...  41.6 us
    ppermute x9, waiting for transfers between devices, over_shard(): lax.ppermute(of(by), 'shard', turns('shard', by))  39.9 us
    ppermute x12, waiting for transfers between devices, send(): lax.ppermute(side(part, place + self.bits.index(own), own, False), 'rep',...  34.1 us
    unnamed x233, local copies, waits for them, and re-layouts  34.1 us
  transfers between devices with their start and end apart: 68, of which 24 were waited for; matrix products, arithmetic and copies ran while one was open for 27% of the time, Pallas kernels for 17%

profile of v2, /device:TPU:0, one launch (start us, length us, event | category | flops | bytes accessed | tf_op | source)
XLA Modules:
  0.0 635.3 jit_solution(12153456954098261281)
XLA Ops:
  7.3 2.0 fusion.49
  11.0 3.0 collective-permute-start
  14.0 2.6 collective-permute-start.1
  21.1 2.0 concatenate.168
  23.5 2.2 fusion.13
  31.8 3.3 collective-permute-start.11
  50.2 2.9 collective-permute-done.10
  57.0 17.5 %collective-permute-done.12 = bf16[2,1,1,1,32,3456]{5,4,3,2,1,0:T(8,128)(2,1)S(1)} collective-permute-done((bf16[2,1,1,1,32,3456]{5,4,3,2,1,0:T(8,128)(2,1)S(1)}, bf16[2,1,1,1,32,3456]{5,4,3,2,1,0:T(8,128)(2,1)S(1)}, u32[]{:S(2)}, u32[]{:S(2)}) %collective-permute-start.12) | collective-permute-done | bytes 442400 | tf_op jit(solution)/shard_map/ppermute | solution.py:715
  74.7 2.2 collective-permute-start.16
  80.8 3.5 fusion.39.proj_ref
  84.3 14.6 %collective-permute-done.16 = bf16[2,1,1,2,32,3456]{5,4,3,2,1,0:T(8,128)(2,1)S(1)} collective-permute-done((bf16[2,1,1,2,32,3456]{5,4,3,2,1,0:T(8,128)(2,1)S(1)}, bf16[2,1,1,2,32,3456]{5,4,3,2,1,0:T(8,128)(2,1)S(1)}, u32[]{:S(2)}, u32[]{:S(2)}) %collective-permute-start.16) | collective-permute-done | bytes 884768 | tf_op jit(solution)/shard_map/ppermute | solution.py:715
  101.5 11.8 %attention_fwd.1 = (bf16[1024,512]{1,0:T(8,128)(2,1)S(1)}, bf16[1024,128]{1,0:T(8,128)(2,1)S(1)}, bf16[1024,128]{1,0:T(8,128)(2,1)S(1)}, bf16[1024,512]{1,0:T(8,128)(2,1)S(1)}, f32[8,1024]{1,0:T(8,128)S(1)}) custom-call(f32[1024,768]{1,0:T(8,128)} %fusion.39.proj_ref, f32[1024,128]{1,0:T(8,128)S(1)} %get-tuple-element.220.cos_ref.refs_7_, ...), custom_call_target="tpu_custom_call" | custom-call | flops 30000001024 | bytes 8388608 | tf_op jit(solution)/shard_map/attention_fwd/pallas_call | solution.py:122
  118.5 9.4 %convolution_convert_fusion.2.proj_ref.refs_3_.refs_4_.refs_5_.refs_6_ = bf16[1024,3328]{1,0:T(8,128)(2,1)} fusion(bf16[1024,3456]{1,0:T(8,128)(2,1)S(1)} %bitcast.153, bf16[1,1024,1024]{2,1,0:T(8,128)(2,1)S(1)} %copy-done.65, f32[1024]{0:T(1024)S(1)} %get-tuple-element.107, f32[1024]{0:T(1024)S(1)} %add_rsqrt_fusion.1), kind=kOutput, calls=%fused_computation.17 | convolution fusion | flops 6986924032 | bytes 15736832 | tf_op jit(solution)/shard_map/dot_general | solution.py:27
  128.0 19.2 %mixer_fwd.1 = (f32[1024,1536]{1,0:T(8,128)}, bf16[8,128,1536]{2,1,0:T(8,128)(2,1)S(1)}, bf16[1024,1536]{1,0:T(8,128)(2,1)}) custom-call(bf16[1024,3328]{1,0:T(8,128)(2,1)} %convolution_convert_fusion.2.proj_ref.refs_3_.refs_4_.refs_5_.refs_6_, f32[1024,128]{1,0:T(8,128)S(1)} %fusion.67.step_ref.refs_5_.refs_7_, ...), custom_call_target="tpu_custom_call" | custom-call | flops 30000001024 | bytes 20971520 | tf_op jit(solution)/shard_map/mixer_fwd/pallas_call | solution.py:365
  148.9 4.0 constant_dynamic-update-slice_fusion
  152.9 8.7 %multiply_reduce_fusion.2 = (f32[1024]{0:T(1024)S(1)}, f32[1024,1024]{1,0:T(8,128)S(1)}) fusion(bf16[1024,2048]{1,0:T(8,128)(2,1)} %constant_dynamic-update-slice_fusion, bf16[1024,8192]{1,0:T(8,128)(2,1)} %all-gather.2.cloned.1.call-done, bf16[1,1024,1024]{2,1,0:T(8,128)(2,1)} %param.17), kind=kOutput, calls=%fused_computation.47 | convolution fusion | flops 4299160576 | bytes 14684160 | tf_op jit(solution)/shard_map/dot_general | solution.py:33
  161.7 16.5 %fusion.6 = f32[1024,4096]{1,0:T(8,128)} fusion(bf16[1024,8192]{1,0:T(8,128)(2,1)} %all-gather.2.cloned.1.call-done, f32[1024,1024]{1,0:T(8,128)S(1)} %get-tuple-element.235, f32[1024]{0:T(1024)S(1)} %get-tuple-element.106, f32[1024]{0:T(1024)S(1)} %add_rsqrt_fusion), kind=kOutput, calls=%fused_computation.20 | convolution fusion | flops 8593080320 | bytes 29368320 | tf_op jit(solution)/shard_map/dot_general | solution.py:27
  178.2 13.6 %fusion.1 = (bf16[1024,2048]{1,0:T(8,128)(2,1)S(1)}, bf16[1024,2048]{1,0:T(8,128)(2,1)}, bf16[1024,2048]{1,0:T(8,128)(2,1)}) fusion(f32[1024,4096]{1,0:T(8,128)} %fusion.6, bf16[1024,8192]{1,0:T(8,128)(2,1)} %all-gather.2.cloned.1.call-done, bf16[1,1024,1024]{2,1,0:T(8,128)(2,1)S(1)} %copy-done.63), kind=kOutput, calls=%fused_computation.4 | convolution fusion | flops 4324327424 | bytes 35651584 | tf_op jit(solution)/shard_map/dot_general | solution.py:27
  193.7 13.8 %convolution_convert_fusion.1 = bf16[1024,4096]{1,0:T(8,128)(2,1)} fusion(bf16[1024,2048]{1,0:T(8,128)(2,1)} %get-tuple-element.111, bf16[1024,2048]{1,0:T(8,128)(2,1)S(1)} %get-tuple-element.110, f32[1024,1024]{1,0:T(8,128)S(1)} %get-tuple-element.235, f32[1024]{0:T(1024)S(1)} %get-tuple-element.106, f32[1024]{0:T(1024)S(1)} %add_rsqrt_fusion), kind=kOutput, calls=%fused_computation.16 | convolution fusion | flops 8614051840 | bytes 20979712 | tf_op jit(solution)/shard_map/dot_general | solution.py:37
  207.5 16.5 %multiply_reduce_fusion = (f32[1024]{0:T(1024)}, f32[1024]{0:T(1024)S(1)}, f32[1024,1024]{1,0:T(8,128)}) fusion(f32[1024,1024]{1,0:T(8,128)S(1)} %get-tuple-element.235, f32[1024]{0:T(1024)S(1)} %add_rsqrt_fusion, f32[1024]{0:T(1024)S(1)} %get-tuple-element.106, bf16[1024,8192]{1,0:T(8,128)(2,1)} %all-gather.2.cloned.1.call-done, ...), kind=kOutput, calls=%fused_computation.40 | convolution fusion | flops 8613001216 | bytes 25182208 | tf_op jit(solution)/shard_map/dot_general | solution.py:33
  224.0 3.6 fusion.113.refs_1_
  227.7 7.7 %convolution_convert_fusion.4 = bf16[1024,2048]{1,0:T(8,128)(2,1)S(1)} fusion(bf16[1024,1024]{1,0:T(8,128)(2,1)S(1)} %fusion.113.refs_1_, bf16[1024,8192]{1,0:T(8,128)(2,1)} %all-gather.2.cloned.1.call-done), kind=kOutput, calls=%fused_computation.49 | convolution fusion | flops 4297064448 | bytes 10485760 | tf_op jit(solution)/shard_map/dot_general | solution.py:27
  235.5 2.0 slice.282.refs_2_.refs_4_
  237.6 2.4 constant_dynamic-slice_fusion.13
  241.9 5.0 convolution_convert_fusion.5
  248.9 7.1 %convolution_convert_fusion.3 = bf16[1024,2048]{1,0:T(8,128)(2,1)S(1)} fusion(bf16[1024,1024]{1,0:T(8,128)(2,1)S(1)} %fusion.113.refs_1_, bf16[1024,2048]{1,0:T(8,128)(2,1)} %constant_dynamic-update-slice_fusion), kind=kOutput, calls=%fused_computation.48 | convolution fusion | flops 4297064448 | bytes 10485760 | tf_op jit(solution)/shard_map/dot_general | solution.py:37
  256.1 2.1 copy-done.69
  260.6 7.9 %fusion.26 = bf16[1,1024,1024]{2,1,0:T(8,128)(2,1)} fusion(f32[1024,1024]{1,0:T(8,128)S(1)} %copy-done.57, bf16[1024,2048]{1,0:T(8,128)(2,1)S(1)} %copy-done.107, bf16[1024,8192]{1,0:T(8,128)(2,1)} %all-gather.2.cloned.1.call-done), kind=kOutput, calls=%fused_computation.77 | convolution fusion | flops 4297064448 | bytes 14680064 | tf_op jit(solution)/shard_map/dot_general | solution.py:33
  268.5 4.4 add_convert_fusion.3
  273.0 5.1 add_convert_fusion
  278.1 2.3 pad_maximum_fusion.4
  280.7 2.3 collective-permute-start.20
  285.8 20.8 %attention_bwd.1.refs_1_ = bf16[1024,768]{1,0:T(8,128)(2,1)S(1)} custom-call(bf16[2,1,2,2,32,6144]{5,4,3,2,1,0:T(8,128)(2,1)} %copy-done.60, bf16[2,1,2,2,32,6144]{5,4,3,2,1,0:T(8,128)(2,1)} %get-tuple-element.113.refs_1_, bf16[1024,512]{1,0:T(8,128)(2,1)S(1)} %copy-done.44, bf16[1024,128]{1,0:T(8,128)(2,1)S(1)} %copy-done.46, ...), custom_call_target="tpu_custom_call" | custom-call | flops 49999998976 | bytes 8388608 | tf_op jit(solution)/shard_map/attention_bwd/pallas_call | solution.py:209
  306.7 2.2 convolution_convert_fusion.6
  310.0 3.8 fusion.37
  313.8 3.8 collective-permute-done.20.refs_0_
  317.6 2.2 add_convert_fusion.6.refs_0_
  322.4 2.3 add_convert_fusion.5.refs_1_
  327.6 29.7 %mixer_bwd_first.1 = (bf16[1024,1536]{1,0:T(8,128)(2,1)}, f32[8,768]{1,0:T(8,128)S(1)}, f32[8,768]{1,0:T(8,128)S(1)}, f32[8,768]{1,0:T(8,128)S(1)}, f32[8,128]{1,0:T(8,128)S(1)}, /*index=5*/f32[1024,640]{1,0:T(8,128)}) custom-call(bf16[2,1,1,2,32,6144]{5,4,3,2,1,0:T(8,128)(2,1)S(1)} %add_convert_fusion.6.refs_0_, ...), custom_call_target="tpu_custom_call" | custom-call | flops 30000001024 | bytes 20971520 | tf_op jit(solution)/shard_map/mixer_bwd_first/pallas_call | solution.py:593
  360.2 3.4 add_convert_fusion.2
  381.4 28.1 %mixer_bwd_second.1 = (bf16[1024,3456]{1,0:T(8,128)(2,1)}, f32[8,1024]{1,0:T(8,128)S(1)}, f32[8,768]{1,0:T(8,128)S(1)}, f32[8,768]{1,0:T(8,128)S(1)}, f32[8,128]{1,0:T(8,128)S(1)}) custom-call(bf16[2,1,1,1,32,6144]{5,4,3,2,1,0:T(8,128)(2,1)S(1)} %add_convert_fusion.11.refs_0_, bf16[2,1,1,1,32,6144]{5,4,3,2,1,0:T(8,128)(2,1)S(1)} %add_convert_fusion.10.refs_1_, ...), custom_call_target="tpu_custom_call" | custom-call | flops 30000001024 | bytes 20971520 | tf_op jit(solution)/shard_map/mixer_bwd_second/pallas_call | solution.py:593
  409.5 13.5 %convolution_convert_fusion = bf16[1024,3456]{1,0:T(8,128)(2,1)} fusion(bf16[1024,3456]{1,0:T(8,128)(2,1)} %get-tuple-element.45.refs_1_, bf16[1,1024,1024]{2,1,0:T(8,128)(2,1)S(1)} %copy-done.67, f32[1024]{0:T(1024)S(1)} %copy-done.90, f32[1024]{0:T(1024)S(1)} %copy-done.94), kind=kOutput, calls=%fused_computation.15 | convolution fusion | flops 7255490560 | bytes 16261120 | tf_op jit(solution)/shard_map/dot_general | solution.py:37
  423.1 12.2 %fusion.12 = (f32[1024]{0:T(1024)S(1)}, f32[1024]{0:T(1024)S(1)}, f32[1024,1024]{1,0:T(8,128)}) fusion(bf16[1,1024,1024]{2,1,0:T(8,128)(2,1)S(1)} %copy-done.67, f32[1024]{0:T(1024)S(1)} %copy-done.94, f32[1024]{0:T(1024)S(1)} %copy-done.90, f32[1024,1024]{1,0:T(8,128)S(1)} %copy-done.105, bf16[1024,3456]{1,0:T(8,128)(2,1)S(1)} %copy-done.51, ...), kind=kOutput, calls=%fused_computation.30 | convolution fusion | flops 7256143872 | bytes 24657920 | tf_op jit(solution)/shard_map/dot_general | solution.py:33
  435.7 4.0 constant_dynamic-slice_fusion.7
  441.1 2.1 add_convert_fusion.14
  454.2 6.5 %collective-permute-done.28 = f32[12616]{0:T(1024)S(1)} collective-permute-done((f32[12616]{0:T(1024)S(1)}, f32[12616]{0:T(1024)S(1)}, u32[]{:S(2)}, u32[]{:S(2)}) %collective-permute-start.28) | collective-permute-done | bytes 50496 | tf_op jit(solution)/shard_map/ppermute | solution.py:855
  460.7 7.7 %collective-permute-start.29 = (f32[12616]{0:T(1024)S(1)}, f32[12616]{0:T(1024)S(1)}, u32[]{:S(2)}, u32[]{:S(2)}) collective-permute-start(f32[12616]{0:T(1024)S(1)} %add.381), channel_id=1, source_target_pairs={{0,1},{1,0},{2,3},{3,2},{4,5},{5,4},{6,7},{7,6},{8,9},{9,8},{10,11... | collective-permute-start | bytes 151400 | tf_op jit(solution)/shard_map/ppermute | solution.py:855
  471.3 5.5 fusion.27
  476.8 5.7 collective-permute-done.30
  486.8 2.5 collective-permute-start.58
  494.6 20.8 %collective-permute-done.59.refs_0_ = bf16[32,6144]{1,0:T(8,128)(2,1)} collective-permute-done((bf16[32,6144]{1,0:T(8,128)(2,1)}, bf16[32,6144]{1,0:T(8,128)(2,1)}, u32[]{:S(2)}, u32[]{:S(2)}) %collective-permute-start.59) | collective-permute-done | bytes 393248 | tf_op jit(solution)/shard_map/ppermute | solution.py:834
  518.1 2.6 collective-permute-start.61
  522.2 3.5 collective-permute-done.50
  532.5 2.1 collective-permute-start.56
  535.7 6.8 %collective-permute-done.56 = bf16[1,1,2,16,2816]{4,3,2,1,0:T(8,128)(2,1)S(1)} collective-permute-done((bf16[1,1,2,16,2816]{4,3,2,1,0:T(8,128)(2,1)S(1)}, bf16[1,1,2,16,2816]{4,3,2,1,0:T(8,128)(2,1)S(1)}, u32[]{:S(2)}, u32[]{:S(2)}) %collective-permute-start.56) | collective-permute-done | bytes 180256 | tf_op jit(solution)/shard_map/ppermute | solution.py:715
  549.7 2.9 add_convert_fusion.1
  554.9 19.8 %collective-permute-done.32 = bf16[2,1,1,2,32,3456]{5,4,3,2,1,0:T(8,128)(2,1)S(1)} collective-permute-done((bf16[2,1,1,2,32,3456]{5,4,3,2,1,0:T(8,128)(2,1)S(1)}, bf16[2,1,1,2,32,3456]{5,4,3,2,1,0:T(8,128)(2,1)S(1)}, u32[]{:S(2)}, u32[]{:S(2)}) %collective-permute-start.32) | collective-permute-done | bytes 884768 | tf_op jit(solution)/shard_map/ppermute | solution.py:731
  577.0 9.4 %collective-permute-done.33 = bf16[2,1,1,1,32,3456]{5,4,3,2,1,0:T(8,128)(2,1)S(1)} collective-permute-done((bf16[2,1,1,1,32,3456]{5,4,3,2,1,0:T(8,128)(2,1)S(1)}, bf16[2,1,1,1,32,3456]{5,4,3,2,1,0:T(8,128)(2,1)S(1)}, u32[]{:S(2)}, u32[]{:S(2)}) %collective-permute-start.33) | collective-permute-done | bytes 442400 | tf_op jit(solution)/shard_map/ppermute | solution.py:731
  589.8 1.9 collective-permute-start.36
  592.1 2.8 collective-permute-done.38
  594.8 12.9 %collective-permute-done.37 = bf16[32,3456]{1,0:T(8,128)(2,1)S(1)} collective-permute-done((bf16[32,3456]{1,0:T(8,128)(2,1)S(1)}, bf16[32,3456]{1,0:T(8,128)(2,1)S(1)}, u32[]{:S(2)}, u32[]{:S(2)}) %collective-permute-start.37) | collective-permute-done | bytes 221216 | tf_op jit(solution)/shard_map/ppermute | solution.py:834
  610.8 2.5 slice.304
  617.2 3.6 collective-permute-done.43
  625.3 2.9 copy.130
  (535 shorter events, 146.7 us)
Async XLA Ops:
  7.2 145.7 %all-gather.2.cloned.1.call-start = ((), (), s32[]{:S(2)}) async-start(), calls=%async_computation | async-start | bytes 17301504 | tf_op jit(solution)/shard_map/all_gather | solution.py:848
  11.0 19.8 %collective-permute-start = (bf16[32,896]{1,0:T(8,128)(2,1)}, bf16[32,896]{1,0:T(8,128)(2,1)}, u32[]{:S(2)}, u32[]{:S(2)}) collective-permute-start(bf16[32,896]{1,0:T(8,128)(2,1)} %get-tuple-element.109), channel_id=1, source_target_pairs={{0,1},{1,2},{2,3},{3,0},{4,5},{5,6},{6,7},{7,4},{8,9},{9,10},{10,1... | collective-permute-start | bytes 172040 | tf_op jit(solution)/shard_map/ppermute | solution.py:780
  14.0 16.7 %collective-permute-start.1 = (bf16[32,896]{1,0:T(8,128)(2,1)}, bf16[32,896]{1,0:T(8,128)(2,1)}, u32[]{:S(2)}, u32[]{:S(2)}) collective-permute-start(bf16[32,896]{1,0:T(8,128)(2,1)} %get-tuple-element.109), channel_id=1, source_target_pairs={{0,2},{1,3},{2,0},{3,1},{4,6},{5,7},{6,4},{7,5},{8,10},{9,11},{10,... | collective-permute-start | bytes 172040 | tf_op jit(solution)/shard_map/ppermute | solution.py:780
  16.6 14.2 %collective-permute-start.2 = (bf16[32,896]{1,0:T(8,128)(2,1)}, bf16[32,896]{1,0:T(8,128)(2,1)}, u32[]{:S(2)}, u32[]{:S(2)}) collective-permute-start(bf16[32,896]{1,0:T(8,128)(2,1)} %get-tuple-element.109), channel_id=1, source_target_pairs={{0,3},{1,0},{2,1},{3,2},{4,7},{5,4},{6,5},{7,6},{8,11},{9,8},{10,9... | collective-permute-start | bytes 172040 | tf_op jit(solution)/shard_map/ppermute | solution.py:780
  30.8 19.3 %collective-permute-start.9 = (bf16[32,3456]{1,0:T(8,128)(2,1)}, bf16[32,3456]{1,0:T(8,128)(2,1)S(1)}, u32[]{:S(2)}, u32[]{:S(2)}) collective-permute-start(bf16[32,3456]{1,0:T(8,128)(2,1)} %after.14), channel_id=1, source_target_pairs={{0,1},{1,2},{2,3},{3,0},{4,5},{5,6},{6,7},{7,4},{8,9},{9,10},{10,1... | collective-permute-start | bytes 663560 | tf_op jit(solution)/shard_map/ppermute | solution.py:780
  31.6 21.5 %collective-permute-start.10 = (bf16[32,3456]{1,0:T(8,128)(2,1)}, bf16[32,3456]{1,0:T(8,128)(2,1)S(1)}, u32[]{:S(2)}, u32[]{:S(2)}) collective-permute-start(bf16[32,3456]{1,0:T(8,128)(2,1)} %after.14), channel_id=1, source_target_pairs={{0,2},{1,3},{2,0},{3,1},{4,6},{5,7},{6,4},{7,5},{8,10},{9,11},{10,... | collective-permute-start | bytes 663560 | tf_op jit(solution)/shard_map/ppermute | solution.py:780
  31.8 21.2 %collective-permute-start.11 = (bf16[32,3456]{1,0:T(8,128)(2,1)}, bf16[32,3456]{1,0:T(8,128)(2,1)S(1)}, u32[]{:S(2)}, u32[]{:S(2)}) collective-permute-start(bf16[32,3456]{1,0:T(8,128)(2,1)} %after.14), channel_id=1, source_target_pairs={{0,3},{1,0},{2,1},{3,2},{4,7},{5,4},{6,5},{7,6},{8,11},{9,8},{10,9... | collective-permute-start | bytes 663560 | tf_op jit(solution)/shard_map/ppermute | solution.py:780
  40.5 4.9 collective-permute-start.3
  42.1 4.8 collective-permute-start.6
  47.9 8.2 %collective-permute-start.7 = (bf16[2,1,1,2,32,896]{5,4,3,2,1,0:T(8,128)(2,1)S(1)}, bf16[2,1,1,2,32,896]{5,4,3,2,1,0:T(8,128)(2,1)S(1)}, u32[]{:S(2)}, u32[]{:S(2)}) collective-permute-start(bf16[2,1,1,2,32,896]{5,4,3,2,1,0:T(8,128)(2,1)S(1)} %pad_maximum_fusion.21), channel_id=1, source_target_pairs={{0,8},{4,12},{8,0},{12,4},{16,24},{20,28},{24,16},{28,20},{1,9},{5... | collective-permute-start | bytes 688136 | tf_op jit(solution)/shard_map/ppermute | solution.py:715
  48.5 7.8 %collective-permute-start.4 = (bf16[2,1,2,1,32,896]{5,4,3,2,1,0:T(8,128)(2,1)S(1)}, bf16[2,1,2,1,32,896]{5,4,3,2,1,0:T(8,128)(2,1)S(1)}, u32[]{:S(2)}, u32[]{:S(2)}) collective-permute-start(bf16[2,1,2,1,32,896]{5,4,3,2,1,0:T(8,128)(2,1)S(1)} %pad_maximum_fusion.20), channel_id=1, source_target_pairs={{0,16},{4,20},{8,24},{12,28},{16,0},{20,4},{24,8},{28,12},{1,17},{... | collective-permute-start | bytes 688136 | tf_op jit(solution)/shard_map/ppermute | solution.py:715
  53.2 21.3 %collective-permute-start.12 = (bf16[2,1,1,1,32,3456]{5,4,3,2,1,0:T(8,128)(2,1)S(1)}, bf16[2,1,1,1,32,3456]{5,4,3,2,1,0:T(8,128)(2,1)S(1)}, u32[]{:S(2)}, u32[]{:S(2)}) collective-permute-start(bf16[2,1,1,1,32,3456]{5,4,3,2,1,0:T(8,128)(2,1)S(1)} %get-tuple-element.157), channel_id=1, source_target_pairs={{0,8},{4,12},{8,0},{12,4},{16,24},{20,28},{24,16},{28,20},{1,9},{5... | collective-permute-start | bytes 1327112 | tf_op jit(solution)/shard_map/ppermute | solution.py:715
  54.8 19.7 %collective-permute-start.15 = (bf16[2,1,1,1,32,3456]{5,4,3,2,1,0:T(8,128)(2,1)S(1)}, bf16[2,1,1,1,32,3456]{5,4,3,2,1,0:T(8,128)(2,1)S(1)}, u32[]{:S(2)}, u32[]{:S(2)}) collective-permute-start(bf16[2,1,1,1,32,3456]{5,4,3,2,1,0:T(8,128)(2,1)S(1)} %get-tuple-element.158), channel_id=1, source_target_pairs={{0,16},{4,20},{8,24},{12,28},{16,0},{20,4},{24,8},{28,12},{1,17},{... | collective-permute-start | bytes 1327112 | tf_op jit(solution)/shard_map/ppermute | solution.py:715
  56.2 22.2 %collective-permute-start.8 = (bf16[2,1,2,2,32,896]{5,4,3,2,1,0:T(8,128)(2,1)S(1)}, bf16[2,1,2,2,32,896]{5,4,3,2,1,0:T(8,128)(2,1)S(1)}, u32[]{:S(2)}, u32[]{:S(2)}) collective-permute-start(bf16[2,1,2,2,32,896]{5,4,3,2,1,0:T(8,128)(2,1)S(1)} %pad_maximum_fusion.13), channel_id=1, source_target_pairs={{0,4},{4,0},{8,12},{12,8},{16,20},{20,16},{24,28},{28,24},{1,5},{5... | collective-permute-start | bytes 1376264 | tf_op jit(solution)/shard_map/ppermute | solution.py:715
  56.5 22.2 %collective-permute-start.5 = (bf16[2,1,2,2,32,896]{5,4,3,2,1,0:T(8,128)(2,1)S(1)}, bf16[2,1,2,2,32,896]{5,4,3,2,1,0:T(8,128)(2,1)S(1)}, u32[]{:S(2)}, u32[]{:S(2)}) collective-permute-start(bf16[2,1,2,2,32,896]{5,4,3,2,1,0:T(8,128)(2,1)S(1)} %pad_maximum_fusion.12), channel_id=1, source_target_pairs={{0,4},{4,0},{8,12},{12,8},{16,20},{20,16},{24,28},{28,24},{1,5},{5... | collective-permute-start | bytes 1376264 | tf_op jit(solution)/shard_map/ppermute | solution.py:715
  74.7 24.2 %collective-permute-start.16 = (bf16[2,1,1,2,32,3456]{5,4,3,2,1,0:T(8,128)(2,1)S(1)}, bf16[2,1,1,2,32,3456]{5,4,3,2,1,0:T(8,128)(2,1)S(1)}, u32[]{:S(2)}, u32[]{:S(2)}) collective-permute-start(bf16[2,1,1,2,32,3456]{5,4,3,2,1,0:T(8,128)(2,1)S(1)} %pad_maximum_fusion.9), channel_id=1, source_target_pairs={{0,8},{4,12},{8,0},{12,4},{16,24},{20,28},{24,16},{28,20},{1,9},{5... | collective-permute-start | bytes 2654216 | tf_op jit(solution)/shard_map/ppermute | solution.py:715
  77.1 22.3 %collective-permute-start.13 = (bf16[2,1,2,1,32,3456]{5,4,3,2,1,0:T(8,128)(2,1)S(1)}, bf16[2,1,2,1,32,3456]{5,4,3,2,1,0:T(8,128)(2,1)S(1)}, u32[]{:S(2)}, u32[]{:S(2)}) collective-permute-start(bf16[2,1,2,1,32,3456]{5,4,3,2,1,0:T(8,128)(2,1)S(1)} %pad_maximum_fusion.8), channel_id=1, source_target_pairs={{0,16},{4,20},{8,24},{12,28},{16,0},{20,4},{24,8},{28,12},{1,17},{... | collective-permute-start | bytes 2654216 | tf_op jit(solution)/shard_map/ppermute | solution.py:715
  99.3 15.1 %collective-permute-start.17 = (bf16[2,1,2,2,32,3456]{5,4,3,2,1,0:T(8,128)(2,1)S(1)}, bf16[2,1,2,2,32,3456]{5,4,3,2,1,0:T(8,128)(2,1)S(1)}, u32[]{:S(2)}, u32[]{:S(2)}) collective-permute-start(bf16[2,1,2,2,32,3456]{5,4,3,2,1,0:T(8,128)(2,1)S(1)} %pad_maximum_fusion.6), channel_id=1, source_target_pairs={{0,4},{4,0},{8,12},{12,8},{16,20},{20,16},{24,28},{28,24},{1,5},{5... | collective-permute-start | bytes 5308424 | tf_op jit(solution)/shard_map/ppermute | solution.py:715
  101.0 13.9 %collective-permute-start.14 = (bf16[2,1,2,2,32,3456]{5,4,3,2,1,0:T(8,128)(2,1)}, bf16[2,1,2,2,32,3456]{5,4,3,2,1,0:T(8,128)(2,1)}, u32[]{:S(2)}, u32[]{:S(2)}) collective-permute-start(bf16[2,1,2,2,32,3456]{5,4,3,2,1,0:T(8,128)(2,1)} %pad_maximum_fusion.5), channel_id=1, source_target_pairs={{0,4},{4,0},{8,12},{12,8},{16,20},{20,16},{24,28},{28,24},{1,5},{5... | collective-permute-start | bytes 5308424 | tf_op jit(solution)/shard_map/ppermute | solution.py:715
  240.0 33.0 %collective-permute-start.19 = (bf16[4,1,2,2,32,4096]{5,4,3,2,1,0:T(8,128)(2,1)}, bf16[4,1,2,2,32,4096]{5,4,3,2,1,0:T(8,128)(2,1)}, u32[]{:S(2)}, u32[]{:S(2)}) collective-permute-start(bf16[4,1,2,2,32,4096]{5,4,3,2,1,0:T(8,128)(2,1)} %constant_dynamic-slice_fusion.13), channel_id=1, source_target_pairs={{0,4},{4,0},{8,12},{12,8},{16,20},{20,16},{24,28},{28,24},{1,5},{5... | collective-permute-start | bytes 12582920 | tf_op jit(solution)/shard_map/ppermute | solution.py:817
  247.2 21.3 %collective-permute-start.18 = (bf16[4,1,2,2,32,2048]{5,4,3,2,1,0:T(8,128)(2,1)S(1)}, bf16[4,1,2,2,32,2048]{5,4,3,2,1,0:T(8,128)(2,1)}, u32[]{:S(2)}, u32[]{:S(2)}) collective-permute-start(bf16[4,1,2,2,32,2048]{5,4,3,2,1,0:T(8,128)(2,1)S(1)} %constant_dynamic-slice_fusion.14), channel_id=1, source_target_pairs={{0,4},{4,0},{8,12},{12,8},{16,20},{20,16},{24,28},{28,24},{1,5},{5... | collective-permute-start | bytes 6291464 | tf_op jit(solution)/shard_map/ppermute | solution.py:817
  259.7 100.5 %collective-permute-start.24 = (bf16[4,1,2,2,32,2048]{5,4,3,2,1,0:T(8,128)(2,1)}, bf16[4,1,2,2,32,2048]{5,4,3,2,1,0:T(8,128)(2,1)}, u32[]{:S(2)}, u32[]{:S(2)}) collective-permute-start(bf16[4,1,2,2,32,2048]{5,4,3,2,1,0:T(8,128)(2,1)} %constant_dynamic-slice_fusion.9), channel_id=1, source_target_pairs={{0,4},{4,0},{8,12},{12,8},{16,20},{20,16},{24,28},{28,24},{1,5},{5... | collective-permute-start | bytes 6291464 | tf_op jit(solution)/shard_map/ppermute | solution.py:817
  280.7 37.0 %collective-permute-start.20 = (bf16[2,1,1,2,32,6144]{5,4,3,2,1,0:T(8,128)(2,1)S(1)}, bf16[2,1,1,2,32,6144]{5,4,3,2,1,0:T(8,128)(2,1)}, u32[]{:S(2)}, u32[]{:S(2)}) collective-permute-start(bf16[2,1,1,2,32,6144]{5,4,3,2,1,0:T(8,128)(2,1)S(1)} %constant_dynamic-slice_fusion.12), channel_id=1, source_target_pairs={{0,8},{4,12},{8,0},{12,4},{16,24},{20,28},{24,16},{28,20},{1,9},{5... | collective-permute-start | bytes 4718600 | tf_op jit(solution)/shard_map/ppermute | solution.py:731
  284.2 38.1 %collective-permute-start.22 = (bf16[2,1,2,1,32,6144]{5,4,3,2,1,0:T(8,128)(2,1)}, bf16[2,1,2,1,32,6144]{5,4,3,2,1,0:T(8,128)(2,1)}, u32[]{:S(2)}, u32[]{:S(2)}) collective-permute-start(bf16[2,1,2,1,32,6144]{5,4,3,2,1,0:T(8,128)(2,1)} %fusion.35), channel_id=1, source_target_pairs={{0,16},{4,20},{8,24},{12,28},{16,0},{20,4},{24,8},{28,12},{1,17},{... | collective-permute-start | bytes 4718600 | tf_op jit(solution)/shard_map/ppermute | solution.py:731
  310.0 48.6 %collective-permute-start.25 = (bf16[4,1,2,2,32,768]{5,4,3,2,1,0:T(8,128)(2,1)}, bf16[4,1,2,2,32,768]{5,4,3,2,1,0:T(8,128)(2,1)}, u32[]{:S(2)}, u32[]{:S(2)}) collective-permute-start(bf16[4,1,2,2,32,768]{5,4,3,2,1,0:T(8,128)(2,1)} %constant_dynamic-slice_fusion.8), channel_id=1, source_target_pairs={{0,4},{4,0},{8,12},{12,8},{16,20},{20,16},{24,28},{28,24},{1,5},{5... | collective-permute-start | bytes 2359304 | tf_op jit(solution)/shard_map/ppermute | solution.py:817
  320.8 48.7 %collective-permute-start.21 = (bf16[2,1,1,1,32,6144]{5,4,3,2,1,0:T(8,128)(2,1)}, bf16[2,1,1,1,32,6144]{5,4,3,2,1,0:T(8,128)(2,1)}, u32[]{:S(2)}, u32[]{:S(2)}) collective-permute-start(bf16[2,1,1,1,32,6144]{5,4,3,2,1,0:T(8,128)(2,1)} %constant_dynamic-slice_fusion.11), channel_id=1, source_target_pairs={{0,16},{4,20},{8,24},{12,28},{16,0},{20,4},{24,8},{28,12},{1,17},{... | collective-permute-start | bytes 2359304 | tf_op jit(solution)/shard_map/ppermute | solution.py:731
  325.8 45.1 %collective-permute-start.23 = (bf16[2,1,1,1,32,6144]{5,4,3,2,1,0:T(8,128)(2,1)}, bf16[2,1,1,1,32,6144]{5,4,3,2,1,0:T(8,128)(2,1)}, u32[]{:S(2)}, u32[]{:S(2)}) collective-permute-start(bf16[2,1,1,1,32,6144]{5,4,3,2,1,0:T(8,128)(2,1)} %constant_dynamic-slice_fusion.10), channel_id=1, source_target_pairs={{0,8},{4,12},{8,0},{12,4},{16,24},{20,28},{24,16},{28,20},{1,9},{5... | collective-permute-start | bytes 2359304 | tf_op jit(solution)/shard_map/ppermute | solution.py:731
  367.1 72.6 %collective-permute-start.45 = (bf16[2,1,1,2,32,2816]{5,4,3,2,1,0:T(8,128)(2,1)}, bf16[2,1,1,2,32,2816]{5,4,3,2,1,0:T(8,128)(2,1)}, u32[]{:S(2)}, u32[]{:S(2)}) collective-permute-start(bf16[2,1,1,2,32,2816]{5,4,3,2,1,0:T(8,128)(2,1)} %constant_dynamic-slice_fusion.2), channel_id=1, source_target_pairs={{0,8},{4,12},{8,0},{12,4},{16,24},{20,28},{24,16},{28,20},{1,9},{5... | collective-permute-start | bytes 2162696 | tf_op jit(solution)/shard_map/ppermute | solution.py:731
  368.4 74.9 %collective-permute-start.47 = (bf16[2,1,2,1,32,2816]{5,4,3,2,1,0:T(8,128)(2,1)}, bf16[2,1,2,1,32,2816]{5,4,3,2,1,0:T(8,128)(2,1)}, u32[]{:S(2)}, u32[]{:S(2)}) collective-permute-start(bf16[2,1,2,1,32,2816]{5,4,3,2,1,0:T(8,128)(2,1)} %fusion.46), channel_id=1, source_target_pairs={{0,16},{4,20},{8,24},{12,28},{16,0},{20,4},{24,8},{28,12},{1,17},{... | collective-permute-start | bytes 2162696 | tf_op jit(solution)/shard_map/ppermute | solution.py:731
  435.7 10.9 %collective-permute-start.26 = (f32[12616]{0:T(1024)S(1)}, f32[12616]{0:T(1024)S(1)}, u32[]{:S(2)}, u32[]{:S(2)}) collective-permute-start(f32[12616]{0:T(1024)S(1)} %concatenate.186), channel_id=1, source_target_pairs={{0,4},{4,0},{8,12},{12,8},{16,20},{20,16},{24,28},{28,24},{1,5},{5... | collective-permute-start | bytes 151400 | tf_op jit(solution)/shard_map/ppermute | solution.py:855
  446.0 103.3 %collective-permute-start.31 = (bf16[4,1,2,2,32,3456]{5,4,3,2,1,0:T(8,128)(2,1)}, bf16[4,1,2,2,32,3456]{5,4,3,2,1,0:T(8,128)(2,1)}, u32[]{:S(2)}, u32[]{:S(2)}) collective-permute-start(bf16[4,1,2,2,32,3456]{5,4,3,2,1,0:T(8,128)(2,1)} %constant_dynamic-slice_fusion.7), channel_id=1, source_target_pairs={{0,4},{4,0},{8,12},{12,8},{16,20},{20,16},{24,28},{28,24},{1,5},{5... | collective-permute-start | bytes 10616840 | tf_op jit(solution)/shard_map/ppermute | solution.py:817
  446.6 4.4 collective-permute-start.27
  449.4 37.4 %collective-permute-start.46 = (bf16[2,1,1,1,32,2816]{5,4,3,2,1,0:T(8,128)(2,1)S(1)}, bf16[2,1,1,1,32,2816]{5,4,3,2,1,0:T(8,128)(2,1)}, u32[]{:S(2)}, u32[]{:S(2)}) collective-permute-start(bf16[2,1,1,1,32,2816]{5,4,3,2,1,0:T(8,128)(2,1)S(1)} %constant_dynamic-slice_fusion.1), channel_id=1, source_target_pairs={{0,16},{4,20},{8,24},{12,28},{16,0},{20,4},{24,8},{28,12},{1,17},{... | collective-permute-start | bytes 1081352 | tf_op jit(solution)/shard_map/ppermute | solution.py:731
  451.0 9.7 %collective-permute-start.28 = (f32[12616]{0:T(1024)S(1)}, f32[12616]{0:T(1024)S(1)}, u32[]{:S(2)}, u32[]{:S(2)}) collective-permute-start(f32[12616]{0:T(1024)S(1)} %add.380), channel_id=1, source_target_pairs={{0,16},{4,20},{8,24},{12,28},{16,0},{20,4},{24,8},{28,12},{1,17},{... | collective-permute-start | bytes 151400 | tf_op jit(solution)/shard_map/ppermute | solution.py:855
  452.4 38.1 %collective-permute-start.48 = (bf16[2,1,1,1,32,2816]{5,4,3,2,1,0:T(8,128)(2,1)S(1)}, bf16[2,1,1,1,32,2816]{5,4,3,2,1,0:T(8,128)(2,1)}, u32[]{:S(2)}, u32[]{:S(2)}) collective-permute-start(bf16[2,1,1,1,32,2816]{5,4,3,2,1,0:T(8,128)(2,1)S(1)} %constant_dynamic-slice_fusion), channel_id=1, source_target_pairs={{0,8},{4,12},{8,0},{12,4},{16,24},{20,28},{24,16},{28,20},{1,9},{5... | collective-permute-start | bytes 1081352 | tf_op jit(solution)/shard_map/ppermute | solution.py:731
  460.7 9.8 %collective-permute-start.29 = (f32[12616]{0:T(1024)S(1)}, f32[12616]{0:T(1024)S(1)}, u32[]{:S(2)}, u32[]{:S(2)}) collective-permute-start(f32[12616]{0:T(1024)S(1)} %add.381), channel_id=1, source_target_pairs={{0,1},{1,0},{2,3},{3,2},{4,5},{5,4},{6,7},{7,6},{8,9},{9,8},{10,11... | collective-permute-start | bytes 151400 | tf_op jit(solution)/shard_map/ppermute | solution.py:855
  469.6 24.2 %collective-permute-start.60 = (bf16[32,6144]{1,0:T(8,128)(2,1)}, bf16[32,6144]{1,0:T(8,128)(2,1)S(1)}, u32[]{:S(2)}, u32[]{:S(2)}) collective-permute-start(bf16[32,6144]{1,0:T(8,128)(2,1)} %get-tuple-element.139), channel_id=1, source_target_pairs={{0,3},{1,0},{2,1},{3,2},{4,7},{5,4},{6,5},{7,6},{8,11},{9,8},{10,9... | collective-permute-start | bytes 1179656 | tf_op jit(solution)/shard_map/ppermute | solution.py:834
  470.5 12.0 %collective-permute-start.30 = (f32[12616]{0:T(1024)S(1)}, f32[12616]{0:T(1024)S(1)}, u32[]{:S(2)}, u32[]{:S(2)}) collective-permute-start(f32[12616]{0:T(1024)S(1)} %add.382), channel_id=1, source_target_pairs={{0,2},{1,3},{2,0},{3,1},{4,6},{5,7},{6,4},{7,5},{8,10},{9,11},{10,... | collective-permute-start | bytes 151400 | tf_op jit(solution)/shard_map/ppermute | solution.py:855
  482.5 33.0 %collective-permute-start.59 = (bf16[32,6144]{1,0:T(8,128)(2,1)}, bf16[32,6144]{1,0:T(8,128)(2,1)}, u32[]{:S(2)}, u32[]{:S(2)}) collective-permute-start(bf16[32,6144]{1,0:T(8,128)(2,1)} %get-tuple-element.138), channel_id=1, source_target_pairs={{0,2},{1,3},{2,0},{3,1},{4,6},{5,7},{6,4},{7,5},{8,10},{9,11},{10,... | collective-permute-start | bytes 1179656 | tf_op jit(solution)/shard_map/ppermute | solution.py:834
  486.8 28.9 %collective-permute-start.58 = (bf16[32,6144]{1,0:T(8,128)(2,1)}, bf16[32,6144]{1,0:T(8,128)(2,1)}, u32[]{:S(2)}, u32[]{:S(2)}) collective-permute-start(bf16[32,6144]{1,0:T(8,128)(2,1)} %get-tuple-element.137), channel_id=1, source_target_pairs={{0,1},{1,2},{2,3},{3,0},{4,5},{5,6},{6,7},{7,4},{8,9},{9,10},{10,1... | collective-permute-start | bytes 1179656 | tf_op jit(solution)/shard_map/ppermute | solution.py:834
  492.5 28.3 %collective-permute-start.51 = (bf16[32,2816]{1,0:T(8,128)(2,1)}, bf16[32,2816]{1,0:T(8,128)(2,1)S(1)}, u32[]{:S(2)}, u32[]{:S(2)}) collective-permute-start(bf16[32,2816]{1,0:T(8,128)(2,1)} %get-tuple-element.169), channel_id=1, source_target_pairs={{0,3},{1,0},{2,1},{3,2},{4,7},{5,4},{6,5},{7,6},{8,11},{9,8},{10,9... | collective-permute-start | bytes 540680 | tf_op jit(solution)/shard_map/ppermute | solution.py:834
  493.9 31.8 %collective-permute-start.50 = (bf16[32,2816]{1,0:T(8,128)(2,1)}, bf16[32,2816]{1,0:T(8,128)(2,1)}, u32[]{:S(2)}, u32[]{:S(2)}) collective-permute-start(bf16[32,2816]{1,0:T(8,128)(2,1)} %get-tuple-element.168), channel_id=1, source_target_pairs={{0,2},{1,3},{2,0},{3,1},{4,6},{5,7},{6,4},{7,5},{8,10},{9,11},{10,... | collective-permute-start | bytes 540680 | tf_op jit(solution)/shard_map/ppermute | solution.py:834
  515.4 10.3 %collective-permute-start.49 = (bf16[32,2816]{1,0:T(8,128)(2,1)S(1)}, bf16[32,2816]{1,0:T(8,128)(2,1)S(1)}, u32[]{:S(2)}, u32[]{:S(2)}) collective-permute-start(bf16[32,2816]{1,0:T(8,128)(2,1)S(1)} %get-tuple-element.167), channel_id=1, source_target_pairs={{0,1},{1,2},{2,3},{3,0},{4,5},{5,6},{6,7},{7,4},{8,9},{9,10},{10,1... | collective-permute-start | bytes 540680 | tf_op jit(solution)/shard_map/ppermute | solution.py:834
  518.1 10.0 %collective-permute-start.61 = (bf16[1,1,1,16,6144]{4,3,2,1,0:T(8,128)(2,1)S(1)}, bf16[1,1,1,16,6144]{4,3,2,1,0:T(8,128)(2,1)S(1)}, u32[]{:S(2)}, u32[]{:S(2)}) collective-permute-start(bf16[1,1,1,16,6144]{4,3,2,1,0:T(8,128)(2,1)S(1)} %get-tuple-element.184), channel_id=1, source_target_pairs={{0,8},{4,12},{8,0},{12,4},{16,24},{20,28},{24,16},{28,20},{1,9},{5... | collective-permute-start | bytes 589832 | tf_op jit(solution)/shard_map/ppermute | solution.py:715
  520.8 7.3 %collective-permute-start.64 = (bf16[1,1,1,16,6144]{4,3,2,1,0:T(8,128)(2,1)S(1)}, bf16[1,1,1,16,6144]{4,3,2,1,0:T(8,128)(2,1)S(1)}, u32[]{:S(2)}, u32[]{:S(2)}) collective-permute-start(bf16[1,1,1,16,6144]{4,3,2,1,0:T(8,128)(2,1)S(1)} %get-tuple-element.185), channel_id=1, source_target_pairs={{0,16},{4,20},{8,24},{12,28},{16,0},{20,4},{24,8},{28,12},{1,17},{... | collective-permute-start | bytes 589832 | tf_op jit(solution)/shard_map/ppermute | solution.py:715
  526.8 5.6 collective-permute-start.52
  526.9 5.5 collective-permute-start.55
  528.2 15.7 %collective-permute-start.65 = (bf16[1,1,2,16,6144]{4,3,2,1,0:T(8,128)(2,1)S(1)}, bf16[1,1,2,16,6144]{4,3,2,1,0:T(8,128)(2,1)S(1)}, u32[]{:S(2)}, u32[]{:S(2)}) collective-permute-start(bf16[1,1,2,16,6144]{4,3,2,1,0:T(8,128)(2,1)S(1)} %pad_maximum_fusion.17), channel_id=1, source_target_pairs={{0,8},{4,12},{8,0},{12,4},{16,24},{20,28},{24,16},{28,20},{1,9},{5... | collective-permute-start | bytes 1179656 | tf_op jit(solution)/shard_map/ppermute | solution.py:715
  530.2 14.5 %collective-permute-start.62 = (bf16[1,2,1,16,6144]{4,3,2,1,0:T(8,128)(2,1)S(1)}, bf16[1,2,1,16,6144]{4,3,2,1,0:T(8,128)(2,1)S(1)}, u32[]{:S(2)}, u32[]{:S(2)}) collective-permute-start(bf16[1,2,1,16,6144]{4,3,2,1,0:T(8,128)(2,1)S(1)} %pad_maximum_fusion.16), channel_id=1, source_target_pairs={{0,16},{4,20},{8,24},{12,28},{16,0},{20,4},{24,8},{28,12},{1,17},{... | collective-permute-start | bytes 1179656 | tf_op jit(solution)/shard_map/ppermute | solution.py:715
  532.5 10.1 %collective-permute-start.56 = (bf16[1,1,2,16,2816]{4,3,2,1,0:T(8,128)(2,1)S(1)}, bf16[1,1,2,16,2816]{4,3,2,1,0:T(8,128)(2,1)S(1)}, u32[]{:S(2)}, u32[]{:S(2)}) collective-permute-start(bf16[1,1,2,16,2816]{4,3,2,1,0:T(8,128)(2,1)S(1)} %pad_maximum_fusion.25), channel_id=1, source_target_pairs={{0,8},{4,12},{8,0},{12,4},{16,24},{20,28},{24,16},{28,20},{1,9},{5... | collective-permute-start | bytes 540680 | tf_op jit(solution)/shard_map/ppermute | solution.py:715
  534.6 9.2 %collective-permute-start.53 = (bf16[1,2,1,16,2816]{4,3,2,1,0:T(8,128)(2,1)S(1)}, bf16[1,2,1,16,2816]{4,3,2,1,0:T(8,128)(2,1)S(1)}, u32[]{:S(2)}, u32[]{:S(2)}) collective-permute-start(bf16[1,2,1,16,2816]{4,3,2,1,0:T(8,128)(2,1)S(1)} %pad_maximum_fusion.24), channel_id=1, source_target_pairs={{0,16},{4,20},{8,24},{12,28},{16,0},{20,4},{24,8},{28,12},{1,17},{... | collective-permute-start | bytes 540680 | tf_op jit(solution)/shard_map/ppermute | solution.py:715
  544.1 5.1 collective-permute-start.66
  544.8 8.8 %collective-permute-start.63 = (bf16[1,2,2,16,6144]{4,3,2,1,0:T(8,128)(2,1)S(1)}, bf16[1,2,2,16,6144]{4,3,2,1,0:T(8,128)(2,1)S(1)}, u32[]{:S(2)}, u32[]{:S(2)}) collective-permute-start(bf16[1,2,2,16,6144]{4,3,2,1,0:T(8,128)(2,1)S(1)} %pad_maximum_fusion.10), channel_id=1, source_target_pairs={{0,4},{4,0},{8,12},{12,8},{16,20},{20,16},{24,28},{28,24},{1,5},{5... | collective-permute-start | bytes 2359304 | tf_op jit(solution)/shard_map/ppermute | solution.py:715
  552.9 21.8 %collective-permute-start.32 = (bf16[2,1,1,2,32,3456]{5,4,3,2,1,0:T(8,128)(2,1)S(1)}, bf16[2,1,1,2,32,3456]{5,4,3,2,1,0:T(8,128)(2,1)S(1)}, u32[]{:S(2)}, u32[]{:S(2)}) collective-permute-start(bf16[2,1,1,2,32,3456]{5,4,3,2,1,0:T(8,128)(2,1)S(1)} %constant_dynamic-slice_fusion.6), channel_id=1, source_target_pairs={{0,8},{4,12},{8,0},{12,4},{16,24},{20,28},{24,16},{28,20},{1,9},{5... | collective-permute-start | bytes 2654216 | tf_op jit(solution)/shard_map/ppermute | solution.py:731
  553.8 22.4 %collective-permute-start.34 = (bf16[2,1,2,1,32,3456]{5,4,3,2,1,0:T(8,128)(2,1)S(1)}, bf16[2,1,2,1,32,3456]{5,4,3,2,1,0:T(8,128)(2,1)S(1)}, u32[]{:S(2)}, u32[]{:S(2)}) collective-permute-start(bf16[2,1,2,1,32,3456]{5,4,3,2,1,0:T(8,128)(2,1)S(1)} %constant_dynamic-slice_fusion.4), channel_id=1, source_target_pairs={{0,16},{4,20},{8,24},{12,28},{16,0},{20,4},{24,8},{28,12},{1,17},{... | collective-permute-start | bytes 2654216 | tf_op jit(solution)/shard_map/ppermute | solution.py:731
  575.0 11.4 %collective-permute-start.33 = (bf16[2,1,1,1,32,3456]{5,4,3,2,1,0:T(8,128)(2,1)S(1)}, bf16[2,1,1,1,32,3456]{5,4,3,2,1,0:T(8,128)(2,1)S(1)}, u32[]{:S(2)}, u32[]{:S(2)}) collective-permute-start(bf16[2,1,1,1,32,3456]{5,4,3,2,1,0:T(8,128)(2,1)S(1)} %constant_dynamic-slice_fusion.5), channel_id=1, source_target_pairs={{0,16},{4,20},{8,24},{12,28},{16,0},{20,4},{24,8},{28,12},{1,17},{... | collective-permute-start | bytes 1327112 | tf_op jit(solution)/shard_map/ppermute | solution.py:731
  576.4 11.2 %collective-permute-start.35 = (bf16[2,1,1,1,32,3456]{5,4,3,2,1,0:T(8,128)(2,1)S(1)}, bf16[2,1,1,1,32,3456]{5,4,3,2,1,0:T(8,128)(2,1)S(1)}, u32[]{:S(2)}, u32[]{:S(2)}) collective-permute-start(bf16[2,1,1,1,32,3456]{5,4,3,2,1,0:T(8,128)(2,1)S(1)} %constant_dynamic-slice_fusion.3), channel_id=1, source_target_pairs={{0,8},{4,12},{8,0},{12,4},{16,24},{20,28},{24,16},{28,20},{1,9},{5... | collective-permute-start | bytes 1327112 | tf_op jit(solution)/shard_map/ppermute | solution.py:731
  588.0 6.8 %collective-permute-start.38 = (bf16[32,3456]{1,0:T(8,128)(2,1)S(1)}, bf16[32,3456]{1,0:T(8,128)(2,1)S(1)}, u32[]{:S(2)}, u32[]{:S(2)}) collective-permute-start(bf16[32,3456]{1,0:T(8,128)(2,1)S(1)} %get-tuple-element.154), channel_id=1, source_target_pairs={{0,3},{1,0},{2,1},{3,2},{4,7},{5,4},{6,5},{7,6},{8,11},{9,8},{10,9... | collective-permute-start | bytes 663560 | tf_op jit(solution)/shard_map/ppermute | solution.py:834
  588.6 19.1 %collective-permute-start.37 = (bf16[32,3456]{1,0:T(8,128)(2,1)S(1)}, bf16[32,3456]{1,0:T(8,128)(2,1)S(1)}, u32[]{:S(2)}, u32[]{:S(2)}) collective-permute-start(bf16[32,3456]{1,0:T(8,128)(2,1)S(1)} %get-tuple-element.153), channel_id=1, source_target_pairs={{0,2},{1,3},{2,0},{3,1},{4,6},{5,7},{6,4},{7,5},{8,10},{9,11},{10,... | collective-permute-start | bytes 663560 | tf_op jit(solution)/shard_map/ppermute | solution.py:834
  589.8 17.9 %collective-permute-start.36 = (bf16[32,3456]{1,0:T(8,128)(2,1)S(1)}, bf16[32,3456]{1,0:T(8,128)(2,1)S(1)}, u32[]{:S(2)}, u32[]{:S(2)}) collective-permute-start(bf16[32,3456]{1,0:T(8,128)(2,1)S(1)} %get-tuple-element.152), channel_id=1, source_target_pairs={{0,1},{1,2},{2,3},{3,0},{4,5},{5,6},{6,7},{7,4},{8,9},{9,10},{10,1... | collective-permute-start | bytes 663560 | tf_op jit(solution)/shard_map/ppermute | solution.py:834
  607.9 6.9 %collective-permute-start.39 = (bf16[1,1,1,16,3456]{4,3,2,1,0:T(8,128)(2,1)S(1)}, bf16[1,1,1,16,3456]{4,3,2,1,0:T(8,128)(2,1)S(1)}, u32[]{:S(2)}, u32[]{:S(2)}) collective-permute-start(bf16[1,1,1,16,3456]{4,3,2,1,0:T(8,128)(2,1)S(1)} %get-tuple-element.208), channel_id=1, source_target_pairs={{0,8},{4,12},{8,0},{12,4},{16,24},{20,28},{24,16},{28,20},{1,9},{5... | collective-permute-start | bytes 331784 | tf_op jit(solution)/shard_map/ppermute | solution.py:715
  609.2 5.6 collective-permute-start.42
  614.9 6.0 collective-permute-start.43
  616.2 6.0 collective-permute-start.40
  (117 other events, 2538.5 us)
Sparse Core Ops, SparseCore 0:
  11.5 139.6 all-gather.1

commit v3 on v2

--- a/solution.py
+++ b/solution.py
@@ -784,37 +784,51 @@
         return jnp.concatenate(self.parts, axis=0).reshape(self.shape)
 
 
+def pair_hop(part, axis, bit):
+    return lax.ppermute(side(part, axis, bit, False), "rep", places("rep", bit))
+
+
+def by_place(grad):
+    bits = rep_bits()
+    groups = lax.axis_size("shard")
+    rows, columns = grad.shape[0] // groups >> len(bits), grad.shape[1]
+    return grad.reshape((groups,) + (2,) * len(bits) + (rows, columns))
+
+
+def early_hop(grad):
+    bits = rep_bits()
+    return [pair_hop(by_place(grad), len(bits), bits[0])] if bits else []
+
+
 class Sum(Moves):
-    def __init__(self, *grads):
-        self.bits = rep_bits()
+    def __init__(self, *grads, early=()):
+        bits = rep_bits()
+        self.bits = bits[::-1]
+        self.early = early
         self.groups = lax.axis_size("shard")
-        self.rows = grads[0].shape[0] // self.groups >> len(self.bits)
+        self.rows = grads[0].shape[0] // self.groups >> len(bits)
         self.widths = [grad.shape[1] for grad in grads]
         self.columns = sum(self.widths)
-        inside = (self.groups,) + (2,) * len(self.bits) + (self.rows,)
-        self.grads = [grad.reshape(inside + (grad.shape[1],)) for grad in grads]
-        orders = list(zip(*bit_orders(self.bits)))
-        self.start(
-            [self.over_bit_0]
-            + [self.fold(bit, 1) for bit in orders[:-1]]
-            + [self.over_shard]
-            + [self.swap(bit, 0) for bit in orders]
-        )
+        self.grads = [by_place(grad) for grad in grads]
+        orders = list(zip(*bit_orders(bits)))
+        self.start([self.over_bit_0] + [self.fold(bit, 1) for bit in orders[:-1]] + [self.over_shard])
         self.advance()
 
     def over_bit_0(self):
+        axis = len(self.bits)
+
         def take(others):
             parts = self.grads
             if self.bits:
-                parts = [folded(part, other, 1, self.bits[0]) for part, other in zip(parts, others)]
+                parts = [folded(part, other, axis, self.bits[-1]) for part, other in zip(parts, others)]
             part = jnp.concatenate(parts, axis=-1)
             half = self.groups // 2
             self.parts = [part[:half], part[half:]] if half else [part]
 
         if not self.bits:
             return [], take
-        bit = self.bits[0]
-        return [lax.ppermute(side(part, 1, bit, False), "rep", places("rep", bit)) for part in self.grads], take
+        late = self.grads[len(self.early) :]
+        return list(self.early) + [pair_hop(part, axis, self.bits[-1]) for part in late], take
 
     def over_shard(self):
         part = jnp.concatenate(self.parts, axis=0).reshape(self.groups, self.rows, self.columns)
@@ -827,16 +841,17 @@
             total = of(0).astype(F32)
             for other in others:
                 total = total + other.astype(F32)
-            mine = total.astype(BF16).reshape((1,) * len(self.bits) + (self.rows, self.columns))
-            half = self.rows // 2
-            self.parts = [mine[..., :half, :], mine[..., half:, :]]
+            self.parts = [total.astype(BF16)]
 
         return [lax.ppermute(of(by), "shard", turns("shard", by)) for by in range(1, self.groups)], take
 
+    def gather(self, *deps):
+        self.finish()
+        self.whole = lax.all_gather(after(self.parts[0], *deps), "rep", axis=0, tiled=True)
+        return self.whole
+
     def result(self):
-        self.finish()
-        whole = jnp.concatenate(self.parts, axis=-2)
-        whole = whole.reshape(-1, self.columns).astype(F32)
+        whole = self.whole.astype(F32)
         ends = [sum(self.widths[: at + 1]) for at in range(len(self.widths))]
         return [whole[:, end - width : end] for end, width in zip(ends, self.widths)]
 
@@ -977,22 +992,28 @@
     )
     sum_ff.advance(d_first)
     sum_mid.advance(d_first)
+    first_part = dot_tn(first_low, d_first).astype(BF16)
+    first_hop = early_hop(first_part)
     d_main, d_kern_b, d_gain_b, d_skip_b, d_head_b = mixer_bwd(
         True, sum_ff.parts + sum_mid.parts, grad_branches[:, attw:], projected, *common, part=(handed, d_first)
     )
     sum_ff.advance(d_main)
     sum_mid.advance(d_main)
-    sum_main = Sum(dot_tn(first_low, d_main).astype(BF16))
+    second_part = dot_tn(first_low, d_main[:, inner:]).astype(BF16)
+    sum_main = Sum(first_part, second_part, early=[after(item, d_main) for item in first_hop])
+    sum_main.advance()
     grad_first = dot_nt(d_main, main_in) + dot_nt(d_attn, small_in[:, :qkv])
     grad_resid, norm_in_grad = norm_back(resid, first_scale, full_norms[0], grad_first)
     input_grad = (grad_resid + grad_hidden).astype(BF16).reshape(x_in.shape)
-    sums = (sum_ff, sum_mid, sum_main)
-    while any(item.stages for item in sums):
-        for item in sums:
-            item.advance()
+    while sum_main.stages:
+        landing = tuple(sum_main.flying)
+        sum_main.advance()
+        sum_mid.advance(*landing)
+        sum_ff.advance(*landing)
+    sum_main.gather(sum_mid.gather(sum_ff.gather()))
     ff_out_grad, ff_in_grad = sum_ff.result()
     outs_sum, attn_in_grad = sum_mid.result()
-    main_sum = sum_main.result()[0]
+    main_sum = jnp.concatenate(sum_main.result(), axis=1)
     mix_in_grad = jnp.concatenate(
         [
             main_sum[:, :half],

time: 642 us -> 628 us (0.978)
  starting transfers between devices: 77.1 us -> 60.2 us
  waiting for transfers between devices: 140 us -> 124 us
  matrix products: 142 us -> 154 us
    all_gather x0 -> x3, waiting for transfers between devices: none -> 17.5 us  [gather(): lax.all_gather(after(self.parts[0], *deps), 'rep', axis=0, tiled=True)]
    ppermute x30 -> x12, starting transfers between devices: 29.8 us -> 13.1 us  [send(): lax.ppermute(part, 'rep', places('rep', own))]
    ppermute x30 -> x12, waiting for transfers between devices: 50.5 us -> 34.2 us  [send(): lax.ppermute(part, 'rep', places('rep', own))]
    ppermute x9, waiting for transfers between devices: 39.9 us -> 28.5 us  [over_shard(): lax.ppermute(of(by), 'shard', turns('shard', by))]
    ppermute x5, waiting for transfers between devices: 13 us -> 6.27 us  [summed_small(): values = values + lax.ppermute(values, axis, places(axis, bit))]
    dot_general x5 -> x6, matrix products: 41.6 us -> 47.4 us  [dot_tn(): lax.dot_general(left, right, (((0,), (0,)), ((), ())), preferred_element_...]
    convert_element_type x17 -> x18, other arithmetic: 31.2 us -> 35.5 us  [folded(): (side(part, axis, bit, True).astype(F32) + other.astype(F32)).astype(BF16)]
    unnamed x233 -> x277, local copies, waits for them, and re-layouts: 34.1 us -> 32.7 us
  transfers between devices with their start and end apart: 68 -> 54, of which waited for: 24 -> 15; matrix products, arithmetic and copies ran while one was open for 27% -> 37% of each run, Pallas kernels for 17% -> 18%
where the time goes in v3:
time: 628 us; the launch traced here: 622 us
  matrix products  154 us (25%)
  waiting for transfers between devices  124 us (20%)
  Pallas kernels  109 us (17%)
  local copies, waits for them, and re-layouts  84 us (13%)
  other arithmetic  74.2 us (12%)
  starting transfers between devices  60.2 us (10%)
  between operations  16.3 us (3%)
    pallas_call x2, Pallas kernels, mixer_bwd(): pl.pallas_call(partial(mixer_bwd_kernel, inner, second, len(deps)), grid=...  57.7 us
    dot_general x5, matrix products, dot_nt(): lax.dot_general(left, right, (((1,), (1,)), ((), ())), preferred_element_...  54.5 us
    dot_general x6, matrix products, dot_nn(): lax.dot_general(left, right, (((1,), (0,)), ((), ())), precision=precisio...  52.5 us
    dot_general x6, matrix products, dot_tn(): lax.dot_general(left, right, (((0,), (0,)), ((), ())), preferred_element_...  47.4 us
    convert_element_type x18, other arithmetic, folded(): (side(part, axis, bit, True).astype(F32) + other.astype(F32)).astype(BF16)  35.5 us
    ppermute x12, waiting for transfers between devices, send(): lax.ppermute(part, 'rep', places('rep', own))  34.2 us
    ppermute x12, waiting for transfers between devices, send(): lax.ppermute(side(part, place + self.bits.index(own), own, False), 'rep',...  34.1 us
    unnamed x277, local copies, waits for them, and re-layouts  32.7 us
  transfers between devices with their start and end apart: 54, of which 15 were waited for; matrix products, arithmetic and copies ran while one was open for 37% of the time, Pallas kernels for 18%

profile of v3, /device:TPU:0, one launch (start us, length us, event | category | flops | bytes accessed | tf_op | source)
XLA Modules:
  0.0 622.1 jit_solution(15951676695292338714)
XLA Ops:
  7.3 2.0 fusion.57
  11.1 3.0 collective-permute-start
  14.1 2.6 collective-permute-start.1
  23.5 2.2 fusion.13
  31.9 3.3 collective-permute-start.11
  50.2 2.9 collective-permute-done.10
  57.0 17.5 %collective-permute-done.12 = bf16[2,1,1,1,32,3456]{5,4,3,2,1,0:T(8,128)(2,1)S(1)} collective-permute-done((bf16[2,1,1,1,32,3456]{5,4,3,2,1,0:T(8,128)(2,1)S(1)}, bf16[2,1,1,1,32,3456]{5,4,3,2,1,0:T(8,128)(2,1)S(1)}, u32[]{:S(2)}, u32[]{:S(2)}) %collective-permute-start.12) | collective-permute-done | bytes 442400 | tf_op jit(solution)/shard_map/ppermute | solution.py:715
  74.7 2.2 collective-permute-start.16
  81.0 3.5 fusion.45.proj_ref
  84.5 14.4 %collective-permute-done.16 = bf16[2,1,1,2,32,3456]{5,4,3,2,1,0:T(8,128)(2,1)S(1)} collective-permute-done((bf16[2,1,1,2,32,3456]{5,4,3,2,1,0:T(8,128)(2,1)S(1)}, bf16[2,1,1,2,32,3456]{5,4,3,2,1,0:T(8,128)(2,1)S(1)}, u32[]{:S(2)}, u32[]{:S(2)}) %collective-permute-start.16) | collective-permute-done | bytes 884768 | tf_op jit(solution)/shard_map/ppermute | solution.py:715
  101.5 11.8 %attention_fwd.1 = (bf16[1024,512]{1,0:T(8,128)(2,1)S(1)}, bf16[1024,128]{1,0:T(8,128)(2,1)S(1)}, bf16[1024,128]{1,0:T(8,128)(2,1)S(1)}, bf16[1024,512]{1,0:T(8,128)(2,1)S(1)}, f32[8,1024]{1,0:T(8,128)S(1)}) custom-call(f32[1024,768]{1,0:T(8,128)} %fusion.45.proj_ref, f32[1024,128]{1,0:T(8,128)S(1)} %get-tuple-element.186.cos_ref.refs_7_, ...), custom_call_target="tpu_custom_call" | custom-call | flops 30000001024 | bytes 8388608 | tf_op jit(solution)/shard_map/attention_fwd/pallas_call | solution.py:122
  118.5 9.4 %convolution_convert_fusion.1.proj_ref.refs_3_.refs_4_.refs_5_.refs_6_ = bf16[1024,3328]{1,0:T(8,128)(2,1)} fusion(bf16[1024,3456]{1,0:T(8,128)(2,1)S(1)} %bitcast.138, bf16[1,1024,1024]{2,1,0:T(8,128)(2,1)S(1)} %copy-done.69, f32[1024]{0:T(1024)S(1)} %get-tuple-element.123, f32[1024]{0:T(1024)S(1)} %add_rsqrt_fusion.1), kind=kOutput, calls=%fused_computation.16 | convolution fusion | flops 6986924032 | bytes 15736832 | tf_op jit(solution)/shard_map/dot_general | solution.py:27
  127.9 19.2 %mixer_fwd.1 = (f32[1024,1536]{1,0:T(8,128)}, bf16[8,128,1536]{2,1,0:T(8,128)(2,1)S(1)}, bf16[1024,1536]{1,0:T(8,128)(2,1)}) custom-call(bf16[1024,3328]{1,0:T(8,128)(2,1)} %convolution_convert_fusion.1.proj_ref.refs_3_.refs_4_.refs_5_.refs_6_, f32[1024,128]{1,0:T(8,128)S(1)} %fusion.74.step_ref.refs_5_.refs_7_, ...), custom_call_target="tpu_custom_call" | custom-call | flops 30000001024 | bytes 20971520 | tf_op jit(solution)/shard_map/mixer_fwd/pallas_call | solution.py:365
  148.9 4.0 constant_dynamic-update-slice_fusion
  152.9 8.7 %multiply_reduce_fusion.2 = (f32[1024]{0:T(1024)S(1)}, f32[1024,1024]{1,0:T(8,128)S(1)}) fusion(bf16[1024,2048]{1,0:T(8,128)(2,1)} %constant_dynamic-update-slice_fusion, bf16[1024,8192]{1,0:T(8,128)(2,1)} %all-gather.5.cloned.1.call-done, bf16[1,1024,1024]{2,1,0:T(8,128)(2,1)} %param.17), kind=kOutput, calls=%fused_computation.45 | convolution fusion | flops 4299160576 | bytes 14684160 | tf_op jit(solution)/shard_map/dot_general | solution.py:33
  161.7 16.9 %fusion.6 = f32[1024,4096]{1,0:T(8,128)} fusion(bf16[1024,8192]{1,0:T(8,128)(2,1)} %all-gather.5.cloned.1.call-done, f32[1024,1024]{1,0:T(8,128)S(1)} %get-tuple-element.201, f32[1024]{0:T(1024)S(1)} %get-tuple-element.122, f32[1024]{0:T(1024)S(1)} %add_rsqrt_fusion), kind=kOutput, calls=%fused_computation.19 | convolution fusion | flops 8593080320 | bytes 29368320 | tf_op jit(solution)/shard_map/dot_general | solution.py:27
  178.6 14.3 %fusion.1 = (bf16[1024,2048]{1,0:T(8,128)(2,1)}, bf16[1024,2048]{1,0:T(8,128)(2,1)}, bf16[1024,2048]{1,0:T(8,128)(2,1)}) fusion(f32[1024,4096]{1,0:T(8,128)} %fusion.6, bf16[1024,8192]{1,0:T(8,128)(2,1)} %all-gather.5.cloned.1.call-done, bf16[1,1024,1024]{2,1,0:T(8,128)(2,1)S(1)} %copy-done.67), kind=kOutput, calls=%fused_computation.4 | convolution fusion | flops 4324327424 | bytes 35651584 | tf_op jit(solution)/shard_map/dot_general | solution.py:27
  192.9 7.0 %convolution_convert_fusion.5 = bf16[2048,1024]{0,1:T(8,128)(2,1)S(1)} fusion(bf16[1024,2048]{1,0:T(8,128)(2,1)} %get-tuple-element.128, bf16[1,1024,1024]{2,1,0:T(8,128)(2,1)S(1)} %copy-done.67), kind=kOutput, calls=%fused_computation.53 | convolution fusion | flops 4297064448 | bytes 10485760 | tf_op jit(solution)/shard_map/dot_general | solution.py:37
  201.5 15.5 %convolution_convert_fusion = bf16[1024,4096]{1,0:T(8,128)(2,1)} fusion(bf16[1024,2048]{1,0:T(8,128)(2,1)} %get-tuple-element.127, bf16[1024,2048]{1,0:T(8,128)(2,1)} %get-tuple-element.126, f32[1024,1024]{1,0:T(8,128)S(1)} %get-tuple-element.201, f32[1024]{0:T(1024)S(1)} %get-tuple-element.122, f32[1024]{0:T(1024)S(1)} %add_rsqrt_fusion), kind=kOutput, calls=%fused_computation.15 | convolution fusion | flops 8614051840 | bytes 20979712 | tf_op jit(solution)/shard_map/dot_general | solution.py:37
  217.0 4.7 constant_dynamic-slice_fusion.13
  221.9 16.1 %multiply_reduce_fusion = (f32[1024]{0:T(1024)}, f32[1024]{0:T(1024)S(1)}, f32[1024,1024]{1,0:T(8,128)}) fusion(f32[1024,1024]{1,0:T(8,128)S(1)} %get-tuple-element.201, f32[1024]{0:T(1024)S(1)} %add_rsqrt_fusion, f32[1024]{0:T(1024)S(1)} %get-tuple-element.122, bf16[1024,8192]{1,0:T(8,128)(2,1)} %all-gather.5.cloned.1.call-done, ...), kind=kOutput, calls=%fused_computation.38 | convolution fusion | flops 8613001216 | bytes 25182208 | tf_op jit(solution)/shard_map/dot_general | solution.py:33
  238.1 3.5 fusion.118.refs_1_
  241.6 7.7 %convolution_convert_fusion.4 = bf16[1024,2048]{1,0:T(8,128)(2,1)S(1)} fusion(bf16[1024,1024]{1,0:T(8,128)(2,1)S(1)} %fusion.118.refs_1_, bf16[1024,8192]{1,0:T(8,128)(2,1)} %all-gather.5.cloned.1.call-done), kind=kOutput, calls=%fused_computation.52 | convolution fusion | flops 4297064448 | bytes 10485760 | tf_op jit(solution)/shard_map/dot_general | solution.py:27
  249.4 2.1 slice.268.refs_2_.refs_4_
  251.5 7.0 %convolution_convert_fusion.3 = bf16[1024,2048]{1,0:T(8,128)(2,1)S(1)} fusion(bf16[1024,1024]{1,0:T(8,128)(2,1)S(1)} %fusion.118.refs_1_, bf16[1024,2048]{1,0:T(8,128)(2,1)} %constant_dynamic-update-slice_fusion), kind=kOutput, calls=%fused_computation.51 | convolution fusion | flops 4297064448 | bytes 10485760 | tf_op jit(solution)/shard_map/dot_general | solution.py:37
  262.3 4.4 add_convert_fusion.2
  266.7 5.1 add_convert_fusion
  271.9 2.5 pad_maximum_fusion.4
  274.6 2.3 collective-permute-start.20
  279.8 20.6 %attention_bwd.1.refs_1_ = bf16[1024,768]{1,0:T(8,128)(2,1)S(1)} custom-call(bf16[2,2,2,1,32,6144]{5,4,3,2,1,0:T(8,128)(2,1)} %copy-done.64, bf16[2,2,2,1,32,6144]{5,4,3,2,1,0:T(8,128)(2,1)} %get-tuple-element.129.refs_1_, bf16[1024,512]{1,0:T(8,128)(2,1)S(1)} %copy-done.44, bf16[1024,128]{1,0:T(8,128)(2,1)S(1)} %copy-done.46, ...), custom_call_target="tpu_custom_call" | custom-call | flops 49999998976 | bytes 8388608 | tf_op jit(solution)/shard_map/attention_bwd/pallas_call | solution.py:209
  300.4 2.2 convolution_convert_fusion.6
  303.7 3.8 fusion.43
  307.5 4.3 collective-permute-done.20.refs_0_
  311.8 2.2 add_convert_fusion.7.refs_0_
  316.6 2.3 add_convert_fusion.6.refs_1_
  321.8 29.7 %mixer_bwd_first.1 = (bf16[1024,1536]{1,0:T(8,128)(2,1)}, f32[8,768]{1,0:T(8,128)S(1)}, f32[8,768]{1,0:T(8,128)S(1)}, f32[8,768]{1,0:T(8,128)S(1)}, f32[8,128]{1,0:T(8,128)S(1)}, /*index=5*/f32[1024,640]{1,0:T(8,128)}) custom-call(bf16[2,2,1,1,32,6144]{5,4,3,2,1,0:T(8,128)(2,1)S(1)} %add_convert_fusion.7.refs_0_, ...), custom_call_target="tpu_custom_call" | custom-call | flops 30000001024 | bytes 20971520 | tf_op jit(solution)/shard_map/mixer_bwd_first/pallas_call | solution.py:593
  354.4 8.1 %convolution_convert_fusion.2 = bf16[1024,1536]{1,0:T(8,128)(2,1)} fusion(bf16[1024,1536]{1,0:T(8,128)(2,1)} %get-tuple-element.43.refs_1_.refs_21_, bf16[1,1024,1024]{2,1,0:T(8,128)(2,1)} %param.17, f32[1024]{0:T(1024)S(1)} %copy-done.117, f32[1024]{0:T(1024)S(1)} %copy-done.122), kind=kOutput, calls=%fused_computation.49 | convolution fusion | flops 3226992640 | bytes 8396800 | tf_op jit(solution)/shard_map/dot_general | solution.py:37
  362.5 3.3 add_convert_fusion.1
  384.9 28.0 %mixer_bwd_second.1 = (bf16[1024,3456]{1,0:T(8,128)(2,1)}, f32[8,1024]{1,0:T(8,128)S(1)}, f32[8,768]{1,0:T(8,128)S(1)}, f32[8,768]{1,0:T(8,128)S(1)}, f32[8,128]{1,0:T(8,128)S(1)}) custom-call(bf16[2,1,1,1,32,6144]{5,4,3,2,1,0:T(8,128)(2,1)S(1)} %add_convert_fusion.12.refs_0_, bf16[2,1,1,1,32,6144]{5,4,3,2,1,0:T(8,128)(2,1)S(1)} %add_convert_fusion.11.refs_1_, ...), custom_call_target="tpu_custom_call" | custom-call | flops 30000001024 | bytes 20971520 | tf_op jit(solution)/shard_map/mixer_bwd_second/pallas_call | solution.py:593
  413.0 7.6 %fusion.20 = bf16[1024,1920]{1,0:T(8,128)(2,1)S(1)} fusion(bf16[1024,3456]{1,0:T(8,128)(2,1)} %get-tuple-element.45.refs_1_, bf16[1,1024,1024]{2,1,0:T(8,128)(2,1)S(1)} %copy-done.71, f32[1024]{0:T(1024)S(1)} %copy-done.118, f32[1024]{0:T(1024)S(1)} %copy-done.123), kind=kOutput, calls=%fused_computation.50 | convolution fusion | flops 4032692224 | bytes 9969664 | tf_op jit(solution)/shard_map/dot_general | solution.py:37
  425.3 2.1 add_convert_fusion.15
  428.7 5.8 collective-permute-start.49
  434.5 3.5 collective-permute-start.48
  442.4 3.9 collective-permute-done.49.refs_0_
  448.0 24.6 %collective-permute-done.48.refs_0_ = bf16[32,6144]{1,0:T(8,128)(2,1)S(1)} collective-permute-done((bf16[32,6144]{1,0:T(8,128)(2,1)}, bf16[32,6144]{1,0:T(8,128)(2,1)S(1)}, u32[]{:S(2)}, u32[]{:S(2)}) %collective-permute-start.48) | collective-permute-done | bytes 393248 | tf_op jit(solution)/shard_map/ppermute | solution.py:846
  474.2 2.5 add_convert_fusion.5
  477.2 2.1 add_convert_fusion.4
  482.1 2.1 fusion.51
  487.5 18.7 %collective-permute-done.33.refs_1_ = bf16[2,2,1,1,32,3456]{5,4,3,2,1,0:T(8,128)(2,1)S(1)} collective-permute-done((bf16[2,2,1,1,32,3456]{5,4,3,2,1,0:T(8,128)(2,1)}, bf16[2,2,1,1,32,3456]{5,4,3,2,1,0:T(8,128)(2,1)S(1)}, u32[]{:S(2)}, u32[]{:S(2)}) %collective-permute-start.33) | collective-permute-done | bytes 884768 | tf_op jit(solution)/shard_map/ppermute | solution.py:731
  510.4 6.0 collective-permute-done.35.refs_2_
  521.3 2.0 collective-permute-start.44
  523.3 5.0 collective-permute-done.34.refs_1_
  531.5 2.0 collective-permute-start.37
  534.2 2.1 fusion.73.refs_0_
  536.4 15.0 %fusion.12 = (f32[1024]{0:T(1024)S(1)}, f32[1024]{0:T(1024)S(1)}, f32[1024,1024]{1,0:T(8,128)}) fusion(bf16[1,1024,1024]{2,1,0:T(8,128)(2,1)S(1)} %copy-done.72, f32[1024]{0:T(1024)S(1)} %copy-done.124, f32[1024]{0:T(1024)S(1)} %copy-done.119, f32[1024,1024]{1,0:T(8,128)} %fusion.43, bf16[1024,3456]{1,0:T(8,128)(2,1)} %get-tuple-element.45.refs_1_, ...), kind=kOutput, calls=%fused_computation.28 | convolution fusion | flops 7256143872 | bytes 24657920 | tf_op jit(solution)/shard_map/dot_general | solution.py:33
  551.4 2.0 fusion.62.refs_0_
  553.5 17.5 %all-gather.9.cloned.1.call-done.refs_1_ = bf16[256,2816]{1,0:T(8,128)(2,1)} async-done(((bf16[32,2816]{1,0:T(8,128)(2,1)}), bf16[256,2816]{1,0:T(8,128)(2,1)}) %all-gather.9.cloned.1.call-update) | async-done | bytes 1441808 | tf_op jit(solution)/shard_map/all_gather | solution.py:850
  574.3 2.7 collective-permute-done.27
  578.5 10.9 %fusion.31 = bf16[1,1024,1024]{2,1,0:T(8,128)(2,1)} fusion(f32[1024,1024]{1,0:T(8,128)} %copy-done.60, bf16[1024,2048]{1,0:T(8,128)(2,1)} %get-tuple-element.128, bf16[1024,8192]{1,0:T(8,128)(2,1)} %all-gather.5.cloned.1.call-done), kind=kOutput, calls=%fused_computation.81 | convolution fusion | flops 4297064448 | bytes 14680064 | tf_op jit(solution)/shard_map/dot_general | solution.py:33
  591.0 2.6 collective-permute-done.29
  593.6 2.5 collective-permute-start.30
  596.2 3.0 fusion.32
  603.0 2.5 slice.284
  612.5 2.9 copy.138
  (527 shorter events, 133.7 us)
Async XLA Ops:
  7.2 145.7 %all-gather.5.cloned.1.call-start = ((), (), s32[]{:S(2)}) async-start(), calls=%async_computation | async-start | bytes 17301504 | tf_op jit(solution)/shard_map/all_gather | solution.py:863
  9.3 526.9 %all-gather.7.cloned.1.call-start = ((), (), s32[]{:S(2)}) async-start(), calls=%async_computation.1 | async-start | bytes 3538944 | tf_op jit(solution)/shard_map/all_gather | solution.py:850
  11.1 19.8 %collective-permute-start = (bf16[32,896]{1,0:T(8,128)(2,1)}, bf16[32,896]{1,0:T(8,128)(2,1)}, u32[]{:S(2)}, u32[]{:S(2)}) collective-permute-start(bf16[32,896]{1,0:T(8,128)(2,1)} %get-tuple-element.125), channel_id=1, source_target_pairs={{0,1},{1,2},{2,3},{3,0},{4,5},{5,6},{6,7},{7,4},{8,9},{9,10},{10,1... | collective-permute-start | bytes 172040 | tf_op jit(solution)/shard_map/ppermute | solution.py:780
  14.1 16.7 %collective-permute-start.1 = (bf16[32,896]{1,0:T(8,128)(2,1)}, bf16[32,896]{1,0:T(8,128)(2,1)}, u32[]{:S(2)}, u32[]{:S(2)}) collective-permute-start(bf16[32,896]{1,0:T(8,128)(2,1)} %get-tuple-element.125), channel_id=1, source_target_pairs={{0,2},{1,3},{2,0},{3,1},{4,6},{5,7},{6,4},{7,5},{8,10},{9,11},{10,... | collective-permute-start | bytes 172040 | tf_op jit(solution)/shard_map/ppermute | solution.py:780
  16.7 14.2 %collective-permute-start.2 = (bf16[32,896]{1,0:T(8,128)(2,1)}, bf16[32,896]{1,0:T(8,128)(2,1)}, u32[]{:S(2)}, u32[]{:S(2)}) collective-permute-start(bf16[32,896]{1,0:T(8,128)(2,1)} %get-tuple-element.125), channel_id=1, source_target_pairs={{0,3},{1,0},{2,1},{3,2},{4,7},{5,4},{6,5},{7,6},{8,11},{9,8},{10,9... | collective-permute-start | bytes 172040 | tf_op jit(solution)/shard_map/ppermute | solution.py:780
  23.2 104.7 %copy-start.35 = (f32[8,1,128]{2,1,0:T(1,128)}, f32[8,1,128]{2,1,0:T(1,128)S(1)}, u32[]{:S(2)}) copy-start(f32[8,1,128]{2,1,0:T(1,128)S(1)} %get-tuple-element.189.row_ref.refs_7_.refs_9_) | copy-start | bytes 12292
  23.4 104.4 %copy-start.21 = (f32[8,1536]{1,0:T(8,128)}, f32[8,1536]{1,0:T(8,128)S(1)}, u32[]{:S(2)}) copy-start(f32[8,1536]{1,0:T(8,128)S(1)} %pad_convert_fusion.2.gain_ref.refs_15_.refs_17_) | copy-start | bytes 147460
  23.5 104.4 %copy-start.15 = (f32[8,1792]{1,0:T(8,128)}, f32[8,1792]{1,0:T(8,128)S(1)}, u32[]{:S(2)}) copy-start(f32[8,1792]{1,0:T(8,128)S(1)} %get-tuple-element.206.bias_ref.refs_11_.refs_13_) | copy-start | bytes 172036
  23.5 104.4 %copy-start.18 = (f32[8,1792]{1,0:T(8,128)}, f32[8,1792]{1,0:T(8,128)S(1)}, u32[]{:S(2)}) copy-start(f32[8,1792]{1,0:T(8,128)S(1)} %get-tuple-element.207.kern_ref.refs_10_.refs_12_) | copy-start | bytes 172036
  25.9 102.0 %copy-start.6 = (bf16[256,1536]{1,0:T(8,128)(2,1)}, bf16[256,1536]{1,0:T(8,128)(2,1)S(1)}, u32[]{:S(2)}) copy-start(bf16[256,1536]{1,0:T(8,128)(2,1)S(1)} %add_convert_fusion.13.expand_ref.refs_16_.refs_18_) | copy-start | bytes 2359300
  30.5 291.3 %copy-start.13 = (f32[1024,128]{1,0:T(8,128)}, f32[1024,128]{1,0:T(8,128)S(1)}, u32[]{:S(2)}) copy-start(f32[1024,128]{1,0:T(8,128)S(1)} %pad.67.idc_ref.marks_ref.refs_9_.refs_6_.refs_8_) | copy-start | bytes 1572868
  30.5 97.4 %copy-start.31 = (f32[8,128]{1,0:T(8,128)}, f32[8,128]{1,0:T(8,128)S(1)}, u32[]{:S(2)}) copy-start(f32[8,128]{1,0:T(8,128)S(1)} %pad.72.rate_ref.refs_12_.refs_14_) | copy-start | bytes 12292
  30.6 97.3 %copy-start.33 = (f32[8,128]{1,0:T(8,128)}, f32[8,128]{1,0:T(8,128)S(1)}, u32[]{:S(2)}) copy-start(f32[8,128]{1,0:T(8,128)S(1)} %pad.73.dtb_ref.refs_13_.refs_15_) | copy-start | bytes 12292
  30.8 97.2 %copy-start.24 = (f32[8,1536]{1,0:T(8,128)}, f32[8,1536]{1,0:T(8,128)S(1)}, u32[]{:S(2)}) copy-start(f32[8,1536]{1,0:T(8,128)S(1)} %pad.74.skip_ref.refs_14_.refs_16_) | copy-start | bytes 147460
  30.9 19.3 %collective-permute-start.9 = (bf16[32,3456]{1,0:T(8,128)(2,1)}, bf16[32,3456]{1,0:T(8,128)(2,1)S(1)}, u32[]{:S(2)}, u32[]{:S(2)}) collective-permute-start(bf16[32,3456]{1,0:T(8,128)(2,1)} %after.22), channel_id=1, source_target_pairs={{0,1},{1,2},{2,3},{3,0},{4,5},{5,6},{6,7},{7,4},{8,9},{9,10},{10,1... | collective-permute-start | bytes 663560 | tf_op jit(solution)/shard_map/ppermute | solution.py:780
  31.6 21.5 %collective-permute-start.10 = (bf16[32,3456]{1,0:T(8,128)(2,1)}, bf16[32,3456]{1,0:T(8,128)(2,1)S(1)}, u32[]{:S(2)}, u32[]{:S(2)}) collective-permute-start(bf16[32,3456]{1,0:T(8,128)(2,1)} %after.22), channel_id=1, source_target_pairs={{0,2},{1,3},{2,0},{3,1},{4,6},{5,7},{6,4},{7,5},{8,10},{9,11},{10,... | collective-permute-start | bytes 663560 | tf_op jit(solution)/shard_map/ppermute | solution.py:780
  31.9 21.2 %collective-permute-start.11 = (bf16[32,3456]{1,0:T(8,128)(2,1)}, bf16[32,3456]{1,0:T(8,128)(2,1)S(1)}, u32[]{:S(2)}, u32[]{:S(2)}) collective-permute-start(bf16[32,3456]{1,0:T(8,128)(2,1)} %after.22), channel_id=1, source_target_pairs={{0,3},{1,0},{2,1},{3,2},{4,7},{5,4},{6,5},{7,6},{8,11},{9,8},{10,9... | collective-permute-start | bytes 663560 | tf_op jit(solution)/shard_map/ppermute | solution.py:780
  40.5 4.9 collective-permute-start.3
  42.1 4.8 collective-permute-start.6
  48.0 8.2 %collective-permute-start.7 = (bf16[2,1,1,2,32,896]{5,4,3,2,1,0:T(8,128)(2,1)S(1)}, bf16[2,1,1,2,32,896]{5,4,3,2,1,0:T(8,128)(2,1)S(1)}, u32[]{:S(2)}, u32[]{:S(2)}) collective-permute-start(bf16[2,1,1,2,32,896]{5,4,3,2,1,0:T(8,128)(2,1)S(1)} %pad_maximum_fusion.13), channel_id=1, source_target_pairs={{0,8},{4,12},{8,0},{12,4},{16,24},{20,28},{24,16},{28,20},{1,9},{5... | collective-permute-start | bytes 688136 | tf_op jit(solution)/shard_map/ppermute | solution.py:715
  48.5 7.8 %collective-permute-start.4 = (bf16[2,1,2,1,32,896]{5,4,3,2,1,0:T(8,128)(2,1)S(1)}, bf16[2,1,2,1,32,896]{5,4,3,2,1,0:T(8,128)(2,1)S(1)}, u32[]{:S(2)}, u32[]{:S(2)}) collective-permute-start(bf16[2,1,2,1,32,896]{5,4,3,2,1,0:T(8,128)(2,1)S(1)} %pad_maximum_fusion.12), channel_id=1, source_target_pairs={{0,16},{4,20},{8,24},{12,28},{16,0},{20,4},{24,8},{28,12},{1,17},{... | collective-permute-start | bytes 688136 | tf_op jit(solution)/shard_map/ppermute | solution.py:715
  53.2 21.2 %collective-permute-start.12 = (bf16[2,1,1,1,32,3456]{5,4,3,2,1,0:T(8,128)(2,1)S(1)}, bf16[2,1,1,1,32,3456]{5,4,3,2,1,0:T(8,128)(2,1)S(1)}, u32[]{:S(2)}, u32[]{:S(2)}) collective-permute-start(bf16[2,1,1,1,32,3456]{5,4,3,2,1,0:T(8,128)(2,1)S(1)} %get-tuple-element.163), channel_id=1, source_target_pairs={{0,8},{4,12},{8,0},{12,4},{16,24},{20,28},{24,16},{28,20},{1,9},{5... | collective-permute-start | bytes 1327112 | tf_op jit(solution)/shard_map/ppermute | solution.py:715
  54.7 19.7 %collective-permute-start.15 = (bf16[2,1,1,1,32,3456]{5,4,3,2,1,0:T(8,128)(2,1)S(1)}, bf16[2,1,1,1,32,3456]{5,4,3,2,1,0:T(8,128)(2,1)S(1)}, u32[]{:S(2)}, u32[]{:S(2)}) collective-permute-start(bf16[2,1,1,1,32,3456]{5,4,3,2,1,0:T(8,128)(2,1)S(1)} %get-tuple-element.164), channel_id=1, source_target_pairs={{0,16},{4,20},{8,24},{12,28},{16,0},{20,4},{24,8},{28,12},{1,17},{... | collective-permute-start | bytes 1327112 | tf_op jit(solution)/shard_map/ppermute | solution.py:715
  56.2 22.2 %collective-permute-start.8 = (bf16[2,1,2,2,32,896]{5,4,3,2,1,0:T(8,128)(2,1)S(1)}, bf16[2,1,2,2,32,896]{5,4,3,2,1,0:T(8,128)(2,1)S(1)}, u32[]{:S(2)}, u32[]{:S(2)}) collective-permute-start(bf16[2,1,2,2,32,896]{5,4,3,2,1,0:T(8,128)(2,1)S(1)} %pad_maximum_fusion.11), channel_id=1, source_target_pairs={{0,4},{4,0},{8,12},{12,8},{16,20},{20,16},{24,28},{28,24},{1,5},{5... | collective-permute-start | bytes 1376264 | tf_op jit(solution)/shard_map/ppermute | solution.py:715
  56.4 22.1 %collective-permute-start.5 = (bf16[2,1,2,2,32,896]{5,4,3,2,1,0:T(8,128)(2,1)S(1)}, bf16[2,1,2,2,32,896]{5,4,3,2,1,0:T(8,128)(2,1)S(1)}, u32[]{:S(2)}, u32[]{:S(2)}) collective-permute-start(bf16[2,1,2,2,32,896]{5,4,3,2,1,0:T(8,128)(2,1)S(1)} %pad_maximum_fusion.10), channel_id=1, source_target_pairs={{0,4},{4,0},{8,12},{12,8},{16,20},{20,16},{24,28},{28,24},{1,5},{5... | collective-permute-start | bytes 1376264 | tf_op jit(solution)/shard_map/ppermute | solution.py:715
  74.7 24.2 %collective-permute-start.16 = (bf16[2,1,1,2,32,3456]{5,4,3,2,1,0:T(8,128)(2,1)S(1)}, bf16[2,1,1,2,32,3456]{5,4,3,2,1,0:T(8,128)(2,1)S(1)}, u32[]{:S(2)}, u32[]{:S(2)}) collective-permute-start(bf16[2,1,1,2,32,3456]{5,4,3,2,1,0:T(8,128)(2,1)S(1)} %pad_maximum_fusion.9), channel_id=1, source_target_pairs={{0,8},{4,12},{8,0},{12,4},{16,24},{20,28},{24,16},{28,20},{1,9},{5... | collective-permute-start | bytes 2654216 | tf_op jit(solution)/shard_map/ppermute | solution.py:715
  77.1 22.3 %collective-permute-start.13 = (bf16[2,1,2,1,32,3456]{5,4,3,2,1,0:T(8,128)(2,1)S(1)}, bf16[2,1,2,1,32,3456]{5,4,3,2,1,0:T(8,128)(2,1)S(1)}, u32[]{:S(2)}, u32[]{:S(2)}) collective-permute-start(bf16[2,1,2,1,32,3456]{5,4,3,2,1,0:T(8,128)(2,1)S(1)} %pad_maximum_fusion.8), channel_id=1, source_target_pairs={{0,16},{4,20},{8,24},{12,28},{16,0},{20,4},{24,8},{28,12},{1,17},{... | collective-permute-start | bytes 2654216 | tf_op jit(solution)/shard_map/ppermute | solution.py:715
  79.5 158.5 %copy-start.107 = (f32[1024]{0:T(1024)}, f32[1024]{0:T(1024)S(1)}, u32[]{:S(2)}) copy-start(f32[1024]{0:T(1024)S(1)} %get-tuple-element.122) | copy-start | bytes 12292
  99.3 15.1 %collective-permute-start.17 = (bf16[2,1,2,2,32,3456]{5,4,3,2,1,0:T(8,128)(2,1)S(1)}, bf16[2,1,2,2,32,3456]{5,4,3,2,1,0:T(8,128)(2,1)S(1)}, u32[]{:S(2)}, u32[]{:S(2)}) collective-permute-start(bf16[2,1,2,2,32,3456]{5,4,3,2,1,0:T(8,128)(2,1)S(1)} %pad_maximum_fusion.6), channel_id=1, source_target_pairs={{0,4},{4,0},{8,12},{12,8},{16,20},{20,16},{24,28},{28,24},{1,5},{5... | collective-permute-start | bytes 5308424 | tf_op jit(solution)/shard_map/ppermute | solution.py:715
  101.0 13.9 %collective-permute-start.14 = (bf16[2,1,2,2,32,3456]{5,4,3,2,1,0:T(8,128)(2,1)}, bf16[2,1,2,2,32,3456]{5,4,3,2,1,0:T(8,128)(2,1)}, u32[]{:S(2)}, u32[]{:S(2)}) collective-permute-start(bf16[2,1,2,2,32,3456]{5,4,3,2,1,0:T(8,128)(2,1)} %pad_maximum_fusion.5), channel_id=1, source_target_pairs={{0,4},{4,0},{8,12},{12,8},{16,20},{20,16},{24,28},{28,24},{1,5},{5... | collective-permute-start | bytes 5308424 | tf_op jit(solution)/shard_map/ppermute | solution.py:715
  201.5 60.8 %collective-permute-start.18 = (bf16[4,2,2,1,32,2048]{5,4,3,2,1,0:T(8,128)(2,1)}, bf16[4,2,2,1,32,2048]{5,4,3,2,1,0:T(8,128)(2,1)}, u32[]{:S(2)}, u32[]{:S(2)}) collective-permute-start(bf16[4,2,2,1,32,2048]{5,4,3,2,1,0:T(8,128)(2,1)} %constant_dynamic-slice_fusion.14), channel_id=1, source_target_pairs={{0,4},{4,0},{8,12},{12,8},{16,20},{20,16},{24,28},{28,24},{1,5},{5... | collective-permute-start | bytes 6291464 | tf_op jit(solution)/shard_map/ppermute | solution.py:788
  221.7 45.0 %collective-permute-start.19 = (bf16[4,2,2,1,32,4096]{5,4,3,2,1,0:T(8,128)(2,1)}, bf16[4,2,2,1,32,4096]{5,4,3,2,1,0:T(8,128)(2,1)}, u32[]{:S(2)}, u32[]{:S(2)}) collective-permute-start(bf16[4,2,2,1,32,4096]{5,4,3,2,1,0:T(8,128)(2,1)} %constant_dynamic-slice_fusion.13), channel_id=1, source_target_pairs={{0,4},{4,0},{8,12},{12,8},{16,20},{20,16},{24,28},{28,24},{1,5},{5... | collective-permute-start | bytes 12582920 | tf_op jit(solution)/shard_map/ppermute | solution.py:788
  262.0 100.6 %collective-permute-start.24 = (bf16[4,2,2,1,32,2048]{5,4,3,2,1,0:T(8,128)(2,1)}, bf16[4,2,2,1,32,2048]{5,4,3,2,1,0:T(8,128)(2,1)}, u32[]{:S(2)}, u32[]{:S(2)}) collective-permute-start(bf16[4,2,2,1,32,2048]{5,4,3,2,1,0:T(8,128)(2,1)} %constant_dynamic-slice_fusion.9), channel_id=1, source_target_pairs={{0,4},{4,0},{8,12},{12,8},{16,20},{20,16},{24,28},{28,24},{1,5},{5... | collective-permute-start | bytes 6291464 | tf_op jit(solution)/shard_map/ppermute | solution.py:788
  274.6 37.2 %collective-permute-start.20 = (bf16[2,2,1,1,32,6144]{5,4,3,2,1,0:T(8,128)(2,1)S(1)}, bf16[2,2,1,1,32,6144]{5,4,3,2,1,0:T(8,128)(2,1)}, u32[]{:S(2)}, u32[]{:S(2)}) collective-permute-start(bf16[2,2,1,1,32,6144]{5,4,3,2,1,0:T(8,128)(2,1)S(1)} %constant_dynamic-slice_fusion.12), channel_id=1, source_target_pairs={{0,8},{4,12},{8,0},{12,4},{16,24},{20,28},{24,16},{28,20},{1,9},{5... | collective-permute-start | bytes 4718600 | tf_op jit(solution)/shard_map/ppermute | solution.py:731
  278.2 38.3 %collective-permute-start.22 = (bf16[2,1,2,1,32,6144]{5,4,3,2,1,0:T(8,128)(2,1)}, bf16[2,1,2,1,32,6144]{5,4,3,2,1,0:T(8,128)(2,1)}, u32[]{:S(2)}, u32[]{:S(2)}) collective-permute-start(bf16[2,1,2,1,32,6144]{5,4,3,2,1,0:T(8,128)(2,1)} %fusion.41), channel_id=1, source_target_pairs={{0,16},{4,20},{8,24},{12,28},{16,0},{20,4},{24,8},{28,12},{1,17},{... | collective-permute-start | bytes 4718600 | tf_op jit(solution)/shard_map/ppermute | solution.py:731
  303.7 49.1 %collective-permute-start.25 = (bf16[4,2,2,1,32,768]{5,4,3,2,1,0:T(8,128)(2,1)}, bf16[4,2,2,1,32,768]{5,4,3,2,1,0:T(8,128)(2,1)}, u32[]{:S(2)}, u32[]{:S(2)}) collective-permute-start(bf16[4,2,2,1,32,768]{5,4,3,2,1,0:T(8,128)(2,1)} %constant_dynamic-slice_fusion.8), channel_id=1, source_target_pairs={{0,4},{4,0},{8,12},{12,8},{16,20},{20,16},{24,28},{28,24},{1,5},{5... | collective-permute-start | bytes 2359304 | tf_op jit(solution)/shard_map/ppermute | solution.py:788
  315.0 58.0 %collective-permute-start.21 = (bf16[2,1,1,1,32,6144]{5,4,3,2,1,0:T(8,128)(2,1)}, bf16[2,1,1,1,32,6144]{5,4,3,2,1,0:T(8,128)(2,1)}, u32[]{:S(2)}, u32[]{:S(2)}) collective-permute-start(bf16[2,1,1,1,32,6144]{5,4,3,2,1,0:T(8,128)(2,1)} %constant_dynamic-slice_fusion.11), channel_id=1, source_target_pairs={{0,16},{4,20},{8,24},{12,28},{16,0},{20,4},{24,8},{28,12},{1,17},{... | collective-permute-start | bytes 2359304 | tf_op jit(solution)/shard_map/ppermute | solution.py:731
  320.0 54.4 %collective-permute-start.23 = (bf16[2,1,1,1,32,6144]{5,4,3,2,1,0:T(8,128)(2,1)}, bf16[2,1,1,1,32,6144]{5,4,3,2,1,0:T(8,128)(2,1)}, u32[]{:S(2)}, u32[]{:S(2)}) collective-permute-start(bf16[2,1,1,1,32,6144]{5,4,3,2,1,0:T(8,128)(2,1)} %constant_dynamic-slice_fusion.10), channel_id=1, source_target_pairs={{0,8},{4,12},{8,0},{12,4},{16,24},{20,28},{24,16},{28,20},{1,9},{5... | collective-permute-start | bytes 2359304 | tf_op jit(solution)/shard_map/ppermute | solution.py:731
  367.2 106.9 %collective-permute-start.31 = (bf16[4,2,2,1,32,1536]{5,4,3,2,1,0:T(8,128)(2,1)}, bf16[4,2,2,1,32,1536]{5,4,3,2,1,0:T(8,128)(2,1)}, u32[]{:S(2)}, u32[]{:S(2)}) collective-permute-start(bf16[4,2,2,1,32,1536]{5,4,3,2,1,0:T(8,128)(2,1)} %constant_dynamic-slice_fusion.7), channel_id=1, source_target_pairs={{0,4},{4,0},{8,12},{12,8},{16,20},{20,16},{24,28},{28,24},{1,5},{5... | collective-permute-start | bytes 4718600 | tf_op jit(solution)/shard_map/ppermute | solution.py:788
  370.7 53.2 %collective-permute-start.40 = (bf16[2,2,1,1,32,2816]{5,4,3,2,1,0:T(8,128)(2,1)}, bf16[2,2,1,1,32,2816]{5,4,3,2,1,0:T(8,128)(2,1)}, u32[]{:S(2)}, u32[]{:S(2)}) collective-permute-start(bf16[2,2,1,1,32,2816]{5,4,3,2,1,0:T(8,128)(2,1)} %constant_dynamic-slice_fusion.2), channel_id=1, source_target_pairs={{0,8},{4,12},{8,0},{12,4},{16,24},{20,28},{24,16},{28,20},{1,9},{5... | collective-permute-start | bytes 2162696 | tf_op jit(solution)/shard_map/ppermute | solution.py:731
  371.9 66.0 %collective-permute-start.42 = (bf16[2,1,2,1,32,2816]{5,4,3,2,1,0:T(8,128)(2,1)}, bf16[2,1,2,1,32,2816]{5,4,3,2,1,0:T(8,128)(2,1)}, u32[]{:S(2)}, u32[]{:S(2)}) collective-permute-start(bf16[2,1,2,1,32,2816]{5,4,3,2,1,0:T(8,128)(2,1)} %fusion.54), channel_id=1, source_target_pairs={{0,16},{4,20},{8,24},{12,28},{16,0},{20,4},{24,8},{28,12},{1,17},{... | collective-permute-start | bytes 2162696 | tf_op jit(solution)/shard_map/ppermute | solution.py:731
  423.9 52.8 %collective-permute-start.32 = (bf16[4,2,2,1,32,1920]{5,4,3,2,1,0:T(8,128)(2,1)}, bf16[4,2,2,1,32,1920]{5,4,3,2,1,0:T(8,128)(2,1)}, u32[]{:S(2)}, u32[]{:S(2)}) collective-permute-start(bf16[4,2,2,1,32,1920]{5,4,3,2,1,0:T(8,128)(2,1)} %constant_dynamic-slice_fusion.6), channel_id=1, source_target_pairs={{0,4},{4,0},{8,12},{12,8},{16,20},{20,16},{24,28},{28,24},{1,5},{5... | collective-permute-start | bytes 5898248 | tf_op jit(solution)/shard_map/ppermute | solution.py:788
  428.7 17.6 %collective-permute-start.49 = (bf16[32,6144]{1,0:T(8,128)(2,1)}, bf16[32,6144]{1,0:T(8,128)(2,1)}, u32[]{:S(2)}, u32[]{:S(2)}) collective-permute-start(bf16[32,6144]{1,0:T(8,128)(2,1)} %get-tuple-element.149), channel_id=1, source_target_pairs={{0,3},{1,0},{2,1},{3,2},{4,7},{5,4},{6,5},{7,6},{8,11},{9,8},{10,9... | collective-permute-start | bytes 1179656 | tf_op jit(solution)/shard_map/ppermute | solution.py:846
  434.5 38.2 %collective-permute-start.48 = (bf16[32,6144]{1,0:T(8,128)(2,1)}, bf16[32,6144]{1,0:T(8,128)(2,1)S(1)}, u32[]{:S(2)}, u32[]{:S(2)}) collective-permute-start(bf16[32,6144]{1,0:T(8,128)(2,1)} %get-tuple-element.148), channel_id=1, source_target_pairs={{0,2},{1,3},{2,0},{3,1},{4,6},{5,7},{6,4},{7,5},{8,10},{9,11},{10,... | collective-permute-start | bytes 1179656 | tf_op jit(solution)/shard_map/ppermute | solution.py:846
  438.0 35.5 %collective-permute-start.47 = (bf16[32,6144]{1,0:T(8,128)(2,1)}, bf16[32,6144]{1,0:T(8,128)(2,1)S(1)}, u32[]{:S(2)}, u32[]{:S(2)}) collective-permute-start(bf16[32,6144]{1,0:T(8,128)(2,1)} %get-tuple-element.147), channel_id=1, source_target_pairs={{0,1},{1,2},{2,3},{3,0},{4,5},{5,6},{6,7},{7,4},{8,9},{9,10},{10,1... | collective-permute-start | bytes 1179656 | tf_op jit(solution)/shard_map/ppermute | solution.py:846
  446.3 71.5 %collective-permute-start.41 = (bf16[2,1,1,1,32,2816]{5,4,3,2,1,0:T(8,128)(2,1)}, bf16[2,1,1,1,32,2816]{5,4,3,2,1,0:T(8,128)(2,1)}, u32[]{:S(2)}, u32[]{:S(2)}) collective-permute-start(bf16[2,1,1,1,32,2816]{5,4,3,2,1,0:T(8,128)(2,1)} %constant_dynamic-slice_fusion.1), channel_id=1, source_target_pairs={{0,16},{4,20},{8,24},{12,28},{16,0},{20,4},{24,8},{28,12},{1,17},{... | collective-permute-start | bytes 1081352 | tf_op jit(solution)/shard_map/ppermute | solution.py:731
  472.6 45.2 %collective-permute-start.43 = (bf16[2,1,1,1,32,2816]{5,4,3,2,1,0:T(8,128)(2,1)}, bf16[2,1,1,1,32,2816]{5,4,3,2,1,0:T(8,128)(2,1)}, u32[]{:S(2)}, u32[]{:S(2)}) collective-permute-start(bf16[2,1,1,1,32,2816]{5,4,3,2,1,0:T(8,128)(2,1)} %constant_dynamic-slice_fusion), channel_id=1, source_target_pairs={{0,8},{4,12},{8,0},{12,4},{16,24},{20,28},{24,16},{28,20},{1,9},{5... | collective-permute-start | bytes 1081352 | tf_op jit(solution)/shard_map/ppermute | solution.py:731
  480.9 25.4 %collective-permute-start.33 = (bf16[2,2,1,1,32,3456]{5,4,3,2,1,0:T(8,128)(2,1)}, bf16[2,2,1,1,32,3456]{5,4,3,2,1,0:T(8,128)(2,1)S(1)}, u32[]{:S(2)}, u32[]{:S(2)}) collective-permute-start(bf16[2,2,1,1,32,3456]{5,4,3,2,1,0:T(8,128)(2,1)} %constant_dynamic-slice_fusion.5), channel_id=1, source_target_pairs={{0,8},{4,12},{8,0},{12,4},{16,24},{20,28},{24,16},{28,20},{1,9},{5... | collective-permute-start | bytes 2654216 | tf_op jit(solution)/shard_map/ppermute | solution.py:731
  484.3 86.8 %all-gather.9.cloned.1.call-start = ((), (), s32[]{:S(2)}) async-start(), calls=%async_computation.2 | async-start | bytes 1622016 | tf_op jit(solution)/shard_map/all_gather | solution.py:850
  485.7 30.7 %collective-permute-start.35 = (bf16[2,1,2,1,32,3456]{5,4,3,2,1,0:T(8,128)(2,1)S(1)}, bf16[2,1,2,1,32,3456]{5,4,3,2,1,0:T(8,128)(2,1)S(1)}, u32[]{:S(2)}, u32[]{:S(2)}) collective-permute-start(bf16[2,1,2,1,32,3456]{5,4,3,2,1,0:T(8,128)(2,1)S(1)} %fusion.47), channel_id=1, source_target_pairs={{0,16},{4,20},{8,24},{12,28},{16,0},{20,4},{24,8},{28,12},{1,17},{... | collective-permute-start | bytes 2654216 | tf_op jit(solution)/shard_map/ppermute | solution.py:731
  508.8 19.5 %collective-permute-start.34 = (bf16[2,1,1,1,32,3456]{5,4,3,2,1,0:T(8,128)(2,1)}, bf16[2,1,1,1,32,3456]{5,4,3,2,1,0:T(8,128)(2,1)}, u32[]{:S(2)}, u32[]{:S(2)}) collective-permute-start(bf16[2,1,1,1,32,3456]{5,4,3,2,1,0:T(8,128)(2,1)} %constant_dynamic-slice_fusion.4), channel_id=1, source_target_pairs={{0,16},{4,20},{8,24},{12,28},{16,0},{20,4},{24,8},{28,12},{1,17},{... | collective-permute-start | bytes 1327112 | tf_op jit(solution)/shard_map/ppermute | solution.py:731
  517.6 11.9 %collective-permute-start.36 = (bf16[2,1,1,1,32,3456]{5,4,3,2,1,0:T(8,128)(2,1)}, bf16[2,1,1,1,32,3456]{5,4,3,2,1,0:T(8,128)(2,1)S(1)}, u32[]{:S(2)}, u32[]{:S(2)}) collective-permute-start(bf16[2,1,1,1,32,3456]{5,4,3,2,1,0:T(8,128)(2,1)} %constant_dynamic-slice_fusion.3), channel_id=1, source_target_pairs={{0,8},{4,12},{8,0},{12,4},{16,24},{20,28},{24,16},{28,20},{1,9},{5... | collective-permute-start | bytes 1327112 | tf_op jit(solution)/shard_map/ppermute | solution.py:731
  521.3 10.2 %collective-permute-start.46 = (bf16[32,2816]{1,0:T(8,128)(2,1)S(1)}, bf16[32,2816]{1,0:T(8,128)(2,1)}, u32[]{:S(2)}, u32[]{:S(2)}) collective-permute-start(bf16[32,2816]{1,0:T(8,128)(2,1)S(1)} %get-tuple-element.167), channel_id=1, source_target_pairs={{0,3},{1,0},{2,1},{3,2},{4,7},{5,4},{6,5},{7,6},{8,11},{9,8},{10,9... | collective-permute-start | bytes 540680 | tf_op jit(solution)/shard_map/ppermute | solution.py:846
  521.3 12.2 %collective-permute-start.45 = (bf16[32,2816]{1,0:T(8,128)(2,1)}, bf16[32,2816]{1,0:T(8,128)(2,1)S(1)}, u32[]{:S(2)}, u32[]{:S(2)}) collective-permute-start(bf16[32,2816]{1,0:T(8,128)(2,1)} %get-tuple-element.166), channel_id=1, source_target_pairs={{0,2},{1,3},{2,0},{3,1},{4,6},{5,7},{6,4},{7,5},{8,10},{9,11},{10,... | collective-permute-start | bytes 540680 | tf_op jit(solution)/shard_map/ppermute | solution.py:846
  521.3 12.9 %collective-permute-start.44 = (bf16[32,2816]{1,0:T(8,128)(2,1)}, bf16[32,2816]{1,0:T(8,128)(2,1)}, u32[]{:S(2)}, u32[]{:S(2)}) collective-permute-start(bf16[32,2816]{1,0:T(8,128)(2,1)} %get-tuple-element.165), channel_id=1, source_target_pairs={{0,1},{1,2},{2,3},{3,0},{4,5},{5,6},{6,7},{7,4},{8,9},{9,10},{10,1... | collective-permute-start | bytes 540680 | tf_op jit(solution)/shard_map/ppermute | solution.py:846
  531.5 19.9 %collective-permute-start.39 = (bf16[32,3456]{1,0:T(8,128)(2,1)}, bf16[32,3456]{1,0:T(8,128)(2,1)}, u32[]{:S(2)}, u32[]{:S(2)}) collective-permute-start(bf16[32,3456]{1,0:T(8,128)(2,1)} %get-tuple-element.160), channel_id=1, source_target_pairs={{0,3},{1,0},{2,1},{3,2},{4,7},{5,4},{6,5},{7,6},{8,11},{9,8},{10,9... | collective-permute-start | bytes 663560 | tf_op jit(solution)/shard_map/ppermute | solution.py:846
  531.5 19.9 %collective-permute-start.38 = (bf16[32,3456]{1,0:T(8,128)(2,1)}, bf16[32,3456]{1,0:T(8,128)(2,1)}, u32[]{:S(2)}, u32[]{:S(2)}) collective-permute-start(bf16[32,3456]{1,0:T(8,128)(2,1)} %get-tuple-element.159), channel_id=1, source_target_pairs={{0,2},{1,3},{2,0},{3,1},{4,6},{5,7},{6,4},{7,5},{8,10},{9,11},{10,... | collective-permute-start | bytes 663560 | tf_op jit(solution)/shard_map/ppermute | solution.py:846
  531.5 19.9 %collective-permute-start.37 = (bf16[32,3456]{1,0:T(8,128)(2,1)}, bf16[32,3456]{1,0:T(8,128)(2,1)}, u32[]{:S(2)}, u32[]{:S(2)}) collective-permute-start(bf16[32,3456]{1,0:T(8,128)(2,1)} %get-tuple-element.158), channel_id=1, source_target_pairs={{0,1},{1,2},{2,3},{3,0},{4,5},{5,6},{6,7},{7,4},{8,9},{9,10},{10,1... | collective-permute-start | bytes 663560 | tf_op jit(solution)/shard_map/ppermute | solution.py:846
  536.3 74.1 %all-gather.11.cloned.1.call-start = ((), (), s32[]{:S(2)}) async-start(), calls=%async_computation.3 | async-start | bytes 1990656 | tf_op jit(solution)/shard_map/all_gather | solution.py:850
  571.5 1.2 collective-permute-start.26
  572.7 4.2 collective-permute-start.27
  577.0 12.4 %collective-permute-start.28 = (f32[12616]{0:T(1024)S(1)}, f32[12616]{0:T(1024)S(1)}, u32[]{:S(2)}, u32[]{:S(2)}) collective-permute-start(f32[12616]{0:T(1024)S(1)} %add.385), channel_id=1, source_target_pairs={{0,16},{4,20},{8,24},{12,28},{16,0},{20,4},{24,8},{28,12},{1,17},{... | collective-permute-start | bytes 151400 | tf_op jit(solution)/shard_map/ppermute | solution.py:870
  589.4 4.2 collective-permute-start.29
  593.6 5.6 collective-permute-start.30
  (125 other events, 1406.2 us)
Sparse Core Ops, SparseCore 0:
  11.5 139.6 all-gather.4
  484.4 42.4 all-gather.6
  536.4 34.5 all-gather.8
  573.3 26.5 all-gather.10
